TPU v7x, 32 devices: a whole 2x2x4 slice. The times are simulated.
32 devices in a mesh: seq: 16 (over z, y, x), ffn: 2 (over core).
Axes of the slice: x: 2, y: 2, z: 4, core: 2. Of those that a mesh axis runs over, the one named last changes fastest.
Arguments:
- inputs: float32 [2, 36864, 512], P(None, ('seq', 'ffn')), may hold values from -6 to 6
- lengths: int32 [2, 32, 3], P(None, ('seq', 'ffn')), may hold values from 1 to 1024, 1088 in all within a row
- first_gain: float32 [512], replicated, may hold values from 0.25 to 1.75
- first_shift: float32 [512], replicated, may hold values from -3 to 3
- query_weight: float32 [512, 512], replicated, may hold values from -0.25 to 0.25
- key_weight: float32 [512, 512], replicated, may hold values from -0.25 to 0.25
- value_weight: float32 [512, 512], replicated, may hold values from -0.25 to 0.25
- output_weight: float32 [512, 512], replicated, may hold values from -1 to 1
- output_bias: float32 [512], replicated, may hold values from -3 to 3
- projection: float32 [8, 64, 256], replicated, may hold values from -6 to 6
- second_gain: float32 [512], replicated, may hold values from 0.25 to 1.75
- second_shift: float32 [512], replicated, may hold values from -3 to 3
- up_weight: float32 [512, 2048], P('seq', 'ffn'), may hold values from -0.25 to 0.25
- up_bias: float32 [2048], replicated, may hold values from -3 to 3
- down_weight: float32 [2048, 512], P('ffn', 'seq'), may hold values from -0.25 to 0.25
- down_bias: float32 [512], replicated, may hold values from -3 to 3
- cotangent: float32 [2, 36864, 512], P(None, ('seq', 'ffn')), may hold values from -6 to 6
Outputs:
- output: float32 [2, 36864, 512], P(None, ('seq', 'ffn'))
- input_grad: float32 [2, 36864, 512], P(None, ('seq', 'ffn'))
- first_gain_grad: float32 [512], replicated
- first_shift_grad: float32 [512], replicated
- query_grad: float32 [512, 512], replicated
- key_grad: float32 [512, 512], replicated
- value_grad: float32 [512, 512], replicated
- output_weight_grad: float32 [512, 512], replicated
- output_bias_grad: float32 [512], replicated
- second_gain_grad: float32 [512], replicated
- second_shift_grad: float32 [512], replicated
- up_weight_grad: float32 [512, 2048], P('seq', 'ffn')
- up_bias_grad: float32 [2048], replicated
- down_weight_grad: float32 [2048, 512], P('ffn', 'seq')
- down_bias_grad: float32 [512], replicated
Inputs may be any that keep to these rules, and one draw needn't show every extreme that they name: Each row of 3 lengths sums to 1088, and its largest is exactly 1024.
All inputs are finite; a program needn't handle non-finite values.
Results may differ from a plain program's by a relative error of at most 0.035.
Values may be sent and summed in bfloat16 or wider, within the bound.
A program may use at most 448 MiB of HBM per device.

v0:
```python
from functools import reduce

import jax
import jax.numpy as jnp
from jax import lax
from jax.sharding import PartitionSpec as P

LONG_DEV = 64


EPSILON = 1e-05


def layer_norm(rows, gain, shift):
    mean = jnp.mean(rows, axis=-1, keepdims=True)
    centred = rows - mean
    spread = jnp.mean(centred * centred, axis=-1, keepdims=True)
    return centred * lax.rsqrt(spread + EPSILON) * gain + shift


def exact_gelu(values):
    return jax.nn.gelu(values, approximate=False)


def segment_table(lens, total_rows):
    rows = jnp.arange(total_rows, dtype=jnp.int32)
    ends = jnp.cumsum(lens)
    inside = jnp.sum((rows[:, None] - LONG_DEV >= ends[None, :]).astype(jnp.int32), axis=1)
    segment = jnp.where(rows < LONG_DEV, 0, 1 + inside)
    labels = jnp.arange(lens.shape[0] + 1, dtype=jnp.int32)
    return (segment[None, :] == labels[:, None]).astype(jnp.float32)


def feature_map(heads, projection_low, scale):
    scaled = heads * scale
    product = jnp.einsum(
        "rhd,hdm->rhm",
        scaled.astype(jnp.bfloat16),
        projection_low,
        preferred_element_type=jnp.float32,
    )
    square = 0.5 * jnp.sum(scaled * scaled, axis=-1, keepdims=True)
    mapped = jnp.exp(product - square) / jnp.sqrt(jnp.float32(projection_low.shape[2]))
    return (scaled, mapped)


def feature_back(scaled, mapped, grad_low, projection_low, scale):
    term = grad_low.astype(jnp.float32) * mapped
    back = jnp.einsum(
        "rhm,hdm->rhd",
        term.astype(jnp.bfloat16),
        projection_low,
        preferred_element_type=jnp.float32,
    )
    back = back - scaled * jnp.sum(term, axis=-1, keepdims=True)
    return (back * scale).astype(jnp.bfloat16).reshape(scaled.shape[0], -1)


def contract_rows(left, right):
    return lax.dot_general(
        left, right, (((0,), (0,)), ((), ())), preferred_element_type=jnp.float32
    )


def contract_cols(left, right):
    return lax.dot_general(
        left, right, (((1,), (1,)), ((), ())), preferred_element_type=jnp.float32
    )


def add_pairs(first, second):
    return tuple((left + right for left, right in zip(first, second)))


def body(
    inputs,
    lengths,
    first_gain,
    first_shift,
    query_weight,
    key_weight,
    value_weight,
    output_weight,
    output_bias,
    projection,
    second_gain,
    second_shift,
    up_weight,
    up_bias,
    down_weight,
    down_bias,
    cotangent,
):
    heads, head_size, features = projection.shape
    batches, rows_count, width = inputs.shape
    scale = head_size ** (-0.25)
    projection_low = projection.astype(jnp.bfloat16)
    query_low = query_weight.astype(jnp.bfloat16)
    key_low = key_weight.astype(jnp.bfloat16)
    value_low = value_weight.astype(jnp.bfloat16)
    output_low = output_weight.astype(jnp.bfloat16)
    up_shard = up_weight.astype(jnp.bfloat16)
    down_shard = down_weight.astype(jnp.bfloat16)
    hidden_width = up_bias.shape[0]
    half = hidden_width // lax.axis_size("ffn")
    offset = lax.axis_index("ffn") * half
    outputs = []
    input_grads = []
    shared_parts = []
    ffn_parts = []
    for batch in range(batches):
        batch_rows = inputs[batch]
        grad_out = cotangent[batch]
        table = segment_table(lengths[batch, 0], rows_count)
        table_low = table.astype(jnp.bfloat16)
        segments = table.shape[0]
        gathered_up, gathered_down = (
            lax.all_gather(up_shard, "seq", axis=0, tiled=True),
            lax.all_gather(down_shard, "seq", axis=1, tiled=True),
        )
        layer_bias = lax.dynamic_slice_in_dim(up_bias, offset, half)
        first_f32, first_back = jax.vjp(layer_norm, batch_rows, first_gain, first_shift)
        first_low = first_f32.astype(jnp.bfloat16)
        query_heads = jnp.dot(first_low, query_low, preferred_element_type=jnp.float32).reshape(
            rows_count, heads, head_size
        )
        key_heads = jnp.dot(first_low, key_low, preferred_element_type=jnp.float32).reshape(
            rows_count, heads, head_size
        )
        value_heads = (
            jnp.dot(first_low, value_low, preferred_element_type=jnp.float32)
            .astype(jnp.bfloat16)
            .reshape(rows_count, heads, head_size)
        )
        query_scaled, query_map = feature_map(query_heads, projection_low, scale)
        key_scaled, key_map = feature_map(key_heads, projection_low, scale)
        query_map_low = query_map.astype(jnp.bfloat16)
        key_map_low = key_map.astype(jnp.bfloat16)
        key_masked = [table_low[member][:, None, None] * key_map_low for member in range(segments)]
        query_masked = [
            table_low[member][:, None, None] * query_map_low for member in range(segments)
        ]
        local_sums = [
            jnp.einsum(
                "rhm,rhd->hdm", key_masked[member], value_heads, preferred_element_type=jnp.float32
            )
            for member in range(segments)
        ]
        local_norms = [
            jnp.einsum(
                "r,rhm->hm", table_low[member], key_map_low, preferred_element_type=jnp.float32
            )
            for member in range(segments)
        ]
        long_sum, long_norm = lax.psum((local_sums[0], local_norms[0]), ("seq", "ffn"))
        sums_low = [item.astype(jnp.bfloat16) for item in [long_sum] + local_sums[1:]]
        norms = [long_norm] + local_norms[1:]
        numer = reduce(
            jnp.add,
            [
                jnp.einsum(
                    "rhm,hdm->rhd",
                    query_masked[member],
                    sums_low[member],
                    preferred_element_type=jnp.float32,
                )
                for member in range(segments)
            ],
        )
        row_norm = reduce(
            jnp.add,
            [table[member][:, None, None] * norms[member][None] for member in range(segments)],
        )
        denom = jnp.sum(query_map_low * row_norm, axis=-1)
        mixed_low = (numer / denom[..., None]).reshape(rows_count, width).astype(jnp.bfloat16)
        attended = (
            batch_rows
            + jnp.dot(mixed_low, output_low, preferred_element_type=jnp.float32)
            + output_bias
        )
        second_f32, second_back = jax.vjp(layer_norm, attended, second_gain, second_shift)
        second_low = second_f32.astype(jnp.bfloat16)
        ffn_rows = lax.all_gather(second_low, "ffn", axis=0, tiled=True)
        hidden = jnp.dot(ffn_rows, gathered_up, preferred_element_type=jnp.float32) + layer_bias
        active_f32, gelu_back = jax.vjp(exact_gelu, hidden)
        active = active_f32.astype(jnp.bfloat16)
        branch_terms = jnp.dot(active, gathered_down, preferred_element_type=jnp.float32)
        branch = lax.psum_scatter(
            branch_terms.astype(jnp.bfloat16), "ffn", scatter_dimension=0, tiled=True
        ).astype(jnp.float32)
        outputs.append(attended + branch + down_bias)
        grad_branch = grad_out.astype(jnp.bfloat16)
        grad_rows = lax.all_gather(grad_branch, "ffn", axis=0, tiled=True)
        down_grad = contract_rows(active, grad_rows)
        grad_hidden = gelu_back(contract_cols(grad_rows, gathered_down))[0].astype(jnp.bfloat16)
        up_grad = contract_rows(ffn_rows, grad_hidden)
        bias_piece = jnp.sum(grad_hidden, axis=0, dtype=jnp.float32)
        second_terms = contract_cols(grad_hidden, gathered_up)
        grad_second = lax.psum_scatter(second_terms, "ffn", scatter_dimension=0, tiled=True)
        up_bias_grad = lax.dynamic_update_slice_in_dim(
            jnp.zeros((hidden_width,), jnp.float32), bias_piece, offset, 0
        )
        grad_from_norm, second_gain_grad, second_shift_grad = second_back(grad_second)
        grad_attended = grad_out + grad_from_norm
        grad_attended_low = grad_attended.astype(jnp.bfloat16)
        output_grad = contract_rows(mixed_low, grad_attended_low)
        grad_mixed = (
            contract_cols(grad_attended_low, output_low)
            .astype(jnp.bfloat16)
            .astype(jnp.float32)
            .reshape(rows_count, heads, head_size)
        )
        grad_numer = (grad_mixed / denom[..., None]).astype(jnp.bfloat16)
        grad_denom = -jnp.sum(grad_mixed * numer, axis=-1) / (denom * denom)
        weighted = query_map_low * grad_denom[..., None]
        local_sum_grads = [
            jnp.einsum(
                "rhm,rhd->hdm", query_masked[member], grad_numer, preferred_element_type=jnp.float32
            )
            for member in range(segments)
        ]
        local_norm_grads = [
            jnp.einsum("r,rhm->hm", table[member], weighted, preferred_element_type=jnp.float32)
            for member in range(segments)
        ]
        long_sum_grad, long_norm_grad = lax.psum(
            (local_sum_grads[0], local_norm_grads[0]), ("seq", "ffn")
        )
        sum_grads_low = [
            item.astype(jnp.bfloat16) for item in [long_sum_grad] + local_sum_grads[1:]
        ]
        norm_grads = [long_norm_grad] + local_norm_grads[1:]
        grad_query_map = (
            reduce(
                jnp.add,
                [
                    table[member][:, None, None]
                    * jnp.einsum(
                        "rhd,hdm->rhm",
                        grad_numer,
                        sums_low[member],
                        preferred_element_type=jnp.float32,
                    )
                    for member in range(segments)
                ],
            )
            + grad_denom[..., None] * row_norm
        )
        grad_key_map = reduce(
            jnp.add,
            [
                table[member][:, None, None]
                * (
                    jnp.einsum(
                        "rhd,hdm->rhm",
                        value_heads,
                        sum_grads_low[member],
                        preferred_element_type=jnp.float32,
                    )
                    + norm_grads[member][None]
                )
                for member in range(segments)
            ],
        )
        grad_values = (
            reduce(
                jnp.add,
                [
                    jnp.einsum(
                        "rhm,hdm->rhd",
                        key_masked[member],
                        sum_grads_low[member],
                        preferred_element_type=jnp.float32,
                    )
                    for member in range(segments)
                ],
            )
            .astype(jnp.bfloat16)
            .reshape(rows_count, width)
        )
        grad_queries = feature_back(
            query_scaled, query_map, grad_query_map.astype(jnp.bfloat16), projection_low, scale
        )
        grad_keys = feature_back(
            key_scaled, key_map, grad_key_map.astype(jnp.bfloat16), projection_low, scale
        )
        query_grad = contract_rows(first_low, grad_queries)
        key_grad = contract_rows(first_low, grad_keys)
        value_grad = contract_rows(first_low, grad_values)
        grad_first = (
            contract_cols(grad_queries, query_low)
            + contract_cols(grad_keys, key_low)
            + contract_cols(grad_values, value_low)
        )
        grad_input_norm, first_gain_grad, first_shift_grad = first_back(grad_first)
        input_grads.append(grad_attended + grad_input_norm)
        output_bias_grad = jnp.sum(grad_attended, axis=0)
        down_bias_grad = jnp.sum(grad_out, axis=0)
        shared_now = (
            first_gain_grad,
            first_shift_grad,
            query_grad,
            key_grad,
            value_grad,
            output_grad,
            output_bias_grad,
            second_gain_grad,
            second_shift_grad,
            up_bias_grad,
            down_bias_grad,
        )
        shared_parts.append(
            lax.psum(
                (
                    shared_now[0],
                    shared_now[1],
                    shared_now[2],
                    shared_now[3],
                    shared_now[4],
                    shared_now[5],
                    shared_now[6],
                    shared_now[7],
                    shared_now[8],
                    shared_now[9],
                    shared_now[10],
                ),
                ("seq", "ffn"),
            )
        )
        ffn_parts.append(
            (
                lax.psum_scatter(up_grad, "seq", scatter_dimension=0, tiled=True),
                lax.psum_scatter(down_grad, "seq", scatter_dimension=1, tiled=True),
            )
        )
    shared_total = reduce(add_pairs, shared_parts)
    ffn_total = reduce(add_pairs, ffn_parts)
    return (
        jnp.stack(outputs),
        jnp.stack(input_grads),
        shared_total[0],
        shared_total[1],
        shared_total[2],
        shared_total[3],
        shared_total[4],
        shared_total[5],
        shared_total[6],
        shared_total[7],
        shared_total[8],
        ffn_total[0],
        shared_total[9],
        ffn_total[1],
        shared_total[10],
    )


def solution(mesh):
    in_specs = (
        P(None, ("seq", "ffn"), None),
        P(None, ("seq", "ffn"), None),
        P(),
        P(),
        P(),
        P(),
        P(),
        P(),
        P(),
        P(),
        P(),
        P(),
        P("seq", "ffn"),
        P(),
        P("ffn", "seq"),
        P(),
        P(None, ("seq", "ffn"), None),
    )
    out_specs = (
        P(None, ("seq", "ffn"), None),
        P(None, ("seq", "ffn"), None),
        P(),
        P(),
        P(),
        P(),
        P(),
        P(),
        P(),
        P(),
        P(),
        P("seq", "ffn"),
        P(),
        P("ffn", "seq"),
        P(),
    )
    return jax.shard_map(body, mesh=mesh, in_specs=in_specs, out_specs=out_specs, check_vma=False)
```

profile of v0, /device:TPU:0, one launch (start us, length us, event | category | flops | bytes accessed | tf_op | source)
XLA Modules:
  0.0 813.5 jit_solution(15094373601785846623)
XLA Ops:
  9.4 8.7 %slice_reduce_fusion.16 = (f32[512]{0:T(512)}, f32[512]{0:T(512)}, f32[1,1152,512]{2,1,0:T(8,128)}, f32[1,1152,512]{2,1,0:T(8,128)}, f32[1,1152,512]{2,1,0:T(8,1...) fusion(f32[2,1152,512]{2,1,0:T(8,128)} %param.33, f32[2,1152,512]{2,1,0:T(8,128)} %param.17), kind=kLoop, calls=%fused_computation.467 | loop fusion | flops 2355968 | bytes 18887680 | tf_op jit(solution)/shard_map/reduce_sum | solution.py:298
  41.0 4.7 fusion.34
  55.9 4.9 fusion.32
  70.9 3.8 multiply_reduce_fusion.9
  74.7 4.5 multiply_reduce_fusion.13
  95.2 54.5 %all-reduce.9 = (bf16[8,64,256]{2,1,0:T(8,128)(2,1)S(1)}, f32[8,256]{1,0:T(8,128)S(1)}, bf16[8,64,256]{2,1,0:T(8,128)(2,1)}, f32[8,256]{1,0:T(8,128)S(1)}) all-reduce(f32[8,64,256]{2,1,0:T(8,128)} %fusion.82, f32[8,256]{1,0:T(8,128)} %bitcast.508, f32[8,64,256]{2,1,0:T(8,128)} %fusion.114, ...), channel_id=1, replica_groups=mesh['seq'=16,'ffn'=2] {'seq','ffn'}, use_global_device_ids=true, to_apply=%region_17.18 | all-reduce | flops 266240 | bytes 1605632 | tf_op jit(solution)/shard_map/psum | solution.py:155
  149.8 8.4 %fusion.9 = (f32[1152,8]{0,1:T(8,128)S(1)}, bf16[1152,8,256]{0,2,1:T(8,128)(2,1)S(1)}, f32[8,1152,256]{1,2,0:T(8,128)}) fusion(f32[8,256]{1,0:T(8,128)S(1)} %bitcast.518, f32[1152]{0:T(1024)S(1)} %copy-done.161, f32[8,256]{1,0:T(8,128)S(1)} %bitcast.520, f32[1152]{0:T(1024)S(1)} %copy-done.157, f32[8,256]{1,0:T(8,128)S(1)} %bitcast.522, ...), kind=kOutput, calls=%fused_computation.15 | convolution fusion | flops 333831168 | bytes 16902144 | tf_op jit(solution)/shard_map/rhd,hdm->rhm/dot_general | solution.py:36
  172.2 6.8 fusion.8
  198.6 8.1 %fusion.410 = f32[2304,1024]{1,0:T(8,128)} fusion(bf16[2304,512]{0,1:T(8,128)(2,1)} %all-gather.13.cloned.1.call-done, bf16[512,1024]{1,0:T(8,128)(2,1)} %all-gather.9.cloned.1.call-done), kind=kOutput, calls=%fused_computation.493 | convolution fusion | flops 2415919104 | bytes 12845056 | tf_op jit(solution)/shard_map/dot_general | solution.py:184
  206.8 5.6 all-gather.7.cloned.1.call-done
  212.3 47.9 %multiply_convert_fusion.1 = (bf16[2304,1024]{1,0:T(8,128)(2,1)}, f32[2304,1024]{1,0:T(8,128)}, bf16[2304,1024]{1,0:T(8,128)(2,1)}, f32[2304,1024]{1,0:T(8,128)}, f32[2304,1024]{1,0:T(8,128)}) fusion(f32[1024]{0:T(1024)S(1)} %dynamic_slice.4, f32[2304,1024]{1,0:T(8,128)} %fusion.410, bf16[2304,512]{0,1:T(8,128)(2,1)} %all-gather.7.cloned.1.call-done, ...), kind=kOutput, calls=%fused_computation.58 | convolution fusion | flops 2727346176 | bytes 50597888 | tf_op jit(solution)/shard_map/dot_general | solution.py:184
  260.2 11.8 %all-gather.11.cloned.1.call-done = bf16[1024,512]{0,1:T(8,128)(2,1)} async-done(((bf16[1024,32]{0,1:T(8,128)(2,1)}), bf16[1024,512]{0,1:T(8,128)(2,1)}) %all-gather.11.cloned.1.call-update) | async-done | bytes 1048592 | tf_op jit(solution)/shard_map/all_gather | solution.py:119
  272.0 6.7 convolution_convert_fusion.1
  280.0 6.7 convolution_convert_fusion
  286.8 11.4 %convert_reduce_fusion = (f32[1024]{0:T(1024)S(1)}, bf16[2304,1024]{1,0:T(8,128)(2,1)S(1)}) fusion(f32[2304,1024]{1,0:T(8,128)} %get-tuple-element.158, bf16[2304,512]{0,1:T(8,128)(2,1)} %all-gather.17.cloned.1.call-done, bf16[1024,512]{0,1:T(8,128)(2,1)S(1)} %copy-done.226, f32[2304,1024]{1,0:T(8,128)} %fusion.410, f32[1024]{0:T(1024)S(1)} %dynamic_slice.4), kind=kOutput, calls=%fused_computation.38 | convolution fusion | flops 2456026112 | bytes 27009024 | tf_op jit(solution)/shard_map/dot_general | solution.py:66
  300.4 4.4 fusion.415
  304.9 11.9 %convert_reduce_fusion.1 = (f32[1024]{0:T(1024)S(1)}, bf16[2304,1024]{1,0:T(8,128)(2,1)S(1)}) fusion(f32[2304,1024]{1,0:T(8,128)} %get-tuple-element.137, bf16[2304,512]{0,1:T(8,128)(2,1)} %all-gather.15.cloned.1.call-done, bf16[1024,512]{0,1:T(8,128)(2,1)S(1)} %copy-done.226, f32[2304,1024]{1,0:T(8,128)} %get-tuple-element.197, f32[1024]{0:T(1024)S(1)} %dynamic_slice.4), kind=kOutput, calls=%fused_computation.39 | convolution fusion | flops 2456026112 | bytes 27009024 | tf_op jit(solution)/shard_map/dot_general | solution.py:66
  318.9 4.3 fusion.411
  323.3 5.3 fusion.419
  328.7 6.3 convolution_add_fusion.7
  339.4 5.3 fusion.420
  344.7 6.3 convolution_add_fusion.6
  355.8 4.8 fusion.393
  363.8 4.9 fusion.396
  389.5 5.3 fusion.413
  407.6 5.0 fusion.417
  416.8 5.1 fusion.333
  421.9 5.1 fusion.389
  427.0 5.0 fusion.387
  431.9 5.0 fusion.330
  436.9 5.0 fusion.379
  441.9 5.0 fusion.377
  448.1 65.9 %all-reduce.10 = (bf16[8,64,256]{2,1,0:T(8,128)(2,1)}, f32[8,256]{1,0:T(8,128)}, bf16[8,64,256]{2,1,0:T(8,128)(2,1)}, f32[8,256]{1,0:T(8,128)}) all-reduce(f32[8,64,256]{2,1,0:T(8,128)} %fusion.76, f32[8,256]{1,0:T(8,128)} %bitcast.517, f32[8,64,256]{2,1,0:T(8,128)} %fusion.108, ...), channel_id=1, replica_groups=mesh['seq'=16,'ffn'=2] {'seq','ffn'}, use_global_device_ids=true, to_apply=%region_39.40 | all-reduce | flops 266240 | bytes 1605632 | tf_op jit(solution)/shard_map/psum | solution.py:226
  514.0 6.1 fusion.422
  523.6 5.1 fusion.414
  530.0 4.9 fusion.421
  536.0 4.9 fusion.418
  545.5 18.2 %fusion.407 = (f32[1152,8]{0,1:T(8,128)S(1)}, bf16[1152,8,256]{0,2,1:T(8,128)(2,1)}) fusion(f32[1152,8]{0,1:T(8,128)S(1)} %copy-done.103, f32[8,1152,256]{1,2,0:T(8,128)} %get-tuple-element.178, f32[8,256]{1,0:T(8,128)S(1)} %bitcast.515, bf16[8,64,256]{2,1,0:T(8,128)(2,1)} %fusion.265, bf16[1152,8,64]{0,2,1:T(8,128)(2,1)} %bitcast.480, ...), kind=kOutput, calls=%fused_computation.490 | convolution fusion | flops 344448000 | bytes 44034048 | tf_op jit(solution)/shard_map/rhd,hdm->rhm/dot_general | solution.py:254
  570.1 18.0 %fusion.409 = (f32[1152,8]{0,1:T(8,128)S(1)}, bf16[1152,8,256]{0,2,1:T(8,128)(2,1)}) fusion(f32[1152,8]{0,1:T(8,128)S(1)} %copy-done.101, f32[8,1152,256]{1,2,0:T(8,128)} %get-tuple-element.182, f32[8,256]{1,0:T(8,128)} %bitcast.514, bf16[8,64,256]{2,1,0:T(8,128)(2,1)S(1)} %copy-done.79, bf16[1152,8,64]{0,2,1:T(8,128)(2,1)} %bitcast.476, ...), kind=kOutput, calls=%fused_computation.492 | convolution fusion | flops 344448000 | bytes 44034048 | tf_op jit(solution)/shard_map/rhd,hdm->rhm/dot_general | solution.py:254
  588.3 18.3 %fusion.406 = (f32[1152,8]{0,1:T(8,128)S(1)}, bf16[1152,8,256]{0,2,1:T(8,128)(2,1)}) fusion(f32[1152,8]{0,1:T(8,128)S(1)} %copy-done.151, f32[8,1152,256]{1,2,0:T(8,128)} %get-tuple-element.185, f32[8,256]{1,0:T(8,128)S(1)} %bitcast.529, f32[1152]{0:T(1024)S(1)} %copy-done.170, f32[8,256]{1,0:T(8,128)S(1)} %bitcast.525, f32[1152]{0:T(1024)S(1)} %copy-done.166, ...), kind=kOutput, calls=%fused_computation.489 | convolution fusion | flops 358013952 | bytes 44107776 | tf_op jit(solution)/shard_map/rhd,hdm->rhm/dot_general | solution.py:238
  606.7 16.8 %fusion.408 = (f32[1152,8]{0,1:T(8,128)S(1)}, bf16[1152,8,256]{0,2,1:T(8,128)(2,1)}) fusion(f32[1152,8]{0,1:T(8,128)S(1)} %copy-done.149, f32[8,1152,256]{1,2,0:T(8,128)} %get-tuple-element.192, f32[8,256]{1,0:T(8,128)S(1)} %bitcast.519, f32[1152]{0:T(1024)S(1)} %copy-done.162, f32[8,256]{1,0:T(8,128)S(1)} %bitcast.521, f32[1152]{0:T(1024)S(1)} %copy-done.158, ...), kind=kOutput, calls=%fused_computation.491 | convolution fusion | flops 358013952 | bytes 44107776 | tf_op jit(solution)/shard_map/rhd,hdm->rhm/dot_general | solution.py:238
  623.6 4.1 fusion.205
  659.0 5.8 add_bitcast_fusion.1
  667.3 6.3 copy.265
  673.6 4.2 pad_maximum_fusion
  677.8 6.1 copy.264
  684.1 39.5 %all-reduce = (f32[512]{0:T(512)}, f32[512]{0:T(512)}, f32[512]{0:T(512)}, f32[512]{0:T(512)}, f32[512]{0:T(512)}, /*index=5*/f32[2048]{0:T(1024)}, f32[512]{0:T(512)}) all-reduce(f32[512]{0:T(512)S(1)} %add.596, f32[512]{0:T(512)S(1)} %add.597, f32[512]{0:T(512)S(1)} %add.602, ...), channel_id=1, replica_groups=mesh['seq'=16,'ffn'=2] {'seq','ffn'}, use_global_device_ids=true, to_apply=%region_45.46 | all-reduce | flops 5120 | bytes 40960 | tf_op jit(solution)/shard_map/psum | solution.py:313
  723.6 77.8 %all-reduce.8.cloned.1.call-done = (f32[512,512]{1,0:T(8,128)}, f32[512,512]{1,0:T(8,128)}, f32[512,512]{1,0:T(8,128)}, f32[512,512]{1,0:T(8,128)}) async-done(((f32[512,512]{1,0:T(8,128)}, f32[512,512]{1,0:T(8,128)}, f32[512,512]{1,0:T(8,128)}, f32[512,512]{1,0:T(8,128)}), (f32[512,512]{1,0:T(8,128)}, f32[512,512]{1,0:T(8,128)}, f32[512,512]{1,0:T(8,128)}, ...) | async-done | bytes 4194320 | tf_op jit(solution)/shard_map/psum | solution.py:313
  (725 shorter events, 206.1 us)
Async XLA Ops:
  7.2 191.0 %all-gather.9.cloned.1.call-start = ((), (), s32[]{:S(2)}) async-start(), calls=%async_computation.7 | async-start | bytes 1114112 | tf_op jit(solution)/shard_map/all_gather | solution.py:118
  8.8 189.8 %all-gather.13.cloned.1.call-start = ((), (), s32[]{:S(2)}) async-start(), calls=%async_computation.9 | async-start | bytes 3538944 | tf_op jit(solution)/shard_map/all_gather | solution.py:183
  20.1 143.8 %copy-start.5 = (f32[1,1152,512]{1,2,0:T(8,128)}, f32[1,1152,512]{1,2,0:T(8,128)S(1)}, u32[]{:S(2)}) copy-start(f32[1,1152,512]{1,2,0:T(8,128)S(1)} %copy.339) | copy-start | bytes 7077892
  32.2 60.5 %copy-start.30 = (bf16[1152,512]{0,1:T(8,128)(2,1)}, bf16[1152,512]{0,1:T(8,128)(2,1)S(1)}, u32[]{:S(2)}) copy-start(bf16[1152,512]{0,1:T(8,128)(2,1)S(1)} %convolution_convert_fusion.4) | copy-start | bytes 3538948
  41.0 118.2 %copy-start.137 = (bf16[1152]{0:T(1024)(128)(2,1)}, bf16[1152]{0:T(1024)(128)(2,1)S(1)}, u32[]{:S(2)}) copy-start(bf16[1152]{0:T(1024)(128)(2,1)S(1)} %get-tuple-element.110) | copy-start | bytes 6916
  41.0 119.2 %copy-start.135 = (bf16[1152]{0:T(1024)(128)(2,1)}, bf16[1152]{0:T(1024)(128)(2,1)S(1)}, u32[]{:S(2)}) copy-start(bf16[1152]{0:T(1024)(128)(2,1)S(1)} %get-tuple-element.108) | copy-start | bytes 6916
  55.9 123.9 %copy-start.141 = (bf16[1152]{0:T(1024)(128)(2,1)}, bf16[1152]{0:T(1024)(128)(2,1)S(1)}, u32[]{:S(2)}) copy-start(bf16[1152]{0:T(1024)(128)(2,1)S(1)} %get-tuple-element.106) | copy-start | bytes 6916
  55.9 125.2 %copy-start.139 = (bf16[1152]{0:T(1024)(128)(2,1)}, bf16[1152]{0:T(1024)(128)(2,1)S(1)}, u32[]{:S(2)}) copy-start(bf16[1152]{0:T(1024)(128)(2,1)S(1)} %get-tuple-element.104) | copy-start | bytes 6916
  95.0 54.7 %copy-start.39 = (bf16[8,64,256]{2,1,0:T(8,128)(2,1)S(1)}, bf16[8,64,256]{2,1,0:T(8,128)(2,1)}, u32[]{:S(2)}) copy-start(bf16[8,64,256]{2,1,0:T(8,128)(2,1)} %convert_element_type.293) | copy-start | bytes 786436
  95.0 54.7 %copy-start.148 = (f32[1152,8]{0,1:T(8,128)S(1)}, f32[1152,8]{0,1:T(8,128)}, u32[]{:S(2)}) copy-start(f32[1152,8]{0,1:T(8,128)} %broadcast_multiply_fusion.4) | copy-start | bytes 110596
  95.0 54.7 %copy-start.155 = (f32[1152]{0:T(1024)S(1)}, f32[1152]{0:T(1024)}, u32[]{:S(2)}) copy-start(f32[1152]{0:T(1024)} %get-tuple-element.99) | copy-start | bytes 13828
  95.0 54.7 %copy-start.157 = (f32[1152]{0:T(1024)S(1)}, f32[1152]{0:T(1024)}, u32[]{:S(2)}) copy-start(f32[1152]{0:T(1024)} %get-tuple-element.100) | copy-start | bytes 13828
  95.1 54.7 %copy-start.159 = (f32[1152]{0:T(1024)S(1)}, f32[1152]{0:T(1024)}, u32[]{:S(2)}) copy-start(f32[1152]{0:T(1024)} %get-tuple-element.101) | copy-start | bytes 13828
  95.1 54.7 %copy-start.161 = (f32[1152]{0:T(1024)S(1)}, f32[1152]{0:T(1024)}, u32[]{:S(2)}) copy-start(f32[1152]{0:T(1024)} %get-tuple-element.102) | copy-start | bytes 13828
  95.1 54.7 %copy-start.206 = (f32[1,8,256]{2,1,0:T(8,128)S(1)}, f32[1,8,256]{2,1,0:T(8,128)}, u32[]{:S(2)}) copy-start(f32[1,8,256]{2,1,0:T(8,128)} %copy.370) | copy-start | bytes 24580
  95.1 54.7 %copy-start.208 = (f32[1,8,256]{2,1,0:T(8,128)S(1)}, f32[1,8,256]{2,1,0:T(8,128)}, u32[]{:S(2)}) copy-start(f32[1,8,256]{2,1,0:T(8,128)} %copy.371) | copy-start | bytes 24580
  95.1 54.7 %copy-start.210 = (f32[1,8,256]{2,1,0:T(8,128)S(1)}, f32[1,8,256]{2,1,0:T(8,128)}, u32[]{:S(2)}) copy-start(f32[1,8,256]{2,1,0:T(8,128)} %copy.372) | copy-start | bytes 24580
  95.2 89.4 %copy-start.36 = (bf16[512,512]{1,0:T(8,128)(2,1)}, bf16[512,512]{1,0:T(8,128)(2,1)S(1)}, u32[]{:S(2)}) copy-start(bf16[512,512]{1,0:T(8,128)(2,1)S(1)} %convert_element_type.305) | copy-start | bytes 1572868
  149.7 21.0 %copy-start.229 = (f32[8,256]{1,0:T(8,128)}, f32[8,256]{1,0:T(8,128)S(1)}, u32[]{:S(2)}) copy-start(f32[8,256]{1,0:T(8,128)S(1)} %get-tuple-element.127) | copy-start | bytes 24580
  164.9 21.0 %copy-start.10 = (f32[1152,512]{0,1:T(8,128)}, f32[1152,512]{0,1:T(8,128)S(1)}, u32[]{:S(2)}) copy-start(f32[1152,512]{0,1:T(8,128)S(1)} %get-tuple-element.196) | copy-start | bytes 7077892
  164.9 21.0 %copy-start.108 = (f32[1152]{0:T(1024)}, f32[1152]{0:T(1024)S(1)}, u32[]{:S(2)}) copy-start(f32[1152]{0:T(1024)S(1)} %broadcast_multiply_fusion.8) | copy-start | bytes 13828
  188.6 23.7 %all-gather.7.cloned.1.call-start = ((), (), s32[]{:S(2)}) async-start(), calls=%async_computation.6 | async-start | bytes 3538944 | tf_op jit(solution)/shard_map/all_gather | solution.py:183
  189.3 82.6 %all-gather.11.cloned.1.call-start = ((), (), s32[]{:S(2)}) async-start(), calls=%async_computation.8 | async-start | bytes 1114112 | tf_op jit(solution)/shard_map/all_gather | solution.py:119
  190.1 96.7 %all-gather.17.cloned.1.call-start = ((), (), s32[]{:S(2)}) async-start(), calls=%async_computation.12 | async-start | bytes 3538944 | tf_op jit(solution)/shard_map/all_gather | solution.py:193
  194.0 110.8 %all-gather.15.cloned.1.call-start = ((), (), s32[]{:S(2)}) async-start(), calls=%async_computation.10 | async-start | bytes 3538944 | tf_op jit(solution)/shard_map/all_gather | solution.py:193
  198.2 153.0 %reduce-scatter.19.cloned.1.call-start = ((), (), s32[]{:S(2)}) async-start(), calls=%async_computation.16 | async-start | bytes 3538944
  278.7 74.6 %reduce-scatter.21.cloned.1.call-start = ((), (), s32[]{:S(2)}) async-start(), calls=%async_computation.17 | async-start | bytes 3538944
  286.7 69.0 %reduce-scatter.13.cloned.1.call-start = ((), (), s32[]{:S(2)}) async-start(), calls=%async_computation.13 | async-start | bytes 7077888 | tf_op jit(solution)/shard_map/reduce_scatter | solution.py:199
  304.8 50.9 %reduce-scatter.11.cloned.1.call-start = ((), (), s32[]{:S(2)}) async-start(), calls=%async_computation.11 | async-start | bytes 7077888 | tf_op jit(solution)/shard_map/reduce_scatter | solution.py:199
  323.3 400.3 %reduce-scatter.15.cloned.1.call-start = ((), (), s32[]{:S(2)}) async-start(), calls=%async_computation.14 | async-start | bytes 2228224 | tf_op jit(solution)/shard_map/reduce_scatter | solution.py:332
  335.0 388.6 %reduce-scatter.17.cloned.1.call-start = ((), (), s32[]{:S(2)}) async-start(), calls=%async_computation.15 | async-start | bytes 2228224 | tf_op jit(solution)/shard_map/reduce_scatter | solution.py:333
  351.1 450.4 %all-reduce.8.cloned.1.call-start = ((), (), s32[]{:S(2)}) async-start(), calls=%async_computation.18 | async-start | bytes 8388608 | tf_op jit(solution)/shard_map/psum | solution.py:313
  370.1 56.8 %copy-start.28 = (bf16[1152,512]{0,1:T(8,128)(2,1)}, bf16[1152,512]{0,1:T(8,128)(2,1)S(1)}, u32[]{:S(2)}) copy-start(bf16[1152,512]{0,1:T(8,128)(2,1)S(1)} %get-tuple-element.199) | copy-start | bytes 3538948
  379.7 62.2 %copy-start.26 = (bf16[1152,512]{0,1:T(8,128)(2,1)}, bf16[1152,512]{0,1:T(8,128)(2,1)S(1)}, u32[]{:S(2)}) copy-start(bf16[1152,512]{0,1:T(8,128)(2,1)S(1)} %get-tuple-element.203) | copy-start | bytes 3538948
  545.4 18.2 %copy-start.171 = (f32[1,8,256]{2,0,1:T(1,128)S(1)}, f32[1,8,256]{2,0,1:T(1,128)}, u32[]{:S(2)}) copy-start(f32[1,8,256]{2,0,1:T(1,128)} %fusion.2) | copy-start | bytes 24580
  545.4 20.1 %copy-start.172 = (f32[1,8,256]{2,0,1:T(1,128)S(1)}, f32[1,8,256]{2,0,1:T(1,128)}, u32[]{:S(2)}) copy-start(f32[1,8,256]{2,0,1:T(1,128)} %fusion) | copy-start | bytes 24580
  545.4 20.7 %copy-start.79 = (bf16[8,64,256]{2,1,0:T(8,128)(2,1)S(1)}, bf16[8,64,256]{2,1,0:T(8,128)(2,1)}, u32[]{:S(2)}) copy-start(bf16[8,64,256]{2,1,0:T(8,128)(2,1)} %fusion.283) | copy-start | bytes 786436
  570.0 18.1 %copy-start.29 = (bf16[1152,512]{0,1:T(8,128)(2,1)S(1)}, bf16[1152,512]{0,1:T(8,128)(2,1)}, u32[]{:S(2)}) copy-start(bf16[1152,512]{0,1:T(8,128)(2,1)} %copy-done.28) | copy-start | bytes 3538948
  570.1 18.1 %copy-start.93 = (f32[1152,8]{0,1:T(8,128)S(1)}, f32[1152,8]{0,1:T(8,128)}, u32[]{:S(2)}) copy-start(f32[1152,8]{0,1:T(8,128)} %copy-done.92) | copy-start | bytes 110596
  588.2 18.4 %copy-start.27 = (bf16[1152,512]{0,1:T(8,128)(2,1)S(1)}, bf16[1152,512]{0,1:T(8,128)(2,1)}, u32[]{:S(2)}) copy-start(bf16[1152,512]{0,1:T(8,128)(2,1)} %copy-done.26) | copy-start | bytes 3538948
  588.3 18.4 %copy-start.91 = (f32[1152,8]{0,1:T(8,128)S(1)}, f32[1152,8]{0,1:T(8,128)}, u32[]{:S(2)}) copy-start(f32[1152,8]{0,1:T(8,128)} %copy-done.90) | copy-start | bytes 110596
  588.3 18.4 %copy-start.96 = (f32[1152,8]{0,1:T(8,128)S(1)}, f32[1152,8]{0,1:T(8,128)}, u32[]{:S(2)}) copy-start(f32[1152,8]{0,1:T(8,128)} %copy-done.94) | copy-start | bytes 110596
  588.3 18.4 %copy-start.149 = (f32[1152,8]{0,1:T(8,128)S(1)}, f32[1152,8]{0,1:T(8,128)}, u32[]{:S(2)}) copy-start(f32[1152,8]{0,1:T(8,128)} %broadcast_multiply_fusion.4) | copy-start | bytes 110596
  588.3 18.4 %copy-start.207 = (f32[1,8,256]{2,1,0:T(8,128)S(1)}, f32[1,8,256]{2,1,0:T(8,128)}, u32[]{:S(2)}) copy-start(f32[1,8,256]{2,1,0:T(8,128)} %copy.370) | copy-start | bytes 24580
  588.3 18.4 %copy-start.209 = (f32[1,8,256]{2,1,0:T(8,128)S(1)}, f32[1,8,256]{2,1,0:T(8,128)}, u32[]{:S(2)}) copy-start(f32[1,8,256]{2,1,0:T(8,128)} %copy.371) | copy-start | bytes 24580
  588.3 18.4 %copy-start.211 = (f32[1,8,256]{2,1,0:T(8,128)S(1)}, f32[1,8,256]{2,1,0:T(8,128)}, u32[]{:S(2)}) copy-start(f32[1,8,256]{2,1,0:T(8,128)} %copy.372) | copy-start | bytes 24580
  588.3 18.4 %copy-start.228 = (f32[8,256]{1,0:T(8,128)S(1)}, f32[8,256]{1,0:T(8,128)}, u32[]{:S(2)}) copy-start(f32[8,256]{1,0:T(8,128)} %copy-done.227) | copy-start | bytes 24580
  588.3 18.4 %copy-start.232 = (bf16[8,64,256]{2,1,0:T(8,128)(2,1)S(1)}, bf16[8,64,256]{2,1,0:T(8,128)(2,1)}, u32[]{:S(2)}) copy-start(bf16[8,64,256]{2,1,0:T(8,128)(2,1)} %fusion.280) | copy-start | bytes 786436
  (221 other events, 973.8 us)
Sparse Core Ops, SparseCore 0:
  11.3 57.9 all-gather.8
  188.7 9.8 all-gather.12
  200.2 12.0 all-gather.6
  215.5 56.4 all-gather.10
  273.4 9.7 all-gather.16
  284.6 12.1 all-gather.14
  298.9 11.0 reduce-scatter.18
  312.4 11.0 reduce-scatter.20
  325.8 13.7 reduce-scatter.12
  341.9 13.7 reduce-scatter.10
  358.5 81.9 reduce-scatter.14
  443.2 78.6 reduce-scatter.16
  659.1 142.2 all-reduce.7
where the time goes:
time: 823 us; the launch traced here: 813 us
  matrix products  415 us (50%)
  blocking collectives  160 us (19%)
  waiting for transfers between devices  96.5 us (12%)
  local copies, waits for them, and re-layouts  69.6 us (8%)
  other arithmetic  55.2 us (7%)
  between operations  17 us (2%)
    psum x1, waiting for transfers between devices, body(): lax.psum((shared_now[0], shared_now[1], shared_now[2], shared_now[3], sha...  77.8 us
    dot_general x8, matrix products, body(): jnp.einsum('rhd,hdm->rhm', value_heads, sum_grads_low[member], preferred_...  67.5 us
    psum x1, blocking collectives, body(): lax.psum((local_sum_grads[0], local_norm_grads[0]), ('seq', 'ffn'))  65.9 us
    dot_general x8, matrix products, body(): jnp.einsum('rhd,hdm->rhm', grad_numer, sums_low[member], preferred_elemen...  65.1 us
    unnamed x526, local copies, waits for them, and re-layouts  58.5 us
    dot_general x2, matrix products, body(): jnp.dot(ffn_rows, gathered_up, preferred_element_type=jnp.float32)  56 us
    psum x1, blocking collectives, body(): lax.psum((local_sums[0], local_norms[0]), ('seq', 'ffn'))  54.5 us
    dot_general x12, matrix products, contract_cols(): lax.dot_general(left, right, (((1,), (1,)), ((), ())), preferred_element_...  39.7 us
  transfers between devices with their start and end apart: 13, of which 4 were waited for; matrix products, arithmetic and copies ran while one was open for 63% of the time, Pallas kernels for 0%

commit v1 on v0

v1 whole, which is shorter than its diff:
```python
import functools
import math

import jax
import jax.numpy as jnp
from jax import lax
from jax.experimental import pallas as pl
from jax.experimental.pallas import tpu as pltpu
from jax.sharding import PartitionSpec as P

BF, F32 = jnp.bfloat16, jnp.float32
EPS = 1e-5
LONG = 64
TILE = 256
PAIR = 128
CHUNK = 1024
FEAT = 256
VMEM_LIMIT = 60 << 20
LOG16 = math.log(16.0)


def dot(a, b):
    return jnp.dot(a, b, preferred_element_type=F32)


def dot_nt(a, b):
    return lax.dot_general(a, b, (((1,), (1,)), ((), ())), preferred_element_type=F32)


def dot_tn(a, b):
    return lax.dot_general(a, b, (((0,), (0,)), ((), ())), preferred_element_type=F32)


def iota(shape, dim):
    return lax.broadcasted_iota(jnp.int32, shape, dim)


def normalize(rows):
    mean = jnp.mean(rows, axis=-1, keepdims=True)
    centred = rows - mean
    spread = jnp.mean(centred * centred, axis=-1, keepdims=True)
    scale = lax.rsqrt(spread + EPS)
    return centred * scale, scale


def norm_back(grad, xhat, scale):
    return scale * (
        grad
        - jnp.mean(grad, axis=-1, keepdims=True)
        - xhat * jnp.mean(grad * xhat, axis=-1, keepdims=True)
    )


def head_sums(pair):
    first = iota(pair.shape, 1) < PAIR // 2
    zero = jnp.zeros_like(pair)
    return (
        jnp.sum(jnp.where(first, pair, zero), axis=-1, keepdims=True),
        jnp.sum(jnp.where(first, zero, pair), axis=-1, keepdims=True),
    )


def features(scaled, scaled_low, proj, pair):
    cols = slice(pair * PAIR, (pair + 1) * PAIR)
    part = scaled[:, cols]
    first, second = head_sums(part * part)
    product = dot(scaled_low[:, cols], proj[pair])
    return jnp.concatenate(
        [
            jnp.exp(product[:, :FEAT] - (0.5 * first + LOG16)).astype(BF),
            jnp.exp(product[:, FEAT:] - (0.5 * second + LOG16)).astype(BF),
        ],
        axis=1,
    )


def lane_half(shape):
    return iota(shape, 1) < FEAT


def block_sums(both, norm):
    keep = (iota((PAIR, 2 * FEAT), 0) < PAIR // 2) == lane_half((PAIR, 2 * FEAT))
    zero = jnp.zeros((PAIR, 2 * FEAT), F32)
    return jnp.concatenate(
        [
            jnp.where(keep, both, zero).astype(BF),
            jnp.where(keep, jnp.broadcast_to(norm, (PAIR, 2 * FEAT)), zero).astype(BF),
        ],
        axis=0,
    )


def block_grads(both, norm):
    keep = (iota((PAIR, 2 * FEAT), 0) < PAIR // 2) == lane_half((PAIR, 2 * FEAT))
    zero = jnp.zeros((PAIR, 2 * FEAT), F32)
    row = iota((PAIR, 2 * FEAT), 0)
    high = norm.astype(BF).astype(F32)
    wide = jnp.broadcast_to(high, (PAIR, 2 * FEAT))
    rest = jnp.broadcast_to(norm - high, (PAIR, 2 * FEAT))
    return jnp.concatenate(
        [
            jnp.where(keep, both, zero).astype(BF),
            jnp.where(row == 0, wide, jnp.where(row == 1, rest, zero)).astype(BF),
        ],
        axis=0,
    )


def pack_pair(both):
    return jnp.where(lane_half((PAIR // 2, 2 * FEAT)), both[: PAIR // 2], both[PAIR // 2 :])


def unpack_pair(packed):
    return jnp.concatenate([packed, packed], axis=0)


def value_block(values, cols):
    part = values[:, cols]
    first = iota(part.shape, 1) < PAIR // 2
    zero = jnp.zeros_like(part)
    one = jnp.ones_like(part)
    top = jnp.concatenate([jnp.where(first, part, zero), jnp.where(first, one, zero)], axis=1)
    low = jnp.concatenate([jnp.where(first, zero, part), jnp.where(first, zero, one)], axis=1)
    return jnp.concatenate([top, low], axis=0)


def same_small(bounds):
    shape = (2 * LONG, 2 * LONG)

    def label(dim):
        at = iota(shape, dim)
        cut = jnp.where(at < LONG, bounds[0], LONG + bounds[1])
        return jnp.where(at < cut, 1, 0) + jnp.where(at < LONG, 0, 2)

    return label(0) == label(1)


def swap_rows(buffer, cuts):
    most = buffer.shape[1]
    width = buffer.shape[2]
    for batch in range(2):
        head = buffer[batch, LONG : 2 * LONG]
        tail = buffer[batch, most - LONG :]
        small_first = iota((LONG, width), 0) < cuts[batch]
        buffer[batch, LONG : 2 * LONG] = jnp.where(small_first, tail, head)
        buffer[batch, most - LONG :] = jnp.where(small_first, head, tail)


def edge_rows(buffer):
    most = buffer.shape[1]
    return jnp.concatenate(
        [
            buffer[0, :LONG],
            buffer[1, :LONG],
            buffer[0, most - LONG :],
            buffer[1, most - LONG :],
        ],
        axis=0,
    )


def store_edge(buffer, value):
    most = buffer.shape[1]
    buffer[0, :LONG] = value[:LONG]
    buffer[1, :LONG] = value[LONG : 2 * LONG]
    buffer[0, most - LONG :] = value[2 * LONG : 3 * LONG]
    buffer[1, most - LONG :] = value[3 * LONG :]


def digits_of(size):
    out = []
    while size > 1:
        step = 4 if size % 4 == 0 else size
        out.append(step)
        size //= step
    return tuple(out)


class Net:
    def __init__(self, digits, send, recv):
        self.digits = digits
        self.send, self.recv = send, recv
        self.me = lax.axis_index("seq")
        self.core = lax.axis_index("ffn")
        self.slots = {}
        strides = [math.prod(digits[k + 1 :]) for k in range(len(digits))]
        self.own = [lax.rem(lax.div(self.me, s), n) for s, n in zip(strides, digits)]
        self.strides = strides

    def partner(self):
        return (self.me, 1 - self.core)

    def other(self, k, step):
        return lax.rem(self.own[k] + step, self.digits[k])

    def peer(self, k, step):
        return (self.me + (self.other(k, step) - self.own[k]) * self.strides[k], self.core)

    def barrier(self):
        semaphore = pltpu.get_barrier_semaphore()
        peers = [self.partner()] + [
            self.peer(k, step) for k, n in enumerate(self.digits) for step in range(1, n)
        ]
        for peer in peers:
            pl.semaphore_signal(
                semaphore, inc=1, device_id=peer, device_id_type=pl.DeviceIdType.MESH
            )
        pl.semaphore_wait(semaphore, len(peers))

    def copy(self, key, source, target, device):
        slot = self.slots.setdefault(key, len(self.slots))
        return pltpu.make_async_remote_copy(
            src_ref=source,
            dst_ref=target,
            send_sem=self.send.at[slot],
            recv_sem=self.recv.at[slot],
            device_id=device,
            device_id_type=pl.DeviceIdType.MESH,
        )


class Gather:
    def __init__(self, net, name, out):
        self.net, self.name, self.out = net, name, out

    def copies(self, k):
        net = self.net
        depth = len(net.digits)
        if k == depth:
            block = self.out.at[net.core]
            return [net.copy((self.name, "core"), block, block, net.partner())]
        at = (net.core,) + (slice(None),) * k + tuple(net.own[k:])
        block = self.out.at[at]
        return [
            net.copy((self.name, k, step), block, block, net.peer(k, step))
            for step in range(1, net.digits[k])
        ]

    def steps(self):
        depth = len(self.net.digits)

        def start(k):
            for copy in self.copies(k):
                copy.start()

        def follow(k):
            for copy in self.copies(k - 1):
                copy.wait_recv()
            if k <= depth:
                start(k)

        return [functools.partial(start, 0)] + [
            functools.partial(follow, k) for k in range(1, depth + 2)
        ]

    def drain(self):
        for k in range(len(self.net.digits) + 1):
            for copy in self.copies(k):
                copy.wait_send()


class Scatter:
    def __init__(self, net, name, blocks, first, slots, parts, finish, apart=None):
        self.net, self.name = net, name
        self.away = (blocks if apart is None else apart).at[1 - net.core]
        self.held = blocks.at[net.core] if apart is None else blocks
        self.first, self.slots, self.parts, self.finish = first, slots, parts, finish

    @staticmethod
    def scratch(digits, rows, cols):
        shapes = [pltpu.VMEM(digits + (rows, cols), BF)]
        for k in reversed(range(len(digits))):
            shapes.append(pltpu.VMEM((digits[k] - 1,) + digits[:k] + (rows, cols), BF))
        for k in reversed(range(1, len(digits))):
            shapes.append(pltpu.VMEM(digits[:k] + (rows, cols), BF))
        return shapes

    @classmethod
    def of(cls, net, name, blocks, refs, finish, apart=None):
        depth = len(net.digits)
        slots, parts = refs[1 : 1 + depth], refs[1 + depth :]
        return cls(net, name, blocks, refs[0], slots, parts, finish, apart)

    def copies(self, k):
        net = self.net
        depth = len(net.digits)
        if k == 0:
            return [net.copy((self.name, "core"), self.away, self.first, net.partner())]
        digit = depth - k
        held = self.held if k == 1 else self.parts[k - 2]
        copies = []
        for step in range(1, net.digits[digit]):
            at = (slice(None),) * digit + (net.other(digit, step),)
            copies.append(
                net.copy(
                    (self.name, k, step),
                    held.at[at],
                    self.slots[k - 1].at[step - 1],
                    net.peer(digit, step),
                )
            )
        return copies

    def add(self, k):
        net = self.net
        depth = len(net.digits)
        if k == 0:
            lead = net.digits
            for at in _indices(lead):
                mine = self.held[at].astype(F32)
                self.held[at] = (mine + self.first[at].astype(F32)).astype(BF)
            return
        digit = depth - k
        held = self.held if k == 1 else self.parts[k - 2]
        for at in _indices(net.digits[:digit]):
            total = held[at + (net.own[digit],)].astype(F32)
            for step in range(net.digits[digit] - 1):
                total = total + self.slots[k - 1][(step,) + at].astype(F32)
            if digit:
                self.parts[k - 1][at] = total.astype(BF)
            else:
                self.finish(total)

    def steps(self):
        depth = len(self.net.digits)

        def start(k):
            for copy in self.copies(k):
                copy.start()

        def follow(k):
            for copy in self.copies(k - 1):
                copy.wait_recv()
            self.add(k - 1)
            if k <= depth:
                start(k)

        return [functools.partial(start, 0)] + [
            functools.partial(follow, k) for k in range(1, depth + 2)
        ]

    def drain(self):
        for k in range(len(self.net.digits) + 1):
            for copy in self.copies(k):
                copy.wait_send()


def _indices(lead):
    if not lead:
        return [()]
    return [(i,) + rest for i in range(lead[0]) for rest in _indices(lead[1:])]


class Whole:
    def __init__(self, net, name, held, slots):
        self.net, self.name, self.held, self.slots = net, name, held, slots

    @staticmethod
    def scratch(digits, rows, cols):
        return [
            pltpu.VMEM((len(digits) + 2, rows, cols), F32),
            pltpu.VMEM((1 + sum(n - 1 for n in digits), rows, cols), F32),
        ]

    def base(self, k):
        return 0 if k == 0 else 1 + sum(n - 1 for n in self.net.digits[: k - 1])

    def copies(self, k):
        net = self.net
        source = self.held.at[k]
        if k == 0:
            return [net.copy((self.name, 0), source, self.slots.at[0], net.partner())]
        return [
            net.copy(
                (self.name, k, step),
                source,
                self.slots.at[self.base(k) + step - 1],
                net.peer(k - 1, step),
            )
            for step in range(1, net.digits[k - 1])
        ]

    def steps(self):
        depth = len(self.net.digits)

        def start(k):
            for copy in self.copies(k):
                copy.start()

        def follow(k):
            total = self.held[k - 1]
            for i, copy in enumerate(self.copies(k - 1)):
                copy.wait_recv()
                total = total + self.slots[self.base(k - 1) + i]
            self.held[k] = total
            if k <= depth:
                start(k)

        return [functools.partial(start, 0)] + [
            functools.partial(follow, k) for k in range(1, depth + 2)
        ]

    def drain(self):
        for k in range(len(self.net.digits) + 1):
            for copy in self.copies(k):
                copy.wait_send()


def together(*parts):
    most = max(len(part) for part in parts)

    def run(i):
        for part in parts:
            if i < len(part):
                part[i]()

    return [functools.partial(run, i) for i in range(most)]


def block_shape(ways, rows, cols):
    lanes = cols * (rows // 16) // ways
    return 16, lanes


def block_at(digits, index):
    at = []
    for n in reversed(digits):
        at.append(index % n)
        index //= n
    return tuple(reversed(at))


def store_blocks(blocks, row, value):
    lanes = blocks.shape[-1]
    per_row = value.shape[1] // lanes
    ways = (2,) + blocks.shape[1:-2]
    for i in range(value.shape[0] // 16):
        for j in range(per_row):
            at = block_at(ways, (row // 16 + i) * per_row + j)
            blocks[at] = value[16 * i : 16 * i + 16, j * lanes : (j + 1) * lanes]


def load_blocks(blocks, row, rows, cols):
    lanes = blocks.shape[-1]
    per_row = cols // lanes
    ways = (2,) + blocks.shape[1:-2]
    out = []
    for i in range(rows // 16):
        line = [
            blocks[block_at(ways, (row // 16 + i) * per_row + j)] for j in range(per_row)
        ]
        out.append(line[0] if per_row == 1 else jnp.concatenate(line, axis=1))
    return jnp.concatenate(out, axis=0)


class Loads:
    def __init__(self, semaphores):
        self.semaphores = semaphores
        self.count = 0

    def start(self, source, target):
        copy = pltpu.make_async_copy(source, target, self.semaphores.at[self.count])
        self.count += 1
        copy.start()
        return copy


PIECES = ((0, 128), (1088, 64), (128, 192), (320, 256), (576, 256), (832, 256))


def raw_pieces(rows):
    quarter = (rows - 2 * LONG) // 4
    pieces = [(0, 2 * LONG), (rows - LONG, LONG), (2 * LONG, quarter - LONG)]
    return pieces + [(LONG + quarter * i, quarter) for i in range(1, 4)]


def big_start(batch, rows_big, step, tile):
    return TILE + batch * rows_big + step * tile


def attention_forward(
    digits, cuts, x_hbm, vec, wqkv, wo, proj, block,
    k_out, q_out, v_out, ks_out, qs_out, n_out, mix_out, inv_out, att_out, sd_out, small_out, w_out,
    x, kf, qf, v, ks, qs, n, mix, inv, att, sd, small, acc, nacc, parts, total,
    load_sem, store_sem, own_sem, send, recv, whole_held, whole_slots, *slots,
):
    rows = x.shape[1]
    big = rows - 2 * LONG
    pairs = proj.shape[0]
    width = wo.shape[0]
    scale = (PAIR // 2) ** -0.25
    net = Net(digits, send, recv)
    loads = Loads(load_sem)
    pending = {}
    for piece in raw_pieces(rows):
        for batch in range(2):
            span = pl.ds(*piece)
            pending[batch, piece] = loads.start(x_hbm.at[batch, span], x.at[batch, span])
    first, *later = raw_pieces(rows)
    edges = [first, later[0]]
    place = pltpu.make_async_copy(block, w_out.at[(net.core,) + tuple(net.own)], own_sem)
    place.start()
    net.barrier()
    place.wait()
    gather = Gather(net, "w", w_out)
    gather_steps = gather.steps()
    gather_steps[0]()

    def finish(value):
        total[(net.core,) + tuple(net.own)] = value.astype(BF)

    scatter = Scatter.of(net, "s", parts, slots, finish)
    spread = Gather(net, "t", total)
    whole = Whole(net, "n", whole_held, whole_slots)
    scatter_steps = scatter.steps()
    spread_steps = spread.steps()
    depth = len(digits)

    def turn():
        scatter_steps[-1]()
        spread_steps[0]()

    sum_steps = together(scatter_steps[:-1] + [turn] + spread_steps[1:], whole.steps())

    def front(rows_x):
        xhat, _ = normalize(rows_x)
        low = (xhat * vec[0:1] + vec[1:2]).astype(BF)
        raw = dot(low, wqkv[...])
        q = raw[:, :width] * scale
        k = raw[:, width : 2 * width] * scale
        return low, q, k, raw[:, 2 * width :].astype(BF)

    def attend(numer_denom, at, pair):
        cols = slice(pair * PAIR, (pair + 1) * PAIR)
        inverse = 1.0 / numer_denom[:, PAIR:]
        inv[at, cols] = inverse
        mix[at, cols] = (numer_denom[:, :PAIR] * inverse).astype(BF)

    for batch in range(2):
        for piece in edges:
            pending[batch, piece].wait()
    swap_rows(x, [cuts[0, 0], cuts[1, 0]])
    edge = slice(0, TILE)
    x_edge = edge_rows(x)
    low, q, k, values = front(x_edge)
    n[edge] = low
    v[edge] = values
    k_low = k.astype(BF)
    ks[edge] = k_low
    for pair in range(pairs):
        cols = slice(pair * PAIR, (pair + 1) * PAIR)
        feats = slice(pair * 2 * FEAT, (pair + 1) * 2 * FEAT)
        mapped = features(k, k_low, proj, pair)
        kf[edge, feats] = mapped
        for batch in range(2):
            own = slice(batch * LONG, (batch + 1) * LONG)
            both = dot_tn(values[own, cols], mapped[own])
            row = batch * pairs + pair
            store_blocks(parts, row * LONG, pack_pair(both).astype(BF))
            whole_held[0, row : row + 1] = jnp.sum(mapped[own].astype(F32), axis=0, keepdims=True)
    sum_steps[0]()
    q_low = q.astype(BF)
    qs[edge] = q_low
    same = same_small([cuts[0, 1], cuts[1, 1]])
    shorts = slice(2 * LONG, TILE)
    for pair in range(pairs):
        cols = slice(pair * PAIR, (pair + 1) * PAIR)
        feats = slice(pair * 2 * FEAT, (pair + 1) * 2 * FEAT)
        mapped = features(q, q_low, proj, pair)
        qf[edge, feats] = mapped
        weights = []
        for head in range(2):
            lanes = slice((2 * pair + head) * FEAT, (2 * pair + head + 1) * FEAT)
            score = dot_nt(
                mapped[shorts, head * FEAT : (head + 1) * FEAT], kf[shorts, lanes]
            )
            score = jnp.where(same, score, 0.0).astype(BF)
            small[2 * pair + head] = score
            weights.append(score)
        attend(
            dot(jnp.concatenate(weights, axis=1), value_block(values[shorts], cols)), shorts, pair
        )

    stores = []

    def store(source, target, at, slot):
        copy = pltpu.make_async_copy(source.at[at], target.at[at], store_sem.at[slot])
        copy.start()

    store(kf, k_out, pl.ds(0, TILE), 0)
    store(qf, q_out, pl.ds(0, TILE), 1)
    store(v, v_out, pl.ds(0, TILE), 2)
    store(ks, ks_out, pl.ds(0, TILE), 3)
    store(qs, qs_out, pl.ds(0, TILE), 4)
    store(n, n_out, pl.ds(0, TILE), 5)
    small_copy = pltpu.make_async_copy(small, small_out, store_sem.at[9])
    small_copy.start()

    for piece in later[1:]:
        for batch in range(2):
            pending[batch, piece].wait()
    acc[...] = jnp.zeros_like(acc)
    nacc[...] = jnp.zeros_like(nacc)
    per = big // TILE
    comm = [None] * (2 * 2 * per)
    for i, step in enumerate(sum_steps[1:]):
        comm[i] = step
    for i, step in enumerate(gather_steps[1:]):
        spot = 1 + 3 * i
        comm[spot] = step if comm[spot] is None else functools.partial(_both, comm[spot], step)

    def pass_one(t, _):
        batch, step = lax.div(t, per), lax.rem(t, per)
        for i in range(2 * per):
            if comm[i] is not None:
                pl.when(t == i)(comm[i])
        raw_at = pl.ds(pl.multiple_of(LONG + step * TILE, LONG), TILE)
        at = pl.ds(pl.multiple_of(TILE + t * TILE, TILE), TILE)
        low, q, k, values = front(x[batch, raw_at])
        n[at] = low
        v[at] = values
        k_low = k.astype(BF)
        q_low = q.astype(BF)
        ks[at] = k_low
        qs[at] = q_low
        for pair in range(pairs):
            cols = slice(pair * PAIR, (pair + 1) * PAIR)
            feats = slice(pair * 2 * FEAT, (pair + 1) * 2 * FEAT)
            mapped = features(k, k_low, proj, pair)
            kf[at, feats] = mapped
            acc[batch, pair] += dot_tn(values[:, cols], mapped)
            nacc[batch, pair] += jnp.sum(mapped.astype(F32), axis=0, keepdims=True)
            qf[at, feats] = features(q, q_low, proj, pair)
        store(kf, k_out, at, 0)
        store(qf, q_out, at, 1)
        store(v, v_out, at, 2)
        store(ks, ks_out, at, 3)
        store(qs, qs_out, at, 4)
        store(n, n_out, at, 5)
        return 0

    lax.fori_loop(0, 2 * per, pass_one, 0)
    for batch in range(2):
        for pair in range(pairs):
            sd[batch, pair] = block_sums(acc[batch, pair], nacc[batch, pair])

    def pass_two(t, _):
        batch, step = lax.div(t, per), lax.rem(t, per)
        for i in range(2 * per):
            if comm[2 * per + i] is not None:
                pl.when(t == i)(comm[2 * per + i])
        raw_at = pl.ds(pl.multiple_of(LONG + step * TILE, LONG), TILE)
        at = pl.ds(pl.multiple_of(TILE + t * TILE, TILE), TILE)
        for pair in range(pairs):
            feats = slice(pair * 2 * FEAT, (pair + 1) * 2 * FEAT)
            attend(dot_nt(qf[at, feats], sd[batch, pair]), at, pair)
        att[at] = x[batch, raw_at] + dot(mix[at], wo[...]) + vec[2:3]
        store(mix, mix_out, at, 6)
        store(inv, inv_out, at, 7)
        store(att, att_out, at, 8)
        return 0

    lax.fori_loop(0, 2 * per, pass_two, 0)
    for batch in range(2):
        own = slice(batch * LONG, (batch + 1) * LONG)
        for pair in range(pairs):
            feats = slice(pair * 2 * FEAT, (pair + 1) * 2 * FEAT)
            row = batch * pairs + pair
            packed = load_blocks(total, row * LONG, LONG, 2 * FEAT).astype(F32)
            sd[2 + batch, pair] = block_sums(
                unpack_pair(packed), whole_held[depth + 1, row : row + 1]
            )
            attend(dot_nt(qf[own, feats], sd[2 + batch, pair]), own, pair)
    att[edge] = edge_rows(x) + dot(mix[edge], wo[...]) + vec[2:3]
    store(mix, mix_out, pl.ds(0, TILE), 6)
    store(inv, inv_out, pl.ds(0, TILE), 7)
    store(att, att_out, pl.ds(0, TILE), 8)
    sd_copy = pltpu.make_async_copy(sd, sd_out, store_sem.at[10])
    sd_copy.start()
    pairs_out = (
        (kf, k_out), (qf, q_out), (v, v_out), (ks, ks_out), (qs, qs_out), (n, n_out),
        (mix, mix_out), (inv, inv_out), (att, att_out),
    )
    for slot, (source, target) in enumerate(pairs_out):
        pltpu.make_async_copy(source, target, store_sem.at[slot]).wait()
    small_copy.wait()
    sd_copy.wait()
    gather.drain()
    scatter.drain()
    spread.drain()
    whole.drain()


def _both(first, second):
    first()
    second()


def feed_forward(
    cuts, cot_hbm, att_hbm, mix_hbm, inv_hbm, w_hbm, wo, vec, up_bias,
    out_hbm, ga_out, g_out, x_out, wo_grad, vec_grad, bias_grad,
    cot, att, mix, inv, w, up, down, dup, ddown, gr, load_sem, store_sem,
):
    rows = cot.shape[1]
    big = rows - 2 * LONG
    width = wo.shape[0]
    pairs = width // PAIR
    tile = big // 2
    loads = Loads(load_sem)
    lead = w.shape[:-2]
    deep = w.shape[-2] // 2
    half = w.shape[-1]
    wait_w = loads.start(w_hbm, w)
    pending = {}
    pieces = raw_pieces(rows)
    inner = [(0, TILE)] + [(TILE + tile * i, tile) for i in range(2 * big // tile)]
    for piece in pieces[:2]:
        for batch in range(2):
            span = pl.ds(*piece)
            pending[batch, piece] = loads.start(cot_hbm.at[batch, span], cot.at[batch, span])
    waits = []
    for i, piece in enumerate(inner):
        span = pl.ds(*piece)
        waits.append(
            [
                loads.start(a.at[span], b.at[span])
                for a, b in ((att_hbm, att), (mix_hbm, mix), (inv_hbm, inv))
            ]
        )
        if i == 0:
            for piece in pieces[2:]:
                for batch in range(2):
                    span = pl.ds(*piece)
                    pending[batch, piece] = loads.start(
                        cot_hbm.at[batch, span], cot.at[batch, span]
                    )
    wait_w.wait()
    group = max(1, 16 // deep)
    members = _indices(lead[1:])
    for core in range(2):
        cols = slice(core * half, (core + 1) * half)
        for first in range(0, len(members), group):
            parts = [w[(core,) + members[first + i]] for i in range(group)]
            at = slice(first * deep, (first + group) * deep)
            if group == 1:
                up[at, cols] = parts[0][:deep]
                down[at, cols] = parts[0][deep:]
            else:
                up[at, cols] = jnp.concatenate([part[:deep] for part in parts], axis=0)
                down[at, cols] = jnp.concatenate([part[deep:] for part in parts], axis=0)
    for batch in range(2):
        for piece in pieces[:2]:
            pending[batch, piece].wait()
    swap_rows(cot, [cuts[0, 0], cuts[1, 0]])
    dup[...] = jnp.zeros_like(dup)
    ddown[...] = jnp.zeros_like(ddown)
    wo_grad[...] = jnp.zeros_like(wo_grad)
    vec_grad[...] = jnp.zeros_like(vec_grad)
    bias_grad[...] = jnp.zeros_like(bias_grad)

    def add_row(at, value):
        vec_grad[at : at + 1] += jnp.sum(value, axis=0, keepdims=True)

    def block(att_rows, grad_out, at):
        xhat, scale = normalize(att_rows)
        second = (xhat * vec[0:1] + vec[1:2]).astype(BF)
        grad_low = grad_out.astype(BF)
        second_turned, grad_turned = second.T, grad_low.T
        branch = grad_second = None
        for first in range(0, up.shape[1], CHUNK):
            cols = slice(first, first + CHUNK)
            hidden = dot(second, up[:, cols]) + up_bias[:, cols]
            gauss = jnp.exp(-0.5 * hidden * hidden) * (1.0 / math.sqrt(2.0 * math.pi))
            cdf = 0.5 + 0.5 * lax.erf(hidden * math.sqrt(0.5))
            active = (hidden * cdf).astype(BF)
            slope = cdf + hidden * gauss
            grad_hidden = (dot(grad_low, down[:, cols]) * slope).astype(BF)
            term = dot_nt(active, down[:, cols])
            grad_term = dot_nt(grad_hidden, up[:, cols])
            branch = term if branch is None else branch + term
            grad_second = grad_term if grad_second is None else grad_second + grad_term
            dup[:, cols] += dot(second_turned, grad_hidden)
            ddown[:, cols] += dot(grad_turned, active)
            bias_grad[:, cols] += jnp.sum(grad_hidden.astype(F32), axis=0, keepdims=True)
        output = att_rows + branch + vec[2:3]
        grad_att = grad_out + norm_back(grad_second * vec[0:1], xhat, scale)
        add_row(2, grad_att)
        add_row(3, grad_second * xhat)
        add_row(4, grad_second)
        add_row(5, grad_out)
        grad_att_low = grad_att.astype(BF)
        mixed = mix[at]
        wo_grad[...] += dot_tn(mixed, grad_att_low)
        grad_mixed = dot_nt(grad_att_low, wo[...]).astype(BF).astype(F32)
        for pair in range(pairs):
            cols = slice(pair * PAIR, (pair + 1) * PAIR)
            part = grad_mixed[:, cols]
            inverse = inv[at, cols]
            first, last = head_sums(part * mixed[:, cols].astype(F32))
            lane = iota(part.shape, 1)
            grad_denom = -jnp.where(lane < PAIR // 2, first, last) * inverse
            high = grad_denom.astype(BF).astype(F32)
            both = jnp.where(lane % (PAIR // 2) < PAIR // 4, high, grad_denom - high)
            gr[at, 2 * pair * PAIR : (2 * pair + 1) * PAIR] = (part * inverse).astype(BF)
            gr[at, (2 * pair + 1) * PAIR : (2 * pair + 2) * PAIR] = (
                both * (4.0 / PAIR)
            ).astype(BF)
        att[at] = grad_att
        return output

    def store(at):
        pltpu.make_async_copy(att.at[at], ga_out.at[at], store_sem.at[0]).start()
        pltpu.make_async_copy(gr.at[at], g_out.at[at], store_sem.at[1]).start()

    edge = pl.ds(0, TILE)
    for copy in waits[0]:
        copy.wait()
    cot_edge = edge_rows(cot)
    store_edge(cot, block(att[edge], cot_edge, edge))
    store(edge)
    for batch in range(2):
        for piece in pieces[2:]:
            pending[batch, piece].wait()
    for more in waits[1:]:
        for copy in more:
            copy.wait()
    per = big // tile

    def one(t, _):
        batch, step = lax.div(t, per), lax.rem(t, per)
        raw_at = pl.ds(pl.multiple_of(LONG + step * tile, LONG), tile)
        at = pl.ds(pl.multiple_of(TILE + t * tile, TILE), tile)
        cot[batch, raw_at] = block(att[at], cot[batch, raw_at], at)
        store(at)
        return 0

    lax.fori_loop(0, 2 * per, one, 0)
    swap_rows(cot, [cuts[0, 0], cuts[1, 0]])
    out_copy = pltpu.make_async_copy(cot, out_hbm, store_sem.at[2])
    out_copy.start()
    for core in range(2):
        cols = slice(core * half, (core + 1) * half)
        for i, member in enumerate(members):
            at = slice(i * deep, (i + 1) * deep)
            w[(core,) + member] = jnp.concatenate(
                [dup[at, cols], ddown[at, cols]], axis=0
            ).astype(BF)
    x_copy = pltpu.make_async_copy(w, x_out, store_sem.at[3])
    x_copy.start()
    pltpu.make_async_copy(att, ga_out, store_sem.at[0]).wait()
    pltpu.make_async_copy(gr, g_out, store_sem.at[1]).wait()
    out_copy.wait()
    x_copy.wait()


def attention_backward(
    digits, cuts, x_hbm, ga_hbm, g_hbm, k_hbm, q_hbm, v_hbm, ks_hbm, qs_hbm, n_hbm,
    sd_hbm, small, ffn_hbm, wo_grad, vec_in, bias_in, vec, wqkv, back,
    in_grad, ffn_out, shared_out, vec_out,
    kf, v, ks, qs, n, sd, sg, ffn, total, parts, long_total,
    load_sem, store_sem, send, recv, *refs,
):
    rows = x_hbm.shape[1]
    big = rows - 2 * LONG
    pairs = back.shape[0]
    width = wqkv.shape[0]
    inner_rows = kf.shape[0]
    scale = (PAIR // 2) ** -0.25
    depth = len(digits)
    net = Net(digits, send, recv)
    each = 2 * depth
    ffn_refs, refs = refs[:each], refs[each:]
    shared_refs, refs = refs[:each], refs[each:]
    long_refs, refs = refs[:each], refs[each:]
    norm_held, norm_slots, vec_held, vec_slots = refs
    loads = Loads(load_sem)
    per = big // TILE
    steps = 2 * per
    shorts = slice(2 * LONG, TILE)
    edge = slice(0, TILE)
    same = same_small([cuts[0, 1], cuts[1, 1]])

    def finish_ffn(value):
        ffn_out[...] = value

    ffn_sum = Scatter.of(net, "f", ffn, ffn_refs, finish_ffn, apart=ffn_hbm)

    def finish_long(value):
        long_total[(net.core,) + tuple(net.own)] = value.astype(BF)

    long_sum = Scatter.of(net, "s", parts, long_refs, finish_long)
    long_spread = Gather(net, "t", long_total)
    norm_sum = Whole(net, "n", norm_held, norm_slots)
    vec_sum = Whole(net, "v", vec_held, vec_slots)

    def all_reduce(scatter, spread):
        first, second = scatter.steps(), spread.steps()
        return first[:-1] + [functools.partial(_both, first[-1], second[0])] + second[1:]

    long_steps = together(all_reduce(long_sum, long_spread), norm_sum.steps())
    ffn_steps = ffn_sum.steps()
    vec_steps = vec_sum.steps()
    comm = [[] for _ in range(2 * steps)]
    for i, step in enumerate(long_steps[1:]):
        comm[i].append(step)
    for i, step in enumerate(ffn_steps[1:]):
        comm[min(1 + 4 * i, 2 * steps - 1)].append(step)

    def talk(t, base):
        for i in range(steps):
            if comm[base + i]:
                pl.when(t == i)(functools.partial(_all, comm[base + i]))

    def feat_lanes(pair):
        return slice(pair * 2 * FEAT, (pair + 1) * 2 * FEAT)

    def pair_cols(pair):
        return slice(pair * PAIR, (pair + 1) * PAIR)

    def grad_lanes(pair):
        return slice(2 * pair * PAIR, (2 * pair + 2) * PAIR)

    def feature_back(grad, mapped, scaled, pair):
        term = (grad * mapped.astype(F32)).astype(BF)
        both = dot(term, back[pair])
        return (
            (both[:, :PAIR] - scaled[:, pair_cols(pair)].astype(F32) * both[:, PAIR:]) * scale
        ).astype(BF)

    def norm_rows(both):
        return jnp.where(
            lane_half((1, 2 * FEAT)),
            jnp.sum(both[PAIR : PAIR + PAIR // 2], axis=0, keepdims=True),
            jnp.sum(both[PAIR + PAIR // 2 :], axis=0, keepdims=True),
        )

    def ones_beside(values):
        return jnp.concatenate([values, jnp.ones_like(values)], axis=1)

    inner = [(0, TILE)] + [(TILE + big * i, big) for i in range(2)]

    def load(pairs_of):
        waits = []
        for piece in inner:
            span = pl.ds(*piece)
            waits.append([loads.start(a.at[span], b.at[span]) for a, b in pairs_of])
        return waits

    def query_phase(qf, gr, acc):
        early = load([(g_hbm, gr), (q_hbm, qf), (qs_hbm, qs), (k_hbm, kf), (v_hbm, v), (ks_hbm, ks)])
        wait_sd = loads.start(sd_hbm, sd)
        wait_ffn = loads.start(ffn_hbm.at[net.core], ffn)
        late = load([(n_hbm, n)])
        net.barrier()
        for copy in early[0]:
            copy.wait()
        for batch in range(2):
            own = slice(batch * LONG, (batch + 1) * LONG)
            for pair in range(pairs):
                both = dot_tn(gr[own, grad_lanes(pair)], qf[own, feat_lanes(pair)])
                row = batch * pairs + pair
                store_blocks(parts, row * LONG, pack_pair(both[:PAIR]).astype(BF))
                norm_held[0, row : row + 1] = norm_rows(both)
        long_steps[0]()
        ffn_steps[0]()
        wait_sd.wait()
        for pair in range(pairs):
            lanes, cols = feat_lanes(pair), pair_cols(pair)
            mapped_q, mapped_k = qf[edge, lanes], kf[shorts, lanes]
            grads, values = gr[edge, grad_lanes(pair)], v[shorts, cols]
            grad_q = [
                dot(grads[batch * LONG : (batch + 1) * LONG], sd[2 + batch, pair])
                for batch in range(2)
            ]
            weight = dot_nt(grads[shorts], value_block(values, slice(0, PAIR)))
            more_q, more_k, more_v = [], [], []
            for head in range(2):
                own = slice(head * FEAT, (head + 1) * FEAT)
                part = jnp.where(same, weight[:, head * PAIR : (head + 1) * PAIR], 0.0).astype(BF)
                more_q.append(dot(part, mapped_k[:, own]))
                more_k.append(dot_tn(part, mapped_q[shorts, own]))
                more_v.append(dot_tn(small[2 * pair + head], grads[shorts, :PAIR]))
            grad_q.append(jnp.concatenate(more_q, axis=1))
            grad_k = jnp.concatenate(more_k, axis=1)
            grad_v = jnp.where(iota((2 * LONG, PAIR), 1) < PAIR // 2, more_v[0], more_v[1])
            qs[edge, cols] = feature_back(
                jnp.concatenate(grad_q, axis=0), mapped_q, qs[edge], pair
            )
            ks[shorts, cols] = feature_back(grad_k, mapped_k, ks[shorts], pair)
            v[shorts, cols] = grad_v.astype(BF)
        for more in early[1:] + late:
            for copy in more:
                copy.wait()
        wait_ffn.wait()
        acc[...] = jnp.zeros_like(acc)

        def queries(t, _):
            batch = lax.div(t, per)
            talk(t, 0)
            at = pl.ds(pl.multiple_of(TILE + t * TILE, TILE), TILE)
            for pair in range(pairs):
                mapped = qf[at, feat_lanes(pair)]
                grads = gr[at, grad_lanes(pair)]
                acc[batch, pair] += dot_tn(grads, mapped)
                grad = dot(grads, sd[batch, pair])
                qs[at, pair_cols(pair)] = feature_back(grad, mapped, qs[at], pair)
            return 0

        lax.fori_loop(0, steps, queries, 0)
        for batch in range(2):
            for pair in range(pairs):
                both = acc[batch, pair]
                sg[batch, pair] = block_grads(both[:PAIR], norm_rows(both))

    def key_phase(x, ga, wgrad, shared):
        wait_x = [loads.start(x_hbm, x), loads.start(ga_hbm, ga)]
        wgrad[...] = jnp.zeros_like(wgrad)

        def finish_shared(value):
            total[(net.core,) + tuple(net.own)] = value.astype(BF)

        shared_sum = Scatter.of(net, "g", shared, shared_refs, finish_shared)
        shared_spread = Gather(net, "h", total)
        shared_steps = all_reduce(shared_sum, shared_spread)

        def add_weights(at):
            turned = n[at].T
            wgrad[:, :width] += dot(turned, qs[at])
            wgrad[:, width : 2 * width] += dot(turned, ks[at])
            wgrad[:, 2 * width :] += dot(turned, v[at])

        def keys(t, _):
            batch = lax.div(t, per)
            talk(t, steps)
            at = pl.ds(pl.multiple_of(TILE + t * TILE, TILE), TILE)
            for pair in range(pairs):
                mapped = kf[at, feat_lanes(pair)]
                grad = dot(ones_beside(v[at, pair_cols(pair)]), sg[batch, pair])
                v[at, pair_cols(pair)] = dot_nt(mapped, sg[batch, pair, :PAIR]).astype(BF)
                ks[at, pair_cols(pair)] = feature_back(grad, mapped, ks[at], pair)
            add_weights(at)
            return 0

        lax.fori_loop(0, steps, keys, 0)
        for batch in range(2):
            own = slice(batch * LONG, (batch + 1) * LONG)
            for pair in range(pairs):
                lanes, cols = feat_lanes(pair), pair_cols(pair)
                row = batch * pairs + pair
                packed = load_blocks(long_total, row * LONG, LONG, 2 * FEAT).astype(F32)
                grads = block_grads(unpack_pair(packed), norm_held[depth + 1, row : row + 1])
                mapped = kf[own, lanes]
                grad = dot(ones_beside(v[own, cols]), grads)
                v[own, cols] = dot_nt(mapped, grads[:PAIR]).astype(BF)
                ks[own, cols] = feature_back(grad, mapped, ks[own], pair)
        add_weights(edge)
        for i in range(width // 16):
            at = slice(16 * i, 16 * i + 16)
            line = jnp.concatenate([wgrad[at], wo_grad[at]], axis=1).astype(BF)
            store_blocks(shared, 16 * i, line)
        shared_steps[0]()
        for copy in wait_x:
            copy.wait()
        swap_rows(x, [cuts[0, 0], cuts[1, 0]])
        vec_held[0] = jnp.zeros(vec_held.shape[1:], F32)
        vec_held[0, 2:6] = vec_in[2:6]
        for i in range(bias_in.shape[1] // width):
            vec_held[0, 6 + i : 7 + i] = bias_in[:, i * width : (i + 1) * width]

        def last(rows_x, rows_ga, at):
            xhat, spread = normalize(rows_x)
            grad = (
                dot_nt(qs[at], wqkv[:, :width])
                + dot_nt(ks[at], wqkv[:, width : 2 * width])
                + dot_nt(v[at], wqkv[:, 2 * width :])
            )
            vec_held[0, 0:1] += jnp.sum(grad * xhat, axis=0, keepdims=True)
            vec_held[0, 1:2] += jnp.sum(grad, axis=0, keepdims=True)
            return rows_ga + norm_back(grad * vec[0:1], xhat, spread)

        store_edge(x, last(edge_rows(x), ga[edge], edge))
        final = [[] for _ in range(steps)]
        for i, step in enumerate(shared_steps[1:]):
            final[min(i, steps - 1)].append(step)

        def inputs(t, _):
            batch, step = lax.div(t, per), lax.rem(t, per)
            for i in range(steps):
                if final[i]:
                    pl.when(t == i)(functools.partial(_all, final[i]))
            raw_at = pl.ds(pl.multiple_of(LONG + step * TILE, LONG), TILE)
            at = pl.ds(pl.multiple_of(TILE + t * TILE, TILE), TILE)
            x[batch, raw_at] = last(x[batch, raw_at], ga[at], at)
            return 0

        lax.fori_loop(0, steps, inputs, 0)
        vec_steps[0]()
        swap_rows(x, [cuts[0, 0], cuts[1, 0]])
        copy = pltpu.make_async_copy(x, in_grad, store_sem.at[0])
        copy.start()
        spread_copy = pltpu.make_async_copy(total, shared_out, store_sem.at[1])
        spread_copy.start()
        for step in vec_steps[1:]:
            step()
        vec_out[...] = vec_held[depth + 1]
        copy.wait()
        spread_copy.wait()
        shared_sum.drain()
        shared_spread.drain()

    wide = kf.shape[1]
    pl.run_scoped(
        query_phase,
        pltpu.VMEM((inner_rows, wide), BF),
        pltpu.VMEM((inner_rows, 2 * width), BF),
        pltpu.VMEM((2, pairs, 2 * PAIR, 2 * FEAT), F32),
    )
    pl.run_scoped(
        key_phase,
        pltpu.VMEM(x_hbm.shape, F32),
        pltpu.VMEM((inner_rows, width), F32),
        pltpu.VMEM((width, 3 * width), F32),
        pltpu.VMEM(total.shape, BF),
    )
    for item in (ffn_sum, long_sum, long_spread, norm_sum, vec_sum):
        item.drain()


def _all(steps):
    for step in steps:
        step()


def body(
    inputs,
    lengths,
    first_gain,
    first_shift,
    query_weight,
    key_weight,
    value_weight,
    output_weight,
    output_bias,
    projection,
    second_gain,
    second_shift,
    up_weight,
    up_bias,
    down_weight,
    down_bias,
    cotangent,
):
    heads, head_size, feats = projection.shape
    batches, rows, width = inputs.shape
    digits = digits_of(lax.axis_size("seq"))
    ways = 2 * math.prod(digits)
    depth = len(digits)
    pairs = heads // 2
    big = rows - 2 * LONG
    inner = TILE + batches * big
    deep, half = up_weight.shape
    hidden = up_bias.shape[0]

    lens = lengths[:, 0, :]
    cut = jnp.where(
        lens[:, 0] == big, 0, jnp.where(lens[:, 1] == big, lens[:, 0], lens[:, 0] + lens[:, 1])
    )
    bound = jnp.where(lens[:, 0] == big, lens[:, 1], lens[:, 0])
    cuts = jnp.stack([cut, bound], axis=1)
    wqkv = jnp.concatenate([query_weight, key_weight, value_weight], axis=1).astype(BF)
    wo = output_weight.astype(BF)
    proj_low = projection.astype(BF).reshape(pairs, 2, head_size, feats)
    zero = jnp.zeros((pairs, head_size, feats), BF)
    proj = jnp.concatenate(
        [
            jnp.concatenate([proj_low[:, 0], zero], axis=2),
            jnp.concatenate([zero, proj_low[:, 1]], axis=2),
        ],
        axis=1,
    )
    turned = jnp.swapaxes(proj_low, 2, 3)
    gap = jnp.zeros((pairs, feats, head_size), BF)
    one = jnp.ones((pairs, feats, head_size), BF)
    back = jnp.concatenate(
        [
            jnp.concatenate([turned[:, 0], gap, one, gap], axis=2),
            jnp.concatenate([gap, turned[:, 1], gap, one], axis=2),
        ],
        axis=1,
    )
    block = jnp.concatenate([up_weight, down_weight.T], axis=0).astype(BF)

    hbm = pl.BlockSpec(memory_space=pl.ANY)
    vmem = pl.BlockSpec(memory_space=pltpu.VMEM)
    smem = pl.BlockSpec(memory_space=pltpu.SMEM)

    def shape(*dims, dtype=BF):
        return jax.ShapeDtypeStruct(dims, dtype)

    wide = 2 * FEAT * pairs
    long_block = block_shape(ways, batches * pairs * LONG, 2 * FEAT)
    inner_shapes = [
        ((inner, wide), BF), ((inner, wide), BF), ((inner, width), BF), ((inner, width), BF),
        ((inner, width), BF), ((inner, width), BF), ((inner, width), BF), ((inner, width), F32),
        ((inner, width), F32), ((4, pairs, 2 * PAIR, 2 * FEAT), BF),
        ((heads, 2 * LONG, 2 * LONG), BF),
    ]
    kf, qf, v, ks, qs, n, mix, inv, att, sd, small, w = pl.pallas_call(
        functools.partial(attention_forward, digits),
        out_shape=[shape(*dims, dtype=kind) for dims, kind in inner_shapes]
        + [shape(2, *digits, 2 * deep, half)],
        in_specs=[smem, hbm, vmem, vmem, vmem, vmem, vmem],
        out_specs=[hbm] * 12,
        scratch_shapes=[pltpu.VMEM(inputs.shape, F32)]
        + [pltpu.VMEM(dims, kind) for dims, kind in inner_shapes]
        + [
            pltpu.VMEM((batches, pairs, PAIR, 2 * FEAT), F32),
            pltpu.VMEM((batches, pairs, 1, 2 * FEAT), F32),
            pltpu.VMEM((2,) + digits + long_block, BF),
            pltpu.VMEM((2,) + digits + long_block, BF),
            pltpu.SemaphoreType.DMA((16,)),
            pltpu.SemaphoreType.DMA((16,)),
            pltpu.SemaphoreType.DMA,
            pltpu.SemaphoreType.DMA((64,)),
            pltpu.SemaphoreType.DMA((64,)),
        ]
        + Whole.scratch(digits, batches * pairs, 2 * FEAT)
        + Scatter.scratch(digits, *long_block),
        compiler_params=pltpu.CompilerParams(
            collective_id=0, has_side_effects=True, vmem_limit_bytes=VMEM_LIMIT
        ),
        name="attention_forward",
    )(
        cuts,
        inputs,
        jnp.stack([first_gain, first_shift, output_bias]),
        wqkv,
        wo,
        proj,
        block,
    )

    output, ga, gr, ffn, wo_grad, vec_in, bias_in = pl.pallas_call(
        feed_forward,
        out_shape=[
            shape(*inputs.shape, dtype=F32),
            shape(inner, width, dtype=F32),
            shape(inner, 2 * width),
            shape(2, *digits, 2 * deep, half),
            shape(width, width, dtype=F32),
            shape(8, width, dtype=F32),
            shape(1, hidden, dtype=F32),
        ],
        in_specs=[smem, hbm, hbm, hbm, hbm, hbm, vmem, vmem, vmem],
        out_specs=[hbm] * 4 + [vmem] * 3,
        scratch_shapes=[
            pltpu.VMEM(inputs.shape, F32),
            pltpu.VMEM((inner, width), F32),
            pltpu.VMEM((inner, width), BF),
            pltpu.VMEM((inner, width), F32),
            pltpu.VMEM((2,) + digits + (2 * deep, half), BF),
            pltpu.VMEM((width, hidden), BF),
            pltpu.VMEM((width, hidden), BF),
            pltpu.VMEM((width, hidden), F32),
            pltpu.VMEM((width, hidden), F32),
            pltpu.VMEM((inner, 2 * width), BF),
            pltpu.SemaphoreType.DMA((32,)),
            pltpu.SemaphoreType.DMA((4,)),
        ],
        compiler_params=pltpu.CompilerParams(vmem_limit_bytes=VMEM_LIMIT),
        name="feed_forward",
    )(
        cuts,
        cotangent,
        att,
        mix,
        inv,
        w,
        wo,
        jnp.stack([second_gain, second_shift, down_bias]),
        up_bias[None],
    )

    shared_block = block_shape(ways, width, 4 * width)
    in_grad, ffn_grad, shared, vectors = pl.pallas_call(
        functools.partial(attention_backward, digits),
        out_shape=[
            shape(*inputs.shape, dtype=F32),
            shape(2 * deep, half, dtype=F32),
            shape(2, *digits, *shared_block),
            shape(16, width, dtype=F32),
        ],
        in_specs=[smem] + [hbm] * 10 + [vmem, hbm] + [vmem] * 6,
        out_specs=[hbm, vmem, hbm, vmem],
        scratch_shapes=[
            pltpu.VMEM((inner, wide), BF),
            pltpu.VMEM((inner, width), BF),
            pltpu.VMEM((inner, width), BF),
            pltpu.VMEM((inner, width), BF),
            pltpu.VMEM((inner, width), BF),
            pltpu.VMEM((4, pairs, 2 * PAIR, 2 * FEAT), BF),
            pltpu.VMEM((batches, pairs, 2 * PAIR, 2 * FEAT), BF),
            pltpu.VMEM(digits + (2 * deep, half), BF),
            pltpu.VMEM((2,) + digits + shared_block, BF),
            pltpu.VMEM((2,) + digits + long_block, BF),
            pltpu.VMEM((2,) + digits + long_block, BF),
            pltpu.SemaphoreType.DMA((32,)),
            pltpu.SemaphoreType.DMA((2,)),
            pltpu.SemaphoreType.DMA((96,)),
            pltpu.SemaphoreType.DMA((96,)),
        ]
        + Scatter.scratch(digits, 2 * deep, half)
        + Scatter.scratch(digits, *shared_block)
        + Scatter.scratch(digits, *long_block)
        + Whole.scratch(digits, batches * pairs, 2 * FEAT)
        + Whole.scratch(digits, 16, width),
        compiler_params=pltpu.CompilerParams(
            collective_id=1, has_side_effects=True, vmem_limit_bytes=VMEM_LIMIT
        ),
        name="attention_backward",
    )(
        cuts, inputs, ga, gr, kf, qf, v, ks, qs, n, sd, small, ffn, wo_grad, vec_in, bias_in,
        jnp.stack([first_gain, first_shift]), wqkv, back,
    )

    per_row = 4 * width // shared_block[1]
    shared = shared.reshape(width // 16, per_row, 16, shared_block[1])
    shared = jnp.swapaxes(shared, 1, 2).reshape(width, 4, width).astype(F32)
    return (
        output,
        in_grad,
        vectors[0],
        vectors[1],
        shared[:, 0],
        shared[:, 1],
        shared[:, 2],
        shared[:, 3],
        vectors[2],
        vectors[3],
        vectors[4],
        ffn_grad[:deep],
        vectors[6 : 6 + hidden // width].reshape(hidden),
        ffn_grad[deep:].T,
        vectors[5],
    )


def solution(mesh):
    rows = P(None, ("seq", "ffn"), None)
    up, down = P("seq", "ffn"), P("ffn", "seq")
    in_specs = (rows, rows) + (P(),) * 10 + (up, P(), down, P(), rows)
    out_specs = (rows, rows) + (P(),) * 9 + (up, P(), down, P())
    return jax.shard_map(body, mesh=mesh, in_specs=in_specs, out_specs=out_specs, check_vma=False)
```

time: 823 us -> 293 us (0.36)
  matrix products: 415 us -> 0 us
  Pallas kernels: 0 us -> 253 us
  blocking collectives: 160 us -> 0 us
  waiting for transfers between devices: 96.5 us -> 0 us
  local copies, waits for them, and re-layouts: 69.6 us -> 24.5 us
  other arithmetic: 55.2 us -> 10.8 us
  between operations: 17 us -> 1.33 us
    dot_general x108 -> x0, matrix products: 415 us -> none  [the longest x8 67.5 us: body(): jnp.einsum('rhd,hdm->rhm', value_heads, sum_grads_low[member], preferred_...]
    pallas_call x0 -> x3, Pallas kernels: none -> 253 us  [the longest x1 133 us: body(): pl.pallas_call(functools.partial(attention_backward, digits), out_shape=[...]
    psum x3 -> x0, blocking collectives: 160 us -> none  [the longest x1 65.9 us: body(): lax.psum((local_sum_grads[0], local_norm_grads[0]), ('seq', 'ffn'))]
    psum x1 -> x0, waiting for transfers between devices: 77.8 us -> none  [body(): lax.psum((shared_now[0], shared_now[1], shared_now[2], shared_now[3], sha...]
    unnamed x526 -> x33, local copies, waits for them, and re-layouts: 58.5 us -> 3.6 us
    reduce_sum x10 -> x0, other arithmetic: 26.5 us -> none  [the longest x3 9.95 us: layer_norm(): return centred * lax.rsqrt(spread + EPSILON) * gain + shift]
    all_gather x6 -> x0, waiting for transfers between devices: 17.8 us -> none  [the longest x1 11.8 us: body(): lax.all_gather(down_shard, 'seq', axis=1, tiled=True)]
    convert_element_type x13 -> x2, other arithmetic: 12.6 us -> 2.08 us  [the longest x1 1.22 us: body(): proj_low = projection.astype(BF).reshape(pairs, 2, head_size, feats)]
  transfers between devices with their start and end apart: 13 -> 0, of which waited for: 4 -> 0; matrix products, arithmetic and copies ran while one was open for 63% -> 0% of each run, Pallas kernels for 0% -> 0%
where the time goes in v1:
time: 293 us; the launch traced here: 289 us
  Pallas kernels  253 us (86%)
  local copies, waits for them, and re-layouts  24.5 us (8%)
  other arithmetic  10.8 us (4%)
    pallas_call x1, Pallas kernels, body(): pl.pallas_call(functools.partial(attention_backward, digits), out_shape=[...  133 us
    pallas_call x1, Pallas kernels, body(): pl.pallas_call(functools.partial(attention_forward, digits), out_shape=[s...  68.6 us
    pallas_call x1, Pallas kernels, body(): pl.pallas_call(feed_forward, out_shape=[shape(*inputs.shape, dtype=F32),...  50.5 us
    slice x1, local copies, waits for them, and re-layouts, body(): shared[:, 3]  10.2 us
    convert_element_type x1, local copies, waits for them, and re-layouts, body(): shared = jnp.swapaxes(shared, 1, 2).reshape(width, 4, width).astype(F32)  6 us

profile of v1, /device:TPU:0, one launch (start us, length us, event | category | flops | bytes accessed | tf_op | source)
XLA Modules:
  0.0 289.2 jit_solution(5780033226340273451)
XLA Ops:
  0.6 0.0 copy-start
  0.7 0.0 copy-start.1
  0.7 1.2 convert_element_type.15
  1.9 0.0 copy-start.2
  1.9 0.8 fusion.2.proj
  2.8 0.8 compare_select_fusion.1
  3.6 0.6 pad_add_fusion.cuts
  4.2 1.3 pad_maximum_fusion.2.vec
  5.5 0.0 copy-done
  5.6 0.1 convert.17
  5.6 0.0 copy-done.1
  5.6 0.1 convert.18
  5.7 0.0 copy-done.2
  5.7 0.0 copy-start.3
  5.7 0.1 convert.19
  5.8 0.0 copy-start.5
  5.8 0.0 copy-start.6
  5.8 1.3 pad_maximum_fusion.wqkv
  7.2 0.0 copy-done.3
  7.2 0.9 convert_element_type.14.wo
  8.0 0.0 copy-done.5
  8.0 0.0 copy-done.6
  8.1 0.7 pad_maximum_fusion.1.block
  8.7 68.6 %attention_forward.1 = (bf16[2304,2048]{1,0:T(8,128)(2,1)}, bf16[2304,2048]{1,0:T(8,128)(2,1)}, bf16[2304,512]{1,0:T(8,128)(2,1)}, bf16[2304,512]{1,0:T(8,128)(2...) custom-call(s32[2,2]{1,0:T(2,128)} %pad_add_fusion.cuts, ...), custom_call_target="tpu_custom_call" | custom-call | tf_op jit(solution)/shard_map/attention_forward/pallas_call | solution.py:1208
  77.4 0.0 copy-done.10
  77.4 0.0 copy-done.11
  77.4 0.0 copy-done.12
  77.4 0.6 pad_maximum_fusion.3.vec
  78.0 50.5 %feed_forward.1 = (f32[2,1152,512]{2,1,0:T(8,128)}, f32[2304,512]{1,0:T(8,128)}, bf16[2304,1024]{1,0:T(8,128)(2,1)}, bf16[2,4,4,64,1024]{4,3,2,1,0:T(8,128)(2,1)...) custom-call(s32[2,2]{1,0:T(2,128)} %pad_add_fusion.cuts, f32[2,1152,512]{2,1,0:T(8,128)} %cot_hbm.1, ...), custom_call_target="tpu_custom_call" | custom-call | tf_op jit(solution)/shard_map/feed_forward/pallas_call | solution.py:1243
  128.5 0.0 copy-start.8
  128.5 0.0 copy-start.9
  128.6 0.3 copy.39
  129.0 1.7 maximum_maximum_fusion.back
  130.7 0.0 copy-done.8
  130.7 0.0 copy-done.9
  130.7 0.6 pad_maximum_fusion.4.vec
  131.3 133.4 %attention_backward.1 = (f32[2,1152,512]{2,1,0:T(8,128)}, f32[64,1024]{1,0:T(8,128)}, bf16[2,4,4,16,2048]{4,3,2,1,0:T(8,128)(2,1)}, f32[16,512]{1,0:T(8,128)}) custom-call(s32[2,2]{1,0:T(2,128)} %pad_add_fusion.cuts, f32[2,1152,512]{2,1,0:T(8,128)} %x_hbm.3, f32[2304,512]{1,0:T(8,128)} %get-tuple-element.43.ga_hbm, ...), custom_call_target="tpu_custom_call" | custom-call | tf_op jit(solution)/shard_map/attention_backward/pallas_call | solution.py:1285
  264.7 6.0 %reshape.40 = f32[512,4,512]{2,1,0:T(4,128)} reshape(bf16[2,4,4,16,2048]{4,3,2,1,0:T(8,128)(2,1)} %get-tuple-element.59) | data formatting | bytes 6291456 | tf_op jit(solution)/shard_map/convert_element_type | solution.py:1328
  270.7 10.2 %fusion.3 = (f32[512,1,512]{2,1,0:T(1,128)S(1)}, f32[512,1,512]{2,1,0:T(1,128)S(1)}, f32[512,1,512]{2,1,0:T(1,128)S(1)}, f32[512,1,512]{2,1,0:T(1,128)S(1)}) fusion(f32[512,4,512]{2,1,0:T(4,128)} %reshape.40), kind=kLoop, calls=%fused_computation.26 | loop fusion | bytes 8388608 | tf_op jit(solution)/shard_map/slice | solution.py:1337
  280.9 0.0 slice-start.1
  281.0 1.5 copy_bitcast_fusion
  282.4 1.5 copy_bitcast_fusion.2
  283.9 0.7 copy-done.4
  284.7 0.7 slice_bitcast_fusion.4
  285.4 0.6 copy.50
  286.0 0.6 fusion.4
  286.6 0.0 slice-done.1
  286.6 2.2 copy.56
  (16 shorter events, 0.2 us)
Async XLA Ops:
  0.6 4.9 %copy-start = (f32[512,512]{1,0:T(8,128)S(1)}, f32[512,512]{1,0:T(8,128)}, u32[]{:S(2)}) copy-start(f32[512,512]{1,0:T(8,128)} %param.21) | copy-start | bytes 3145732
  0.7 5.0 %copy-start.1 = (f32[512,512]{1,0:T(8,128)S(1)}, f32[512,512]{1,0:T(8,128)}, u32[]{:S(2)}) copy-start(f32[512,512]{1,0:T(8,128)} %param.22) | copy-start | bytes 3145732
  1.9 3.8 %copy-start.2 = (f32[512,512]{1,0:T(8,128)S(1)}, f32[512,512]{1,0:T(8,128)}, u32[]{:S(2)}) copy-start(f32[512,512]{1,0:T(8,128)} %param.23) | copy-start | bytes 3145732
  5.7 1.4 copy-start.3
  5.8 2.2 copy-start.5
  5.8 2.2 copy-start.6
  8.7 68.7 %copy-start.10 = (f32[512]{0:T(512)S(1)}, f32[512]{0:T(512)}, u32[]{:S(2)}) copy-start(f32[512]{0:T(512)} %param.32) | copy-start | bytes 6148
  8.7 68.7 %copy-start.11 = (f32[512]{0:T(512)S(1)}, f32[512]{0:T(512)}, u32[]{:S(2)}) copy-start(f32[512]{0:T(512)} %param.28) | copy-start | bytes 6148
  8.7 68.7 %copy-start.12 = (f32[512]{0:T(512)S(1)}, f32[512]{0:T(512)}, u32[]{:S(2)}) copy-start(f32[512]{0:T(512)} %param.27) | copy-start | bytes 6148
  128.5 2.1 copy-start.8
  128.5 2.1 copy-start.9
  270.7 15.9 %slice-start = ((s8[4718592]{0:T(1024)(128)(4,1)}), s8[524288]{0:T(1024)(128)(4,1)S(1)}, s32[]{:S(2)}) async-start(s8[4718592]{0:T(1024)(128)(4,1)} %bitcast.45), calls=%async_computation | async-start | bytes 1048576
  280.9 5.7 %slice-start.1 = ((s8[4718592]{0:T(1024)(128)(4,1)}), s8[4194304]{0:T(1024)(128)(4,1)S(1)}, s32[]{:S(2)}) async-start(s8[4718592]{0:T(1024)(128)(4,1)} %bitcast.45), calls=%async_computation.1 | async-start | bytes 8388608
  282.4 2.2 copy-start.4
  282.4 2.9 %copy-start.7 = (f32[16,512]{1,0:T(8,128)S(1)}, f32[16,512]{1,0:T(8,128)}, u32[]{:S(2)}) copy-start(f32[16,512]{1,0:T(8,128)} %get-tuple-element.58) | copy-start | bytes 98308

commit v2 on v1

v2 whole, which is shorter than its diff:
```python
import functools
import math

import jax
import jax.numpy as jnp
from jax import lax
from jax.experimental import pallas as pl
from jax.experimental.pallas import tpu as pltpu
from jax.sharding import PartitionSpec as P

BF, F32 = jnp.bfloat16, jnp.float32
EPS = 1e-5
LONG = 64
TILE = 256
PAIR = 128
AHEAD = 3
CHUNKS = 2
FEAT = 256
VMEM_LIMIT = 63 << 20
LOG16 = math.log(16.0)


def dot(a, b):
    return jnp.dot(a, b, preferred_element_type=F32)


def dot_nt(a, b):
    return lax.dot_general(a, b, (((1,), (1,)), ((), ())), preferred_element_type=F32)


def dot_tn(a, b):
    return lax.dot_general(a, b, (((0,), (0,)), ((), ())), preferred_element_type=F32)


def iota(shape, dim):
    return lax.broadcasted_iota(jnp.int32, shape, dim)


def normalize(rows):
    mean = jnp.mean(rows, axis=-1, keepdims=True)
    centred = rows - mean
    spread = jnp.mean(centred * centred, axis=-1, keepdims=True)
    scale = lax.rsqrt(spread + EPS)
    return centred * scale, scale


def norm_back(grad, xhat, scale):
    return scale * (
        grad
        - jnp.mean(grad, axis=-1, keepdims=True)
        - xhat * jnp.mean(grad * xhat, axis=-1, keepdims=True)
    )


def head_sums(pair):
    first = iota(pair.shape, 1) < PAIR // 2
    zero = jnp.zeros_like(pair)
    return (
        jnp.sum(jnp.where(first, pair, zero), axis=-1, keepdims=True),
        jnp.sum(jnp.where(first, zero, pair), axis=-1, keepdims=True),
    )


def features(scaled, scaled_low, proj, pair):
    cols = slice(pair * PAIR, (pair + 1) * PAIR)
    part = scaled[:, cols]
    first, second = head_sums(part * part)
    product = dot(scaled_low[:, cols], proj[pair])
    return jnp.concatenate(
        [
            jnp.exp(product[:, :FEAT] - (0.5 * first + LOG16)).astype(BF),
            jnp.exp(product[:, FEAT:] - (0.5 * second + LOG16)).astype(BF),
        ],
        axis=1,
    )


def lane_half(shape):
    return iota(shape, 1) < FEAT


def block_sums(both, norm):
    keep = (iota((PAIR, 2 * FEAT), 0) < PAIR // 2) == lane_half((PAIR, 2 * FEAT))
    zero = jnp.zeros((PAIR, 2 * FEAT), F32)
    return jnp.concatenate(
        [
            jnp.where(keep, both, zero).astype(BF),
            jnp.where(keep, jnp.broadcast_to(norm, (PAIR, 2 * FEAT)), zero).astype(BF),
        ],
        axis=0,
    )


def block_grads(both, norm):
    keep = (iota((PAIR, 2 * FEAT), 0) < PAIR // 2) == lane_half((PAIR, 2 * FEAT))
    zero = jnp.zeros((PAIR, 2 * FEAT), F32)
    row = iota((PAIR, 2 * FEAT), 0)
    high = norm.astype(BF).astype(F32)
    wide = jnp.broadcast_to(high, (PAIR, 2 * FEAT))
    rest = jnp.broadcast_to(norm - high, (PAIR, 2 * FEAT))
    return jnp.concatenate(
        [
            jnp.where(keep, both, zero).astype(BF),
            jnp.where(row == 0, wide, jnp.where(row == 1, rest, zero)).astype(BF),
        ],
        axis=0,
    )


def pack_pair(both):
    return jnp.where(lane_half((PAIR // 2, 2 * FEAT)), both[: PAIR // 2], both[PAIR // 2 :])


def norm_rows(both):
    return jnp.where(
        lane_half((1, 2 * FEAT)),
        jnp.sum(both[PAIR : PAIR + PAIR // 2], axis=0, keepdims=True),
        jnp.sum(both[PAIR + PAIR // 2 :], axis=0, keepdims=True),
    )


def unpack_pair(packed):
    return jnp.concatenate([packed, packed], axis=0)


def value_block(values, cols):
    part = values[:, cols]
    first = iota(part.shape, 1) < PAIR // 2
    zero = jnp.zeros_like(part)
    one = jnp.ones_like(part)
    top = jnp.concatenate([jnp.where(first, part, zero), jnp.where(first, one, zero)], axis=1)
    low = jnp.concatenate([jnp.where(first, zero, part), jnp.where(first, zero, one)], axis=1)
    return jnp.concatenate([top, low], axis=0)


def same_small(bounds):
    shape = (2 * LONG, 2 * LONG)

    def label(dim):
        at = iota(shape, dim)
        cut = jnp.where(at < LONG, bounds[0], LONG + bounds[1])
        return jnp.where(at < cut, 1, 0) + jnp.where(at < LONG, 0, 2)

    return label(0) == label(1)


def cuts_of(lens, big):
    cuts, bounds = [], []
    for batch in range(2):
        first, second = lens[batch, 0], lens[batch, 1]
        behind = jnp.where(second == big, first, first + second)
        cuts.append(jnp.where(first == big, 0, behind))
        bounds.append(jnp.where(first == big, second, first))
    return cuts, bounds


def swap_rows(buffer, cuts):
    most = buffer.shape[1]
    width = buffer.shape[2]
    for batch in range(2):
        head = buffer[batch, LONG : 2 * LONG]
        tail = buffer[batch, most - LONG :]
        small_first = iota((LONG, width), 0) < cuts[batch]
        buffer[batch, LONG : 2 * LONG] = jnp.where(small_first, tail, head)
        buffer[batch, most - LONG :] = jnp.where(small_first, head, tail)


def edge_rows(buffer):
    most = buffer.shape[1]
    return jnp.concatenate(
        [
            buffer[0, :LONG],
            buffer[1, :LONG],
            buffer[0, most - LONG :],
            buffer[1, most - LONG :],
        ],
        axis=0,
    )


def store_edge(buffer, value):
    most = buffer.shape[1]
    buffer[0, :LONG] = value[:LONG]
    buffer[1, :LONG] = value[LONG : 2 * LONG]
    buffer[0, most - LONG :] = value[2 * LONG : 3 * LONG]
    buffer[1, most - LONG :] = value[3 * LONG :]


def digits_of(size):
    out = []
    while size > 1:
        step = 4 if size % 4 == 0 else size
        out.append(step)
        size //= step
    return tuple(out)


class Net:
    def __init__(self, digits, send, recv):
        self.digits = digits
        self.send, self.recv = send, recv
        self.me = lax.axis_index("seq")
        self.core = lax.axis_index("ffn")
        self.slots = {}
        strides = [math.prod(digits[k + 1 :]) for k in range(len(digits))]
        self.own = [lax.rem(lax.div(self.me, s), n) for s, n in zip(strides, digits)]
        self.strides = strides

    def partner(self):
        return (self.me, 1 - self.core)

    def other(self, k, step):
        return lax.rem(self.own[k] + step, self.digits[k])

    def peer(self, k, step):
        return (self.me + (self.other(k, step) - self.own[k]) * self.strides[k], self.core)

    def greet(self):
        semaphore = pltpu.get_barrier_semaphore()
        peers = [self.partner()] + [
            self.peer(k, step) for k, n in enumerate(self.digits) for step in range(1, n)
        ]
        for peer in peers:
            pl.semaphore_signal(
                semaphore, inc=1, device_id=peer, device_id_type=pl.DeviceIdType.MESH
            )

    def meet(self):
        pl.semaphore_wait(
            pltpu.get_barrier_semaphore(), 1 + sum(n - 1 for n in self.digits)
        )

    def copy(self, key, source, target, device):
        slot = self.slots.setdefault(key, len(self.slots))
        return pltpu.make_async_remote_copy(
            src_ref=source,
            dst_ref=target,
            send_sem=self.send.at[slot],
            recv_sem=self.recv.at[slot],
            device_id=device,
            device_id_type=pl.DeviceIdType.MESH,
        )

    def group(self, key, size):
        return self.copy(key, size, size, self.partner())


def groups(depth, gathers, others):
    return gathers * (depth + 1) * (depth + 2) // 2 + others * (depth + 1)


class Gather:
    def __init__(self, net, name, out):
        self.net, self.name, self.out = net, name, out

    def fresh(self, j):
        net = self.net
        if j == 0:
            return [(net.core,) + tuple(net.own)]
        lead = (net.core,) + (slice(None),) * (j - 1)
        return [
            lead + (net.other(j - 1, step),) + tuple(net.own[j:])
            for step in range(1, net.digits[j - 1])
        ]

    def copies(self, j, k):
        net = self.net
        depth = len(net.digits)
        copies = []
        for at in self.fresh(j):
            block = self.out.at[at]
            if k == depth:
                copies.append(net.copy((self.name, j, k), block, block, net.partner()))
                continue
            for step in range(1, net.digits[k]):
                copies.append(net.copy((self.name, j, k), block, block, net.peer(k, step)))
        return copies

    def group(self, j, k):
        digits = self.net.digits
        at = [0] * (1 + len(digits))
        if j:
            at[1:j] = [slice(None)] * (j - 1)
            at[j] = pl.ds(0, digits[j - 1] - 1)
        if k < len(digits):
            at[1 + k] = pl.ds(0, digits[k] - 1)
        return self.net.group((self.name, j, k), self.out.at[tuple(at)])

    def steps(self):
        depth = len(self.net.digits)

        def run(j):
            for i in range(j):
                self.group(i, j - 1).wait_recv()
            for k in range(j, depth + 1):
                for copy in self.copies(j, k):
                    copy.start()

        def last():
            for j in range(depth + 1):
                self.group(j, depth).wait_recv()

        return [functools.partial(run, j) for j in range(depth + 1)] + [last]

    def drain(self):
        depth = len(self.net.digits)
        for j in range(depth + 1):
            for k in range(j, depth + 1):
                self.group(j, k).wait_send()


class Scatter:
    def __init__(self, net, name, blocks, first, slots, parts, finish, apart=None):
        self.net, self.name = net, name
        self.away = (blocks if apart is None else apart).at[1 - net.core]
        self.held = blocks.at[net.core] if apart is None else blocks
        self.first, self.slots, self.parts, self.finish = first, slots, parts, finish

    @staticmethod
    def scratch(digits, rows, cols):
        shapes = [pltpu.VMEM(digits + (rows, cols), BF)]
        for k in reversed(range(len(digits))):
            shapes.append(pltpu.VMEM((digits[k] - 1,) + digits[:k] + (rows, cols), BF))
        for k in reversed(range(1, len(digits))):
            shapes.append(pltpu.VMEM(digits[:k] + (rows, cols), BF))
        return shapes

    @classmethod
    def of(cls, net, name, blocks, refs, finish, apart=None):
        depth = len(net.digits)
        slots, parts = refs[1 : 1 + depth], refs[1 + depth :]
        return cls(net, name, blocks, refs[0], slots, parts, finish, apart)

    def copies(self, k):
        net = self.net
        depth = len(net.digits)
        if k == 0:
            return [net.copy((self.name, 0), self.away, self.first, net.partner())]
        digit = depth - k
        held = self.held if k == 1 else self.parts[k - 2]
        copies = []
        for step in range(1, net.digits[digit]):
            at = (slice(None),) * digit + (net.other(digit, step),)
            copies.append(
                net.copy(
                    (self.name, k),
                    held.at[at],
                    self.slots[k - 1].at[step - 1],
                    net.peer(digit, step),
                )
            )
        return copies

    def group(self, k):
        return self.net.group((self.name, k), self.slots[k - 1] if k else self.first)

    def add(self, k):
        net = self.net
        depth = len(net.digits)
        if k == 0:
            lead = net.digits
            for at in _indices(lead):
                mine = self.held[at].astype(F32)
                self.held[at] = (mine + self.first[at].astype(F32)).astype(BF)
            return
        digit = depth - k
        held = self.held if k == 1 else self.parts[k - 2]
        for at in _indices(net.digits[:digit]):
            total = held[at + (net.own[digit],)].astype(F32)
            for step in range(net.digits[digit] - 1):
                total = total + self.slots[k - 1][(step,) + at].astype(F32)
            if digit:
                self.parts[k - 1][at] = total.astype(BF)
            else:
                self.finish(total)

    def steps(self):
        depth = len(self.net.digits)

        def start(k):
            for copy in self.copies(k):
                copy.start()

        def follow(k):
            self.group(k - 1).wait_recv()
            self.add(k - 1)
            if k <= depth:
                start(k)

        return [functools.partial(start, 0)] + [
            functools.partial(follow, k) for k in range(1, depth + 2)
        ]

    def drain(self):
        for k in range(len(self.net.digits) + 1):
            self.group(k).wait_send()


def _indices(lead):
    if not lead:
        return [()]
    return [(i,) + rest for i in range(lead[0]) for rest in _indices(lead[1:])]


class Whole:
    def __init__(self, net, name, held, slots):
        self.net, self.name, self.held, self.slots = net, name, held, slots

    @staticmethod
    def scratch(digits, rows, cols):
        return [
            pltpu.VMEM((len(digits) + 2, rows, cols), F32),
            pltpu.VMEM((1 + sum(n - 1 for n in digits), rows, cols), F32),
        ]

    def span(self, k):
        digits = self.net.digits
        return (0, 1) if k == 0 else (1 + sum(n - 1 for n in digits[: k - 1]), digits[k - 1] - 1)

    def copies(self, k):
        net = self.net
        source = self.held.at[k]
        first, number = self.span(k)
        peers = [net.partner()] if k == 0 else [net.peer(k - 1, 1 + i) for i in range(number)]
        return [
            net.copy((self.name, k), source, self.slots.at[first + i], peer)
            for i, peer in enumerate(peers)
        ]

    def group(self, k):
        return self.net.group((self.name, k), self.slots.at[pl.ds(*self.span(k))])

    def steps(self):
        depth = len(self.net.digits)

        def start(k):
            for copy in self.copies(k):
                copy.start()

        def follow(k):
            self.group(k - 1).wait_recv()
            total = self.held[k - 1]
            first, number = self.span(k - 1)
            for i in range(number):
                total = total + self.slots[first + i]
            self.held[k] = total
            if k <= depth:
                start(k)

        return [functools.partial(start, 0)] + [
            functools.partial(follow, k) for k in range(1, depth + 2)
        ]

    def drain(self):
        for k in range(len(self.net.digits) + 1):
            self.group(k).wait_send()


def together(*parts):
    most = max(len(part) for part in parts)

    def run(i):
        for part in parts:
            if i < len(part):
                part[i]()

    return [functools.partial(run, i) for i in range(most)]


def block_shape(ways, rows, cols):
    lanes = cols * (rows // 16) // ways
    return 16, lanes


def block_at(digits, index):
    at = []
    for n in reversed(digits):
        at.append(index % n)
        index //= n
    return tuple(reversed(at))


def store_blocks(blocks, row, value):
    lanes = blocks.shape[-1]
    per_row = value.shape[1] // lanes
    ways = (2,) + blocks.shape[1:-2]
    for i in range(value.shape[0] // 16):
        for j in range(per_row):
            at = block_at(ways, (row // 16 + i) * per_row + j)
            blocks[at] = value[16 * i : 16 * i + 16, j * lanes : (j + 1) * lanes]


def load_blocks(blocks, row, rows, cols):
    lanes = blocks.shape[-1]
    per_row = cols // lanes
    ways = (2,) + blocks.shape[1:-2]
    out = []
    for i in range(rows // 16):
        line = [
            blocks[block_at(ways, (row // 16 + i) * per_row + j)] for j in range(per_row)
        ]
        out.append(line[0] if per_row == 1 else jnp.concatenate(line, axis=1))
    return jnp.concatenate(out, axis=0)


class Loads:
    def __init__(self, semaphores):
        self.semaphores = semaphores
        self.count = 0

    def start(self, source, target):
        copy = pltpu.make_async_copy(source, target, self.semaphores.at[self.count])
        self.count += 1
        copy.start()
        return copy


PIECES = ((0, 128), (1088, 64), (128, 192), (320, 256), (576, 256), (832, 256))


def raw_pieces(rows):
    quarter = (rows - 2 * LONG) // 4
    pieces = [(0, 2 * LONG), (rows - LONG, LONG), (2 * LONG, quarter - LONG)]
    return pieces + [(LONG + quarter * i, quarter) for i in range(1, 4)]


def big_start(batch, rows_big, step, tile):
    return TILE + batch * rows_big + step * tile


def pair_projection(projection, pair):
    first, second = projection[2 * pair], projection[2 * pair + 1]
    gap = jnp.zeros_like(first)
    return jnp.concatenate(
        [jnp.concatenate([first, gap], axis=1), jnp.concatenate([gap, second], axis=1)], axis=0
    )


def place(steps, spots, count):
    lists = [[] for _ in range(count)]
    for step, spot in zip(steps, spots, strict=True):
        lists[spot].append(step)
    return lists


def spots(known, number):
    if number == len(known):
        return list(known)
    last = len(known) - 1
    return [known[min(last, -(-i * last // max(1, number - 1)))] for i in range(number)]


def side_by_side(chains):
    most = max(len(chain) for chain in chains)
    return [
        chain[i - most] for i in range(most) for chain in chains if i >= most - len(chain)
    ]


def talk(lists, t):
    for i, steps in enumerate(lists):
        if steps:
            pl.when(t == i)(functools.partial(_all, steps))


def _all(steps):
    for step in steps:
        step()


def all_reduce(scatter, spread):
    first, second = scatter.steps(), spread.steps()
    return first[:-1] + [functools.partial(_both, first[-1], second[0])] + second[1:]


def weight_block(up, down, chunk):
    half = up.shape[1] // CHUNKS
    at = slice(chunk * half, (chunk + 1) * half)
    return jnp.concatenate([up[:, at], down[:, at]], axis=0).astype(BF)


def attention_forward(
    digits, lens, x_hbm, gain, shift, bias, wq_hbm, wk_hbm, wv_hbm, wo_hbm, projection, up, down,
    k_out, q_out, v_out, ks_out, qs_out, n_out, mix_out, inv_out, att_out, sd_out, small_out,
    wqkv_out, wo_out, w_out,
    x, kf, qf, v, ks, qs, n, mix, inv, att, sd, small, wqkv, wo, proj, block, acc, nacc, parts,
    total, load_sem, store_sem, own_sem, send, recv, whole_held, whole_slots, *slots,
):
    rows = x.shape[1]
    big = rows - 2 * LONG
    pairs = proj.shape[0]
    width = wo.shape[0]
    scale = (PAIR // 2) ** -0.25
    depth = len(digits)
    net = Net(digits, send, recv)
    loads = Loads(load_sem)
    pieces = raw_pieces(rows)
    pending = {}

    def load_rows(some):
        for piece in some:
            for batch in range(2):
                span = pl.ds(*piece)
                pending[batch, piece] = loads.start(x_hbm.at[batch, span], x.at[batch, span])

    load_rows(pieces[:2])
    weights = [
        loads.start(source, att.at[pl.ds(i * width, width)])
        for i, source in enumerate((wq_hbm, wk_hbm, wv_hbm, wo_hbm))
    ]
    net.greet()
    block[...] = weight_block(up, down, 0)
    own_block = pltpu.make_async_copy(block, w_out.at[(net.core,) + tuple(net.own)], own_sem)
    own_block.start()
    for pair in range(pairs):
        proj[pair] = pair_projection(projection, pair).astype(BF)
    own_block.wait()
    net.meet()
    gather = Gather(net, "w", w_out)
    gather_steps = gather.steps()
    gather_steps[0]()

    def finish(value):
        total[(net.core,) + tuple(net.own)] = value.astype(BF)

    scatter = Scatter.of(net, "s", parts, slots, finish)
    spread = Gather(net, "t", total)
    whole = Whole(net, "n", whole_held, whole_slots)
    sum_steps = together(all_reduce(scatter, spread), whole.steps())
    cuts, bounds = cuts_of(lens, big)
    for i, copy in enumerate(weights):
        copy.wait()
        rounded = att[i * width : (i + 1) * width].astype(BF)
        if i < 3:
            wqkv[:, i * width : (i + 1) * width] = rounded
        else:
            wo[...] = rounded

    def front(rows_x, tile):
        xhat, _ = normalize(rows_x)
        low = (xhat * gain[...] + shift[...]).astype(BF)
        n[tile] = low.T
        raw = dot(low, wqkv[...])
        q = raw[:, :width] * scale
        k = raw[:, width : 2 * width] * scale
        return q, k, raw[:, 2 * width :].astype(BF)

    def attend(numer_denom, at, pair):
        cols = slice(pair * PAIR, (pair + 1) * PAIR)
        inverse = 1.0 / numer_denom[:, PAIR:]
        inv[at, cols] = inverse
        mix[at, cols] = (numer_denom[:, :PAIR] * inverse).astype(BF)

    load_rows(pieces[2:])
    for piece in pieces[:2]:
        for batch in range(2):
            pending[batch, piece].wait()
    swap_rows(x, cuts)
    edge = slice(0, TILE)
    q, k, values = front(edge_rows(x), 0)
    v[edge] = values
    k_low = k.astype(BF)
    ks[edge] = k_low
    for pair in range(pairs):
        cols = slice(pair * PAIR, (pair + 1) * PAIR)
        feats = slice(pair * 2 * FEAT, (pair + 1) * 2 * FEAT)
        mapped = features(k, k_low, proj, pair)
        kf[edge, feats] = mapped
        for batch in range(2):
            own = slice(batch * LONG, (batch + 1) * LONG)
            both = dot_tn(values[own, cols], mapped[own])
            row = batch * pairs + pair
            store_blocks(parts, row * LONG, pack_pair(both).astype(BF))
            whole_held[0, row : row + 1] = jnp.sum(mapped[own].astype(F32), axis=0, keepdims=True)
    sum_steps[0]()
    q_low = q.astype(BF)
    qs[edge] = q_low
    same = same_small(bounds)
    shorts = slice(2 * LONG, TILE)
    for pair in range(pairs):
        cols = slice(pair * PAIR, (pair + 1) * PAIR)
        feats = slice(pair * 2 * FEAT, (pair + 1) * 2 * FEAT)
        mapped = features(q, q_low, proj, pair)
        qf[edge, feats] = mapped
        scores = []
        for head in range(2):
            lanes = slice((2 * pair + head) * FEAT, (2 * pair + head + 1) * FEAT)
            score = dot_nt(
                mapped[shorts, head * FEAT : (head + 1) * FEAT], kf[shorts, lanes]
            )
            score = jnp.where(same, score, 0.0).astype(BF)
            small[2 * pair + head] = score
            scores.append(score)
        attend(
            dot(jnp.concatenate(scores, axis=1), value_block(values[shorts], cols)), shorts, pair
        )

    def store(source, target, at, slot):
        pltpu.make_async_copy(source.at[at], target.at[at], store_sem.at[slot]).start()

    first_pass = ((kf, k_out), (qf, q_out), (v, v_out), (ks, ks_out), (qs, qs_out), (n, n_out))
    second_pass = ((mix, mix_out), (inv, inv_out), (att, att_out))
    once = ((small, small_out), (wqkv, wqkv_out), (wo, wo_out), (sd, sd_out))

    def store_first(at, tile):
        for slot, (source, target) in enumerate(first_pass):
            store(source, target, tile if source is n else at, slot)

    def store_second(at):
        for slot, (source, target) in enumerate(second_pass):
            store(source, target, at, len(first_pass) + slot)

    def whole_copy(i):
        slot = len(first_pass) + len(second_pass) + i
        return pltpu.make_async_copy(*once[i], store_sem.at[slot])

    store_first(pl.ds(0, TILE), 0)
    for i in range(3):
        whole_copy(i).start()
    for piece in pieces[2:]:
        for batch in range(2):
            pending[batch, piece].wait()
    acc[...] = jnp.zeros_like(acc)
    nacc[...] = jnp.zeros_like(nacc)
    per = big // TILE
    count = 2 * per
    comm = place(
        sum_steps[1:] + gather_steps[1:],
        spots((1, 3, 5, 7, count + 2, count + 6), len(sum_steps) - 1)
        + spots((3, count, count + 4), len(gather_steps) - 1),
        2 * count,
    )

    def pass_one(t, _):
        batch, step = lax.div(t, per), lax.rem(t, per)
        talk(comm[:count], t)
        raw_at = pl.ds(pl.multiple_of(LONG + step * TILE, LONG), TILE)
        at = pl.ds(pl.multiple_of(TILE + t * TILE, TILE), TILE)
        q, k, values = front(x[batch, raw_at], 1 + t)
        v[at] = values
        k_low = k.astype(BF)
        q_low = q.astype(BF)
        ks[at] = k_low
        qs[at] = q_low
        for pair in range(pairs):
            cols = slice(pair * PAIR, (pair + 1) * PAIR)
            feats = slice(pair * 2 * FEAT, (pair + 1) * 2 * FEAT)
            mapped = features(k, k_low, proj, pair)
            kf[at, feats] = mapped
            acc[batch, pair] += dot_tn(values[:, cols], mapped)
            nacc[batch, pair] += jnp.sum(mapped.astype(F32), axis=0, keepdims=True)
            qf[at, feats] = features(q, q_low, proj, pair)
        store_first(at, 1 + t)
        return 0

    lax.fori_loop(0, count, pass_one, 0)
    for batch in range(2):
        for pair in range(pairs):
            sd[batch, pair] = block_sums(acc[batch, pair], nacc[batch, pair])

    def pass_two(t, _):
        batch, step = lax.div(t, per), lax.rem(t, per)
        talk(comm[count:], t)
        raw_at = pl.ds(pl.multiple_of(LONG + step * TILE, LONG), TILE)
        at = pl.ds(pl.multiple_of(TILE + t * TILE, TILE), TILE)
        for pair in range(pairs):
            feats = slice(pair * 2 * FEAT, (pair + 1) * 2 * FEAT)
            attend(dot_nt(qf[at, feats], sd[batch, pair]), at, pair)
        att[at] = x[batch, raw_at] + dot(mix[at], wo[...]) + bias[...]
        store_second(at)
        return 0

    lax.fori_loop(0, count, pass_two, 0)
    for batch in range(2):
        own = slice(batch * LONG, (batch + 1) * LONG)
        for pair in range(pairs):
            feats = slice(pair * 2 * FEAT, (pair + 1) * 2 * FEAT)
            row = batch * pairs + pair
            packed = load_blocks(total, row * LONG, LONG, 2 * FEAT).astype(F32)
            sd[2 + batch, pair] = block_sums(
                unpack_pair(packed), whole_held[depth + 1, row : row + 1]
            )
            attend(dot_nt(qf[own, feats], sd[2 + batch, pair]), own, pair)
    att[edge] = edge_rows(x) + dot(mix[edge], wo[...]) + bias[...]
    store_second(pl.ds(0, TILE))
    whole_copy(3).start()
    for slot, (source, target) in enumerate(first_pass + second_pass):
        pltpu.make_async_copy(source, target, store_sem.at[slot]).wait()
    for i in range(len(once)):
        whole_copy(i).wait()
    gather.drain()
    scatter.drain()
    spread.drain()
    whole.drain()


def _both(first, second):
    first()
    second()


def feed_forward(
    digits, lens, cot_hbm, att_hbm, mix_hbm, inv_hbm, w_hbm, wo, gain, shift, up_bias,
    up_own, down_own, q_hbm,
    out_hbm, ga_out, g_out, x_out, ffn_out, wo_grad, vec_grad, bias_grad, long_out, norm_out,
    cot, att, mix, inv, second, branch, grad_second, w_first, w_second, up, down, dup, ddown,
    gr_edge, gr, qf, parts, long_total, load_sem, store_sem, send, recv, *refs,
):
    rows = cot.shape[1]
    big = rows - 2 * LONG
    width = wo.shape[0]
    pairs = width // PAIR
    tile = big // 2
    per = big // tile
    count = 2 * per
    depth = len(digits)
    cuts, _ = cuts_of(lens, big)
    net = Net(digits, send, recv)
    net.greet()
    loads = Loads(load_sem)
    deep = w_first.shape[-2] // 2
    half = w_first.shape[-1]
    wait_w = loads.start(w_hbm, w_first)
    pieces = raw_pieces(rows)
    inner = [(0, TILE)] + [(TILE + tile * i, tile) for i in range(count)]

    def load_cot(some):
        return [
            loads.start(cot_hbm.at[batch, pl.ds(*piece)], cot.at[batch, pl.ds(*piece)])
            for piece in some
            for batch in range(2)
        ]

    def load_inner(source, target, some):
        return [loads.start(source.at[pl.ds(*p)], target.at[pl.ds(*p)]) for p in some]

    first_waits = load_inner(att_hbm, att, inner[:1]) + load_cot(pieces[:2])
    w_second[(net.core,) + tuple(net.own)] = weight_block(up_own, down_own, 1)
    net.meet()
    gather = Gather(net, "w", w_second)
    gather_steps = gather.steps()
    gather_steps[0]()

    def finish(value):
        ffn_out[...] = value

    scatter = Scatter.of(net, "f", w_first, refs[: 2 * depth], finish)
    scatter_steps = scatter.steps()

    def finish_long(value):
        long_total[(net.core,) + tuple(net.own)] = value.astype(BF)

    long_scatter = Scatter.of(net, "s", parts, refs[2 * depth : 4 * depth], finish_long)
    long_spread = Gather(net, "t", long_total)
    norm_held, norm_slots = refs[4 * depth :]
    norm_sum = Whole(net, "n", norm_held, norm_slots)
    long_steps = together(all_reduce(long_scatter, long_spread), norm_sum.steps())
    members = _indices(digits)
    group = max(1, 16 // deep)

    def unpack(w):
        for core in range(2):
            cols = slice(core * half, (core + 1) * half)
            for first in range(0, len(members), group):
                parts = [w[(core,) + members[first + i]] for i in range(group)]
                at = slice(first * deep, (first + group) * deep)
                if group == 1:
                    up[at, cols] = parts[0][:deep]
                    down[at, cols] = parts[0][deep:]
                else:
                    up[at, cols] = jnp.concatenate([part[:deep] for part in parts], axis=0)
                    down[at, cols] = jnp.concatenate([part[deep:] for part in parts], axis=0)

    def pack(w):
        for core in range(2):
            cols = slice(core * half, (core + 1) * half)
            for i, member in enumerate(members):
                at = slice(i * deep, (i + 1) * deep)
                w[(core,) + member] = jnp.concatenate(
                    [dup[at, cols], ddown[at, cols]], axis=0
                ).astype(BF)

    def bias_lanes(chunk):
        return [
            slice((CHUNKS * core + chunk) * half, (CHUNKS * core + chunk + 1) * half)
            for core in range(2)
        ]

    def add_row(at, value):
        vec_grad[at : at + 1] += jnp.sum(value, axis=0, keepdims=True)

    def hidden_part(chunk, second_low, grad_low):
        bias = jnp.concatenate([up_bias[:, lanes] for lanes in bias_lanes(chunk)], axis=1)
        hidden = dot(second_low, up[...]) + bias
        gauss = jnp.exp(-0.5 * hidden * hidden) * (1.0 / math.sqrt(2.0 * math.pi))
        cdf = 0.5 + 0.5 * lax.erf(hidden * math.sqrt(0.5))
        active = (hidden * cdf).astype(BF)
        slope = cdf + hidden * gauss
        grad_hidden = (dot(grad_low, down[...]) * slope).astype(BF)
        dup[...] += dot(second_low.T, grad_hidden)
        ddown[...] += dot(grad_low.T, active)
        bias_sum = jnp.sum(grad_hidden.astype(F32), axis=0, keepdims=True)
        for core, lanes in enumerate(bias_lanes(chunk)):
            bias_grad[:, lanes] += bias_sum[:, core * half : (core + 1) * half]
        return dot_nt(active, down[...]), dot_nt(grad_hidden, up[...])

    def first_block(at, grad_out):
        xhat, _ = normalize(att[at])
        low = (xhat * gain[...] + shift[...]).astype(BF)
        second[at] = low
        branch[at], grad_second[at] = hidden_part(0, low, grad_out.astype(BF))

    def second_block(at, grad_out, put, between=lambda: None):
        more, grad_more = hidden_part(1, second[at], grad_out.astype(BF))
        between()
        att_rows = att[at]
        xhat, scale = normalize(att_rows)
        output = att_rows + (branch[at] + more)
        grad = grad_second[at] + grad_more
        grad_att = grad_out + norm_back(grad * gain[...], xhat, scale)
        add_row(2, grad_att)
        add_row(3, grad * xhat)
        add_row(4, grad)
        add_row(5, grad_out)
        grad_att_low = grad_att.astype(BF)
        mixed = mix[at]
        wo_grad[...] += dot_tn(mixed, grad_att_low)
        grad_mixed = dot_nt(grad_att_low, wo[...]).astype(BF).astype(F32)
        for pair in range(pairs):
            cols = slice(pair * PAIR, (pair + 1) * PAIR)
            part = grad_mixed[:, cols]
            inverse = inv[at, cols]
            first, last = head_sums(part * mixed[:, cols].astype(F32))
            lane = iota(part.shape, 1)
            grad_denom = -jnp.where(lane < PAIR // 2, first, last) * inverse
            high = grad_denom.astype(BF).astype(F32)
            both = jnp.where(lane % (PAIR // 2) < PAIR // 4, high, grad_denom - high)
            put(2 * pair, (part * inverse).astype(BF))
            put(2 * pair + 1, (both * (4.0 / PAIR)).astype(BF))
        att[at] = grad_att
        return output

    def lanes_of(i):
        return slice(i * PAIR, (i + 1) * PAIR)

    def store_g(t):
        slot = lax.rem(t, 2)
        at = pl.ds(pl.multiple_of(TILE + t * tile, TILE), tile)
        return pltpu.make_async_copy(gr.at[slot], g_out.at[at], store_sem.at[slot])

    def store_att(at):
        pltpu.make_async_copy(att.at[at], ga_out.at[at], store_sem.at[2]).start()

    def rows_at(t):
        batch, step = lax.div(t, per), lax.rem(t, per)
        raw_at = pl.ds(pl.multiple_of(LONG + step * tile, LONG), tile)
        return batch, raw_at, pl.ds(pl.multiple_of(TILE + t * tile, TILE), tile)

    for ref in (dup, ddown, wo_grad, vec_grad, bias_grad):
        ref[...] = jnp.zeros_like(ref)
    wait_w.wait()
    for copy in first_waits:
        copy.wait()
    next_waits = load_inner(att_hbm, att, inner[1:]) + load_cot(pieces[2:])
    unpack(w_first)
    edge = pl.ds(0, TILE)
    swap_rows(cot, cuts)
    first_block(edge, edge_rows(cot))
    for copy in next_waits:
        copy.wait()
    last_waits = [loads.start(q_hbm.at[pl.ds(0, 2 * LONG)], qf)]
    for some in (inner[:1], inner[1:]):
        last_waits += load_inner(mix_hbm, mix, some) + load_inner(inv_hbm, inv, some)
    gather_at = place(gather_steps[1:], spots((1, 3, count), len(gather_steps) - 1), count + 1)

    def first_pass(t, _):
        talk(gather_at[:count], t)
        batch, raw_at, at = rows_at(t)
        first_block(at, cot[batch, raw_at])
        return 0

    lax.fori_loop(0, count, first_pass, 0)
    _all(gather_at[count])
    pack(w_first)
    scatter_steps[0]()
    unpack(w_second)
    dup[...] = jnp.zeros_like(dup)
    ddown[...] = jnp.zeros_like(ddown)
    for copy in last_waits:
        copy.wait()

    def put_edge(i, value):
        gr_edge[:, lanes_of(i)] = value

    store_edge(cot, second_block(edge, edge_rows(cot), put_edge))
    store_att(edge)
    edge_copy = pltpu.make_async_copy(gr_edge, g_out.at[edge], store_sem.at[3])
    edge_copy.start()
    for batch in range(2):
        own = slice(batch * LONG, (batch + 1) * LONG)
        for pair in range(pairs):
            grads = gr_edge[own, 2 * pair * PAIR : (2 * pair + 2) * PAIR]
            both = dot_tn(grads, qf[own, 2 * pair * FEAT : (2 * pair + 2) * FEAT])
            row = batch * pairs + pair
            store_blocks(parts, row * LONG, pack_pair(both[:PAIR]).astype(BF))
            norm_held[0, row : row + 1] = norm_rows(both)
    long_steps[0]()
    scatter_at = place(
        scatter_steps[1:] + long_steps[1:],
        spots((0, 5, 2 * count), len(scatter_steps) - 1)
        + spots((0, 2, 3, 5, 6, 2 * count), len(long_steps) - 1),
        2 * count + 1,
    )

    def second_pass(t, _):
        talk(scatter_at[: 2 * count : 2], t)
        batch, raw_at, at = rows_at(t)

        @pl.when(t >= 2)
        def _():
            store_g(t - 2).wait()

        def put(i, value):
            gr[lax.rem(t, 2), :, lanes_of(i)] = value

        cot[batch, raw_at] = second_block(
            at, cot[batch, raw_at], put, functools.partial(talk, scatter_at[1 : 2 * count : 2], t)
        )
        store_att(at)
        store_g(t).start()
        return 0

    lax.fori_loop(0, count, second_pass, 0)
    swap_rows(cot, cuts)
    out_copy = pltpu.make_async_copy(cot, out_hbm, store_sem.at[4])
    out_copy.start()
    gather.drain()
    pack(w_second)
    x_copy = pltpu.make_async_copy(w_second, x_out, store_sem.at[5])
    x_copy.start()
    _all(scatter_at[2 * count])
    long_out[...] = long_total[...]
    norm_out[...] = norm_held[depth + 1]
    store_g(count - 2).wait()
    store_g(count - 1).wait()
    pltpu.make_async_copy(att, ga_out, store_sem.at[2]).wait()
    edge_copy.wait()
    out_copy.wait()
    x_copy.wait()
    for item in (scatter, long_scatter, long_spread, norm_sum):
        item.drain()


def attention_backward(
    digits, lens, x_hbm, ga_hbm, g_hbm, k_hbm, q_hbm, v_hbm, ks_hbm, qs_hbm, n_hbm,
    sd_hbm, small, ffn_hbm, wo_grad, vec_in, bias_in, long_total, long_norm, gain, wqkv,
    projection,
    in_grad, ffn_out, out_out, query_out, key_out, value_out, vec_out,
    kf, v, ks, qs, n, sd, sg, back, ffn, out_x, out_total, query_x, query_total, key_x, key_total,
    value_x, value_total, load_sem, tile_sem, key_sem, store_sem, send, recv, *refs,
):
    rows = x_hbm.shape[1]
    big = rows - 2 * LONG
    pairs = back.shape[0]
    width = wqkv.shape[0]
    inner_rows = kf.shape[0]
    scale = (PAIR // 2) ** -0.25
    depth = len(digits)
    net = Net(digits, send, recv)
    each = 2 * depth
    refs = list(refs)

    def take(number):
        taken, refs[:] = refs[:number], refs[number:]
        return taken

    loads = Loads(load_sem)
    per = big // TILE
    count = 2 * per
    shorts = slice(2 * LONG, TILE)
    edge = slice(0, TILE)
    cuts, bounds = cuts_of(lens, big)
    same = same_small(bounds)

    def finish_ffn(value):
        ffn_out[...] = value

    ffn_sum = Scatter.of(net, "f", ffn, take(each), finish_ffn, apart=ffn_hbm)

    def reduction(name, blocks, total):
        def finish(value):
            total[(net.core,) + tuple(net.own)] = value.astype(BF)

        return Scatter.of(net, name, blocks, take(each), finish), Gather(net, name + "t", total)

    out_sum = reduction("o", out_x, out_total)
    query_sum = reduction("q", query_x, query_total)
    key_sum = reduction("k", key_x, key_total)
    value_sum = reduction("l", value_x, value_total)
    vec_held, vec_slots = take(2)
    vec_sum = Whole(net, "v", vec_held, vec_slots)
    ffn_steps = ffn_sum.steps()
    out_steps = all_reduce(*out_sum)
    query_steps = all_reduce(*query_sum)
    key_steps = all_reduce(*key_sum)
    value_steps = all_reduce(*value_sum)
    vec_steps = vec_sum.steps()
    last_spot = 4 * count
    number = len(out_steps)
    chains = (
        (ffn_steps[1:], spots((0, 9, 18), len(ffn_steps) - 1)),
        (out_steps[1:], spots((0, 6, 9, 13, 18, 24), number - 1)),
        (query_steps, spots((8, 11, 16, 22, 28, 32, 32), number)),
        (key_steps, spots((16, 21, 28, 32, 32, 32, 32), number)),
        (value_steps, spots((24, 27, 32, 32, 32, 32, 32), number)),
    )
    comm = [[] for _ in range(last_spot)]
    ends = []
    for steps, at in chains:
        ends.append([step for step, spot in zip(steps, at, strict=True) if spot == last_spot])
        for step, spot in zip(steps, at, strict=True):
            if spot < last_spot:
                comm[spot].append(step)
    last_steps = side_by_side([end for end in ends if end] + [vec_steps[1:]])

    def feat_lanes(pair):
        return slice(pair * 2 * FEAT, (pair + 1) * 2 * FEAT)

    def pair_cols(pair):
        return slice(pair * PAIR, (pair + 1) * PAIR)

    def grad_lanes(pair):
        return slice(2 * pair * PAIR, (2 * pair + 2) * PAIR)

    def feature_back(grad, mapped, scaled, pair):
        term = (grad * mapped.astype(F32)).astype(BF)
        both = dot(term, back[pair])
        return (
            (both[:, :PAIR] - scaled[:, pair_cols(pair)].astype(F32) * both[:, PAIR:]) * scale
        ).astype(BF)

    def ones_beside(values):
        return jnp.concatenate([values, jnp.ones_like(values)], axis=1)

    def first_tile(tiled):
        waits = []
        for source, target, by_rows in tiled:
            at = pl.ds(0, TILE) if by_rows else pl.ds(0, 1)
            waits.append(loads.start(source.at[at], target.at[at]))
        return waits

    def tile_load(i, source, target, by_rows, t):
        if by_rows:
            at = pl.ds(pl.multiple_of(TILE + t * TILE, TILE), TILE)
        else:
            at = pl.ds(1 + t, 1)
        return pltpu.make_async_copy(source.at[at], target.at[at], tile_sem.at[i, t])

    def query_phase(qf, gr, acc, wgrad):
        query_side = [(g_hbm, gr, True), (q_hbm, qf, True), (qs_hbm, qs, True), (n_hbm, n, False)]
        key_side = [(k_hbm, kf, True), (v_hbm, v, True), (ks_hbm, ks, True)]
        net.greet()
        wait_edge = first_tile(query_side + key_side)
        wait_edge.append(loads.start(sd_hbm.at[pl.ds(2, 2)], sd.at[pl.ds(2, 2)]))
        wait_ffn = loads.start(ffn_hbm.at[net.core], ffn)
        wait_sd = loads.start(sd_hbm.at[pl.ds(0, 2)], sd.at[pl.ds(0, 2)])

        def start_tile(t):
            for i, item in enumerate(query_side):
                tile_load(i, *item, t).start()

        for i in range(width // 16):
            at = slice(16 * i, 16 * i + 16)
            store_blocks(out_x, 16 * i, wo_grad[at].astype(BF))
        net.meet()
        out_steps[0]()
        ffn_steps[0]()
        for pair in range(pairs):
            turned = pair_projection(projection, pair).T
            own = (iota(turned.shape, 0) < FEAT) == (iota(turned.shape, 1) < PAIR // 2)
            back[pair] = jnp.concatenate([turned, jnp.where(own, 1.0, 0.0)], axis=1).astype(BF)
        for copy in wait_edge:
            copy.wait()
        for t in range(AHEAD):
            start_tile(t)
        for pair in range(pairs):
            lanes, cols = feat_lanes(pair), pair_cols(pair)
            mapped_q, mapped_k = qf[edge, lanes], kf[shorts, lanes]
            grads, values = gr[edge, grad_lanes(pair)], v[shorts, cols]
            grad_q = [
                dot(grads[batch * LONG : (batch + 1) * LONG], sd[2 + batch, pair])
                for batch in range(2)
            ]
            weight = dot_nt(grads[shorts], value_block(values, slice(0, PAIR)))
            more_q, more_k, more_v = [], [], []
            for head in range(2):
                own = slice(head * FEAT, (head + 1) * FEAT)
                part = jnp.where(same, weight[:, head * PAIR : (head + 1) * PAIR], 0.0).astype(BF)
                more_q.append(dot(part, mapped_k[:, own]))
                more_k.append(dot_tn(part, mapped_q[shorts, own]))
                more_v.append(dot_tn(small[2 * pair + head], grads[shorts, :PAIR]))
            grad_q.append(jnp.concatenate(more_q, axis=1))
            grad_k = jnp.concatenate(more_k, axis=1)
            grad_v = jnp.where(iota((2 * LONG, PAIR), 1) < PAIR // 2, more_v[0], more_v[1])
            qs[edge, cols] = feature_back(
                jnp.concatenate(grad_q, axis=0), mapped_q, qs[edge], pair
            )
            ks[shorts, cols] = feature_back(grad_k, mapped_k, ks[shorts], pair)
            v[shorts, cols] = grad_v.astype(BF)
        wgrad[...] = dot(n[0], qs[edge])
        wait_ffn.wait()
        wait_sd.wait()

        def key_load(i):
            source, target, _ = key_side[i]
            at = pl.ds(TILE, 2 * big)
            return pltpu.make_async_copy(source.at[at], target.at[at], key_sem.at[i])

        def queries(t, _):
            batch, step = lax.div(t, per), lax.rem(t, per)
            talk(comm[:count], t)
            at = pl.ds(pl.multiple_of(TILE + t * TILE, TILE), TILE)
            for i, item in enumerate(query_side):
                tile_load(i, *item, t).wait()

            @pl.when(t + AHEAD < count)
            def _():
                start_tile(t + AHEAD)

            @pl.when(t + AHEAD == count)
            def _():
                for i in range(len(key_side)):
                    key_load(i).start()

            @pl.when(step == 0)
            def _():
                acc[...] = jnp.zeros_like(acc)

            for pair in range(pairs):
                mapped = qf[at, feat_lanes(pair)]
                grads = gr[at, grad_lanes(pair)]
                acc[pair] += dot_tn(grads, mapped)
                grad = dot(grads, sd[batch, pair])
                qs[at, pair_cols(pair)] = feature_back(grad, mapped, qs[at], pair)
            wgrad[...] += dot(n[1 + t], qs[at])

            @pl.when(step == per - 1)
            def _():
                for pair in range(pairs):
                    both = acc[pair]
                    sg[batch, pair] = block_grads(both[:PAIR], norm_rows(both))

            return 0

        lax.fori_loop(0, count, queries, 0)
        for i in range(width // 16):
            at = slice(16 * i, 16 * i + 16)
            store_blocks(query_x, 16 * i, wgrad[at].astype(BF))
        for i in range(len(key_side)):
            key_load(i).wait()

    def key_phase(x, ga, wgrad):
        wait_x = [loads.start(x_hbm, x), loads.start(ga_hbm, ga)]

        def tile_at(t):
            return pl.ds(pl.multiple_of(TILE + t * TILE, TILE), TILE)

        def pack(blocks):
            for i in range(width // 16):
                at = slice(16 * i, 16 * i + 16)
                store_blocks(blocks, 16 * i, wgrad[at].astype(BF))

        def keys(t, _):
            batch = lax.div(t, per)
            talk(comm[count : 2 * count], t)
            at = tile_at(t)
            for pair in range(pairs):
                grad = dot(ones_beside(v[at, pair_cols(pair)]), sg[batch, pair])
                ks[at, pair_cols(pair)] = feature_back(grad, kf[at, feat_lanes(pair)], ks[at], pair)
            wgrad[...] += dot(n[1 + t], ks[at])
            return 0

        def values(t, _):
            batch = lax.div(t, per)
            talk(comm[2 * count : 3 * count], t)
            at = tile_at(t)
            for pair in range(pairs):
                grad = dot_nt(kf[at, feat_lanes(pair)], sg[batch, pair, :PAIR])
                v[at, pair_cols(pair)] = grad.astype(BF)
            wgrad[...] += dot(n[1 + t], v[at])
            return 0

        wgrad[...] = jnp.zeros_like(wgrad)
        lax.fori_loop(0, count, keys, 0)
        for batch in range(2):
            own = slice(batch * LONG, (batch + 1) * LONG)
            for pair in range(pairs):
                lanes, cols = feat_lanes(pair), pair_cols(pair)
                row = batch * pairs + pair
                packed = load_blocks(long_total, row * LONG, LONG, 2 * FEAT).astype(F32)
                grads = block_grads(unpack_pair(packed), long_norm[row : row + 1])
                mapped = kf[own, lanes]
                grad = dot(ones_beside(v[own, cols]), grads)
                v[own, cols] = dot_nt(mapped, grads[:PAIR]).astype(BF)
                ks[own, cols] = feature_back(grad, mapped, ks[own], pair)
        wgrad[...] += dot(n[0], ks[edge])
        pack(key_x)
        wgrad[...] = dot(n[0], v[edge])
        lax.fori_loop(0, count, values, 0)
        pack(value_x)
        for copy in wait_x:
            copy.wait()
        swap_rows(x, cuts)
        vec_held[0] = jnp.zeros(vec_held.shape[1:], F32)
        vec_held[0, 2:6] = vec_in[2:6]
        for i in range(bias_in.shape[1] // width):
            vec_held[0, 6 + i : 7 + i] = bias_in[:, i * width : (i + 1) * width]

        def last(rows_x, rows_ga, at):
            xhat, spread = normalize(rows_x)
            grad = (
                dot_nt(qs[at], wqkv[:, :width])
                + dot_nt(ks[at], wqkv[:, width : 2 * width])
                + dot_nt(v[at], wqkv[:, 2 * width :])
            )
            vec_held[0, 0:1] += jnp.sum(grad * xhat, axis=0, keepdims=True)
            vec_held[0, 1:2] += jnp.sum(grad, axis=0, keepdims=True)
            return rows_ga + norm_back(grad * gain[...], xhat, spread)

        def inputs(t, _):
            batch, step = lax.div(t, per), lax.rem(t, per)
            talk(comm[3 * count : 4 * count], t)
            raw_at = pl.ds(pl.multiple_of(LONG + step * TILE, LONG), TILE)
            at = tile_at(t)
            x[batch, raw_at] = last(x[batch, raw_at], ga[at], at)
            return 0

        lax.fori_loop(0, count, inputs, 0)
        store_edge(x, last(edge_rows(x), ga[edge], edge))
        vec_steps[0]()
        swap_rows(x, cuts)
        copy = pltpu.make_async_copy(x, in_grad, store_sem.at[0])
        copy.start()
        _all(last_steps)
        totals = [
            pltpu.make_async_copy(source, target, store_sem.at[1 + i])
            for i, (source, target) in enumerate(
                (
                    (out_total, out_out), (query_total, query_out),
                    (key_total, key_out), (value_total, value_out),
                )
            )
        ]
        for total in totals:
            total.start()
        vec_out[...] = vec_held[depth + 1]
        copy.wait()
        for total in totals:
            total.wait()

    wide = kf.shape[1]
    pl.run_scoped(
        query_phase,
        pltpu.VMEM((inner_rows, wide), BF),
        pltpu.VMEM((inner_rows, 2 * width), BF),
        pltpu.VMEM((pairs, 2 * PAIR, 2 * FEAT), F32),
        pltpu.VMEM((width, width), F32),
    )
    pl.run_scoped(
        key_phase,
        pltpu.VMEM(x_hbm.shape, F32),
        pltpu.VMEM((inner_rows, width), F32),
        pltpu.VMEM((width, width), F32),
    )
    for item in (ffn_sum, *out_sum, *query_sum, *key_sum, *value_sum, vec_sum):
        item.drain()


def body(
    inputs,
    lengths,
    first_gain,
    first_shift,
    query_weight,
    key_weight,
    value_weight,
    output_weight,
    output_bias,
    projection,
    second_gain,
    second_shift,
    up_weight,
    up_bias,
    down_weight,
    down_bias,
    cotangent,
):
    heads, head_size, feats = projection.shape
    batches, rows, width = inputs.shape
    digits = digits_of(lax.axis_size("seq"))
    ways = 2 * math.prod(digits)
    depth = len(digits)
    pairs = heads // 2
    big = rows - 2 * LONG
    inner = TILE + batches * big
    deep, half = up_weight.shape
    hidden = up_bias.shape[0]
    part = half // CHUNKS
    down_turned = down_weight.T

    lens = lengths.reshape(batches, lengths.shape[2])
    tiles = inner // TILE
    hbm = pl.BlockSpec(memory_space=pl.ANY)
    vmem = pl.BlockSpec(memory_space=pltpu.VMEM)
    smem = pl.BlockSpec(memory_space=pltpu.SMEM)

    def shape(*dims, dtype=BF):
        return jax.ShapeDtypeStruct(dims, dtype)

    def line(vector):
        return vector.reshape(1, -1)

    wide = 2 * FEAT * pairs
    long_block = block_shape(ways, batches * pairs * LONG, 2 * FEAT)
    inner_shapes = [
        ((inner, wide), BF), ((inner, wide), BF), ((inner, width), BF), ((inner, width), BF),
        ((inner, width), BF), ((tiles, width, TILE), BF), ((inner, width), BF),
        ((inner, width), F32), ((inner, width), F32), ((4, pairs, 2 * PAIR, 2 * FEAT), BF),
        ((heads, 2 * LONG, 2 * LONG), BF), ((width, 3 * width), BF), ((width, width), BF),
    ]
    kf, qf, v, ks, qs, n, mix, inv, att, sd, small, wqkv, wo, w = pl.pallas_call(
        functools.partial(attention_forward, digits),
        out_shape=[shape(*dims, dtype=kind) for dims, kind in inner_shapes]
        + [shape(2, *digits, 2 * deep, part)],
        in_specs=[smem, hbm] + [vmem] * 3 + [hbm] * 4 + [vmem] * 3,
        out_specs=[hbm] * 14,
        scratch_shapes=[pltpu.VMEM(inputs.shape, F32)]
        + [pltpu.VMEM(dims, kind) for dims, kind in inner_shapes]
        + [
            pltpu.VMEM((pairs, PAIR, 2 * FEAT), BF),
            pltpu.VMEM((2 * deep, part), BF),
            pltpu.VMEM((batches, pairs, PAIR, 2 * FEAT), F32),
            pltpu.VMEM((batches, pairs, 1, 2 * FEAT), F32),
            pltpu.VMEM((2,) + digits + long_block, BF),
            pltpu.VMEM((2,) + digits + long_block, BF),
            pltpu.SemaphoreType.DMA((16,)),
            pltpu.SemaphoreType.DMA((13,)),
            pltpu.SemaphoreType.DMA,
            pltpu.SemaphoreType.DMA((groups(depth, 2, 2),)),
            pltpu.SemaphoreType.DMA((groups(depth, 2, 2),)),
        ]
        + Whole.scratch(digits, batches * pairs, 2 * FEAT)
        + Scatter.scratch(digits, *long_block),
        compiler_params=pltpu.CompilerParams(
            collective_id=0, has_side_effects=True, vmem_limit_bytes=VMEM_LIMIT
        ),
        name="attention_forward",
    )(
        lens, inputs, line(first_gain), line(first_shift), line(output_bias),
        query_weight, key_weight, value_weight, output_weight, projection, up_weight, down_turned,
    )

    blocks = (2,) + digits + (2 * deep, part)
    output, ga, gr, ffn, ffn_grad, wo_grad, vec_in, bias_in, long_grad, long_norm = pl.pallas_call(
        functools.partial(feed_forward, digits),
        out_shape=[
            shape(*inputs.shape, dtype=F32),
            shape(inner, width, dtype=F32),
            shape(inner, 2 * width),
            shape(*blocks),
            shape(2 * deep, part, dtype=F32),
            shape(width, width, dtype=F32),
            shape(8, width, dtype=F32),
            shape(1, hidden, dtype=F32),
            shape(2, *digits, *long_block),
            shape(batches * pairs, 2 * FEAT, dtype=F32),
        ],
        in_specs=[smem] + [hbm] * 5 + [vmem] * 6 + [hbm],
        out_specs=[hbm] * 4 + [vmem] * 6,
        scratch_shapes=[
            pltpu.VMEM(inputs.shape, F32),
            pltpu.VMEM((inner, width), F32),
            pltpu.VMEM((inner, width), BF),
            pltpu.VMEM((inner, width), F32),
            pltpu.VMEM((inner, width), BF),
            pltpu.VMEM((inner, width), F32),
            pltpu.VMEM((inner, width), F32),
            pltpu.VMEM(blocks, BF),
            pltpu.VMEM(blocks, BF),
            pltpu.VMEM((width, hidden // CHUNKS), BF),
            pltpu.VMEM((width, hidden // CHUNKS), BF),
            pltpu.VMEM((width, hidden // CHUNKS), F32),
            pltpu.VMEM((width, hidden // CHUNKS), F32),
            pltpu.VMEM((TILE, 2 * width), BF),
            pltpu.VMEM((2, big // 2, 2 * width), BF),
            pltpu.VMEM((2 * LONG, wide), BF),
            pltpu.VMEM((2,) + digits + long_block, BF),
            pltpu.VMEM((2,) + digits + long_block, BF),
            pltpu.SemaphoreType.DMA((30,)),
            pltpu.SemaphoreType.DMA((6,)),
            pltpu.SemaphoreType.DMA((groups(depth, 2, 3),)),
            pltpu.SemaphoreType.DMA((groups(depth, 2, 3),)),
        ]
        + Scatter.scratch(digits, 2 * deep, part)
        + Scatter.scratch(digits, *long_block)
        + Whole.scratch(digits, batches * pairs, 2 * FEAT),
        compiler_params=pltpu.CompilerParams(
            collective_id=1, has_side_effects=True, vmem_limit_bytes=VMEM_LIMIT
        ),
        name="feed_forward",
    )(
        lens, cotangent, att, mix, inv, w, wo, line(second_gain), line(second_shift),
        line(up_bias), up_weight, down_turned, qf,
    )

    late_block = block_shape(ways, width, width)
    late_shape = (2,) + digits + late_block
    in_grad, ffn_more, out_w, query, key, value, vectors = pl.pallas_call(
        functools.partial(attention_backward, digits),
        out_shape=[
            shape(*inputs.shape, dtype=F32),
            shape(2 * deep, part, dtype=F32),
            shape(*late_shape),
            shape(*late_shape),
            shape(*late_shape),
            shape(*late_shape),
            shape(16, width, dtype=F32),
        ],
        in_specs=[smem] + [hbm] * 10 + [vmem, hbm] + [vmem] * 8,
        out_specs=[hbm, vmem, hbm, hbm, hbm, hbm, vmem],
        scratch_shapes=[
            pltpu.VMEM((inner, wide), BF),
            pltpu.VMEM((inner, width), BF),
            pltpu.VMEM((inner, width), BF),
            pltpu.VMEM((inner, width), BF),
            pltpu.VMEM((tiles, width, TILE), BF),
            pltpu.VMEM((4, pairs, 2 * PAIR, 2 * FEAT), BF),
            pltpu.VMEM((batches, pairs, 2 * PAIR, 2 * FEAT), BF),
            pltpu.VMEM((pairs, 2 * FEAT, 2 * PAIR), BF),
            pltpu.VMEM(blocks[1:], BF),
        ]
        + [pltpu.VMEM(late_shape, BF)] * 8
        + [
            pltpu.SemaphoreType.DMA((12,)),
            pltpu.SemaphoreType.DMA((4, tiles - 1)),
            pltpu.SemaphoreType.DMA((3,)),
            pltpu.SemaphoreType.DMA((5,)),
            pltpu.SemaphoreType.DMA((groups(depth, 4, 6),)),
            pltpu.SemaphoreType.DMA((groups(depth, 4, 6),)),
        ]
        + Scatter.scratch(digits, 2 * deep, part)
        + Scatter.scratch(digits, *late_block) * 4
        + Whole.scratch(digits, 16, width),
        compiler_params=pltpu.CompilerParams(
            collective_id=2, has_side_effects=True, vmem_limit_bytes=VMEM_LIMIT
        ),
        name="attention_backward",
    )(
        lens, inputs, ga, gr, kf, qf, v, ks, qs, n, sd, small, ffn,
        wo_grad, vec_in, bias_in, long_grad, long_norm, line(first_gain), wqkv, projection,
    )

    def whole(blocks):
        lanes = blocks.shape[-1]
        if lanes != width:
            blocks = blocks.reshape(width // 16, width // lanes, 16, lanes)
            blocks = jnp.swapaxes(blocks, 1, 2)
        return blocks.reshape(width, width).astype(F32)

    ffn_all = jnp.concatenate([ffn_grad, ffn_more], axis=1)
    return (
        output + down_bias,
        in_grad,
        vectors[0],
        vectors[1],
        whole(query),
        whole(key),
        whole(value),
        whole(out_w),
        vectors[2],
        vectors[3],
        vectors[4],
        ffn_all[:deep],
        vectors[6 : 6 + hidden // width].reshape(hidden),
        ffn_all[deep:].T,
        vectors[5],
    )


def solution(mesh):
    rows = P(None, ("seq", "ffn"), None)
    up, down = P("seq", "ffn"), P("ffn", "seq")
    in_specs = (rows, rows) + (P(),) * 10 + (up, P(), down, P(), rows)
    out_specs = (rows, rows) + (P(),) * 9 + (up, P(), down, P())
    return jax.shard_map(body, mesh=mesh, in_specs=in_specs, out_specs=out_specs, check_vma=False)
```

time: 293 us -> 200 us (0.68); the launches traced: 289 us -> 200 us
  Pallas kernels: 253 us -> 186 us
  local copies, waits for them, and re-layouts: 24.5 us -> 4.18 us
    pallas_call x1, Pallas kernels: 133 us -> 75.9 us  [body(): pl.pallas_call(functools.partial(attention_backward, digits), out_shape=[...]
    pallas_call x1, Pallas kernels: 68.6 us -> 39.8 us  [body(): pl.pallas_call(functools.partial(attention_forward, digits), out_shape=[s...]
    pallas_call x1, Pallas kernels: 50.5 us -> 70.7 us  [body(): pl.pallas_call(functools.partial(feed_forward, digits), out_shape=[shape(...]
    slice x1 -> x0, local copies, waits for them, and re-layouts: 10.2 us -> none  [body(): shared[:, 3]]
    convert_element_type x1 -> x0, local copies, waits for them, and re-layouts: 6 us -> none  [body(): shared = jnp.swapaxes(shared, 1, 2).reshape(width, 4, width).astype(F32)]
    add x0 -> x1, other arithmetic: none -> 5.29 us  [body(): output + down_bias]
    concatenate x4 -> x0, other arithmetic: 4.53 us -> none  [the longest x1 1.7 us: body(): jnp.concatenate([jnp.concatenate([turned[:, 0], gap, one, gap], axis=2),...]
    another operation x8 -> x0, other arithmetic: 3.38 us -> none  [the longest x1 1.32 us: body(): jnp.stack([first_gain, first_shift, output_bias])]
where the time goes in v2:
time: 200 us
  Pallas kernels  186 us (93%)
  other arithmetic  8.65 us (4%)
  local copies, waits for them, and re-layouts  4.18 us (2%)
    pallas_call x1, Pallas kernels, body(): pl.pallas_call(functools.partial(attention_backward, digits), out_shape=[...  75.9 us
    pallas_call x1, Pallas kernels, body(): pl.pallas_call(functools.partial(feed_forward, digits), out_shape=[shape(...  70.7 us
    pallas_call x1, Pallas kernels, body(): pl.pallas_call(functools.partial(attention_forward, digits), out_shape=[s...  39.8 us
    add x1, other arithmetic, body(): output + down_bias  5.29 us

profile of v2, /device:TPU:0, one launch (start us, length us, event | category | flops | bytes accessed | tf_op | source)
XLA Modules:
  0.0 200.0 jit_solution(17079233178302306632)
XLA Ops:
  0.6 39.8 %attention_forward.1 = (bf16[2304,2048]{1,0:T(8,128)(2,1)}, bf16[2304,2048]{1,0:T(8,128)(2,1)}, bf16[2304,512]{1,0:T(8,128)(2,1)}, bf16[2304,512]{1,0:T(8,128)(2...) custom-call(s32[2,3]{1,0:T(2,128)} %bitcast.35, ...), custom_call_target="tpu_custom_call" | custom-call | tf_op jit(solution)/shard_map/attention_forward/pallas_call | solution.py:1431
  40.5 70.7 %feed_forward.1 = (f32[2,1152,512]{2,1,0:T(8,128)}, f32[2304,512]{1,0:T(8,128)}, bf16[2304,1024]{1,0:T(8,128)(2,1)}, bf16[2,4,4,64,512]{4,3,2,1,0:T(8,128)(2,1)}...) custom-call(s32[2,3]{1,0:T(2,128)} %bitcast.36, ...), custom_call_target="tpu_custom_call" | custom-call | tf_op jit(solution)/shard_map/feed_forward/pallas_call | solution.py:1464
  111.1 0.0 copy-start.7
  111.1 75.9 %attention_backward.1 = (f32[2,1152,512]{2,1,0:T(8,128)}, f32[64,512]{1,0:T(8,128)}, bf16[2,4,4,16,512]{4,3,2,1,0:T(8,128)(2,1)}, bf16[2,4,4,16,512]{4,3,2,1,0:T...) custom-call(s32[2,3]{1,0:T(2,128)} %bitcast.37, ...), custom_call_target="tpu_custom_call" | custom-call | tf_op jit(solution)/shard_map/attention_backward/pallas_call | solution.py:1518
  187.0 0.0 slice-start
  187.0 0.0 copy-done.7
  187.1 0.0 copy-start.6
  187.1 0.0 copy-start.4
  187.1 0.0 copy-start.5
  187.1 0.0 copy-start.2
  187.1 0.0 copy-start.3
  187.1 0.0 copy-start
  187.1 0.0 copy-start.1
  187.1 0.0 slice-start.1
  187.1 5.3 %broadcast_add_fusion = f32[2,1152,512]{2,1,0:T(8,128)} fusion(f32[2,1152,512]{2,1,0:T(8,128)} %get-tuple-element.52, f32[512]{0:T(512)S(1)} %copy-done.7), kind=kLoop, calls=%fused_computation | loop fusion | flops 1179648 | bytes 9439232 | tf_op jit(solution)/shard_map/add | solution.py:1572
  192.4 0.0 copy-done.6
  192.4 0.6 fusion
  193.0 0.6 copy.32
  193.6 0.0 copy-done.4
  193.7 0.0 copy-done.5
  193.7 0.7 slice_bitcast_fusion
  194.4 0.0 copy-done.2
  194.4 0.0 copy-done.3
  194.4 1.7 bitcast_convert_fusion.2
  196.1 0.0 copy-done
  196.1 0.0 copy-done.1
  196.1 1.7 bitcast_convert_fusion
  197.8 0.0 slice-done
  197.8 0.0 slice-done.1
  197.8 2.2 %copy.35 = f32[2,1152,512]{2,1,0:T(8,128)} copy(f32[2,1152,512]{2,1,0:T(8,128)S(1)} %bitcast.32) | data formatting | bytes 9437184
  (4 shorter events, 0.0 us)
Async XLA Ops:
  111.1 75.9 %copy-start.7 = (f32[512]{0:T(512)S(1)}, f32[512]{0:T(512)}, u32[]{:S(2)}) copy-start(f32[512]{0:T(512)} %param.32) | copy-start | bytes 6148
  187.0 10.7 %slice-start = ((s8[4718592]{0:T(1024)(128)(4,1)}), s8[4194304]{0:T(1024)(128)(4,1)S(1)}, s32[]{:S(2)}) async-start(s8[4718592]{0:T(1024)(128)(4,1)} %bitcast.31), calls=%async_computation | async-start | bytes 8388608
  187.1 5.4 %copy-start.6 = (f32[16,512]{1,0:T(8,128)S(1)}, f32[16,512]{1,0:T(8,128)}, u32[]{:S(2)}) copy-start(f32[16,512]{1,0:T(8,128)} %get-tuple-element.70) | copy-start | bytes 98308
  187.1 6.6 %copy-start.4 = (f32[64,512]{1,0:T(8,128)S(1)}, f32[64,512]{1,0:T(8,128)}, u32[]{:S(2)}) copy-start(f32[64,512]{1,0:T(8,128)} %get-tuple-element.75) | copy-start | bytes 393220
  187.1 6.6 %copy-start.5 = (f32[64,512]{1,0:T(8,128)S(1)}, f32[64,512]{1,0:T(8,128)}, u32[]{:S(2)}) copy-start(f32[64,512]{1,0:T(8,128)} %get-tuple-element.76) | copy-start | bytes 393220
  187.1 7.3 %copy-start.2 = (bf16[2,4,4,16,512]{4,3,2,1,0:T(8,128)(2,1)S(1)}, bf16[2,4,4,16,512]{4,3,2,1,0:T(8,128)(2,1)}, u32[]{:S(2)}) copy-start(bf16[2,4,4,16,512]{4,3,2,1,0:T(8,128)(2,1)} %get-tuple-element.71) | copy-start | bytes 1572868
  187.1 7.3 %copy-start.3 = (bf16[2,4,4,16,512]{4,3,2,1,0:T(8,128)(2,1)S(1)}, bf16[2,4,4,16,512]{4,3,2,1,0:T(8,128)(2,1)}, u32[]{:S(2)}) copy-start(bf16[2,4,4,16,512]{4,3,2,1,0:T(8,128)(2,1)} %get-tuple-element.72) | copy-start | bytes 1572868
  187.1 9.0 %copy-start = (bf16[2,4,4,16,512]{4,3,2,1,0:T(8,128)(2,1)S(1)}, bf16[2,4,4,16,512]{4,3,2,1,0:T(8,128)(2,1)}, u32[]{:S(2)}) copy-start(bf16[2,4,4,16,512]{4,3,2,1,0:T(8,128)(2,1)} %get-tuple-element.74) | copy-start | bytes 1572868
  187.1 9.0 %copy-start.1 = (bf16[2,4,4,16,512]{4,3,2,1,0:T(8,128)(2,1)S(1)}, bf16[2,4,4,16,512]{4,3,2,1,0:T(8,128)(2,1)}, u32[]{:S(2)}) copy-start(bf16[2,4,4,16,512]{4,3,2,1,0:T(8,128)(2,1)} %get-tuple-element.73) | copy-start | bytes 1572868
  187.1 10.7 %slice-start.1 = ((s8[4718592]{0:T(1024)(128)(4,1)}), s8[524288]{0:T(1024)(128)(4,1)S(1)}, s32[]{:S(2)}) async-start(s8[4718592]{0:T(1024)(128)(4,1)} %bitcast.31), calls=%async_computation.1 | async-start | bytes 1048576

commit v3 on v2

--- a/solution.py
+++ b/solution.py
@@ -163,6 +163,33 @@
         small_first = iota((LONG, width), 0) < cuts[batch]
         buffer[batch, LONG : 2 * LONG] = jnp.where(small_first, tail, head)
         buffer[batch, most - LONG :] = jnp.where(small_first, head, tail)
+
+
+class RowStore:
+    def __init__(self, buffer, out, semaphore, tile):
+        self.buffer, self.out, self.semaphore, self.tile = buffer, out, semaphore, tile
+
+    def start(self, batch, at):
+        pltpu.make_async_copy(
+            self.buffer.at[batch, at], self.out.at[batch, at], self.semaphore
+        ).start()
+
+    def tile_done(self, batch, step):
+        first = LONG + step * self.tile
+        self.start(batch, pl.ds(pl.multiple_of(first + LONG, LONG), self.tile - LONG))
+
+        @pl.when(step > 0)
+        def _():
+            self.start(batch, pl.ds(pl.multiple_of(first, LONG), LONG))
+
+    def finish(self):
+        rows = self.buffer.shape[1]
+        for batch in range(2):
+            self.start(batch, pl.ds(0, 2 * LONG))
+            self.start(batch, pl.ds(rows - LONG, LONG))
+
+    def wait(self):
+        pltpu.make_async_copy(self.buffer, self.out, self.semaphore).wait()
 
 
 def edge_rows(buffer):
@@ -700,7 +727,7 @@
 
     first_pass = ((kf, k_out), (qf, q_out), (v, v_out), (ks, ks_out), (qs, qs_out), (n, n_out))
     second_pass = ((mix, mix_out), (inv, inv_out), (att, att_out))
-    once = ((small, small_out), (wqkv, wqkv_out), (wo, wo_out), (sd, sd_out))
+    once = ((small, small_out), (wqkv, wqkv_out), (wo, wo_out))
 
     def store_first(at, tile):
         for slot, (source, target) in enumerate(first_pass):
@@ -758,6 +785,12 @@
         for pair in range(pairs):
             sd[batch, pair] = block_sums(acc[batch, pair], nacc[batch, pair])
 
+    sd_copies = [
+        pltpu.make_async_copy(sd.at[pl.ds(i, 2)], sd_out.at[pl.ds(i, 2)], store_sem.at[12 + i // 2])
+        for i in (0, 2)
+    ]
+    sd_copies[0].start()
+
     def pass_two(t, _):
         batch, step = lax.div(t, per), lax.rem(t, per)
         talk(comm[count:], t)
@@ -783,11 +816,13 @@
             attend(dot_nt(qf[own, feats], sd[2 + batch, pair]), own, pair)
     att[edge] = edge_rows(x) + dot(mix[edge], wo[...]) + bias[...]
     store_second(pl.ds(0, TILE))
-    whole_copy(3).start()
+    sd_copies[1].start()
     for slot, (source, target) in enumerate(first_pass + second_pass):
         pltpu.make_async_copy(source, target, store_sem.at[slot]).wait()
     for i in range(len(once)):
         whole_copy(i).wait()
+    for copy in sd_copies:
+        copy.wait()
     gather.drain()
     scatter.drain()
     spread.drain()
@@ -1006,11 +1041,16 @@
             norm_held[0, row : row + 1] = norm_rows(both)
     long_steps[0]()
     scatter_at = place(
-        scatter_steps[1:] + long_steps[1:],
-        spots((0, 5, 2 * count), len(scatter_steps) - 1)
-        + spots((0, 2, 3, 5, 6, 2 * count), len(long_steps) - 1),
+        long_steps[1:] + scatter_steps[1:],
+        spots((0, 2, 4, 6, 2 * count, 2 * count), len(long_steps) - 1)
+        + spots((0, 6, 2 * count), len(scatter_steps) - 1),
         2 * count + 1,
     )
+
+    out_store = RowStore(cot, out_hbm, store_sem.at[4], tile)
+    finals = scatter_at[2 * count]
+    split = sum(step in long_steps for step in finals)
+    last_steps = side_by_side([finals[:split], finals[split:]])
 
     def second_pass(t, _):
         talk(scatter_at[: 2 * count : 2], t)
@@ -1026,26 +1066,26 @@
         cot[batch, raw_at] = second_block(
             at, cot[batch, raw_at], put, functools.partial(talk, scatter_at[1 : 2 * count : 2], t)
         )
+        out_store.tile_done(batch, lax.rem(t, per))
         store_att(at)
         store_g(t).start()
         return 0
 
     lax.fori_loop(0, count, second_pass, 0)
     swap_rows(cot, cuts)
-    out_copy = pltpu.make_async_copy(cot, out_hbm, store_sem.at[4])
-    out_copy.start()
+    out_store.finish()
     gather.drain()
     pack(w_second)
     x_copy = pltpu.make_async_copy(w_second, x_out, store_sem.at[5])
     x_copy.start()
-    _all(scatter_at[2 * count])
+    _all(last_steps)
     long_out[...] = long_total[...]
     norm_out[...] = norm_held[depth + 1]
     store_g(count - 2).wait()
     store_g(count - 1).wait()
     pltpu.make_async_copy(att, ga_out, store_sem.at[2]).wait()
     edge_copy.wait()
-    out_copy.wait()
+    out_store.wait()
     x_copy.wait()
     for item in (scatter, long_scatter, long_spread, norm_sum):
         item.drain()
@@ -1108,11 +1148,11 @@
     last_spot = 4 * count
     number = len(out_steps)
     chains = (
-        (ffn_steps[1:], spots((0, 9, 18), len(ffn_steps) - 1)),
-        (out_steps[1:], spots((0, 6, 9, 13, 18, 24), number - 1)),
-        (query_steps, spots((8, 11, 16, 22, 28, 32, 32), number)),
-        (key_steps, spots((16, 21, 28, 32, 32, 32, 32), number)),
-        (value_steps, spots((24, 27, 32, 32, 32, 32, 32), number)),
+        (out_steps[1:], spots((0, 4, 7, 11, 16, 22), number - 1)),
+        (ffn_steps[1:], spots((0, 12, 24), len(ffn_steps) - 1)),
+        (query_steps, spots((8, 10, 16, 25, 31, 32, 32), number)),
+        (key_steps, spots((16, 20, 29, 32, 32, 32, 32), number)),
+        (value_steps, spots((24, 26, 32, 32, 32, 32, 32), number)),
     )
     comm = [[] for _ in range(last_spot)]
     ends = []
@@ -1327,20 +1367,22 @@
             vec_held[0, 1:2] += jnp.sum(grad, axis=0, keepdims=True)
             return rows_ga + norm_back(grad * gain[...], xhat, spread)
 
+        rows_out = RowStore(x, in_grad, store_sem.at[0], TILE)
+
         def inputs(t, _):
             batch, step = lax.div(t, per), lax.rem(t, per)
             talk(comm[3 * count : 4 * count], t)
             raw_at = pl.ds(pl.multiple_of(LONG + step * TILE, LONG), TILE)
             at = tile_at(t)
             x[batch, raw_at] = last(x[batch, raw_at], ga[at], at)
+            rows_out.tile_done(batch, step)
             return 0
 
         lax.fori_loop(0, count, inputs, 0)
         store_edge(x, last(edge_rows(x), ga[edge], edge))
         vec_steps[0]()
         swap_rows(x, cuts)
-        copy = pltpu.make_async_copy(x, in_grad, store_sem.at[0])
-        copy.start()
+        rows_out.finish()
         _all(last_steps)
         totals = [
             pltpu.make_async_copy(source, target, store_sem.at[1 + i])
@@ -1354,7 +1396,7 @@
         for total in totals:
             total.start()
         vec_out[...] = vec_held[depth + 1]
-        copy.wait()
+        rows_out.wait()
         for total in totals:
             total.wait()
 
@@ -1444,7 +1486,7 @@
             pltpu.VMEM((2,) + digits + long_block, BF),
             pltpu.VMEM((2,) + digits + long_block, BF),
             pltpu.SemaphoreType.DMA((16,)),
-            pltpu.SemaphoreType.DMA((13,)),
+            pltpu.SemaphoreType.DMA((14,)),
             pltpu.SemaphoreType.DMA,
             pltpu.SemaphoreType.DMA((groups(depth, 2, 2),)),
             pltpu.SemaphoreType.DMA((groups(depth, 2, 2),)),

time: 200 us -> 181 us (0.905)
  Pallas kernels: 186 us -> 167 us
    pallas_call x1, Pallas kernels: 75.9 us -> 65.9 us  [body(): pl.pallas_call(functools.partial(attention_backward, digits), out_shape=[...]
    pallas_call x1, Pallas kernels: 70.7 us -> 62.1 us  [body(): pl.pallas_call(functools.partial(feed_forward, digits), out_shape=[shape(...]
where the time goes in v3:
time: 181 us
  Pallas kernels  167 us (92%)
  other arithmetic  8.65 us (5%)
  local copies, waits for them, and re-layouts  4.18 us (2%)
    pallas_call x1, Pallas kernels, body(): pl.pallas_call(functools.partial(attention_backward, digits), out_shape=[...  65.9 us
    pallas_call x1, Pallas kernels, body(): pl.pallas_call(functools.partial(feed_forward, digits), out_shape=[shape(...  62.1 us
    pallas_call x1, Pallas kernels, body(): pl.pallas_call(functools.partial(attention_forward, digits), out_shape=[s...  39.2 us
    add x1, other arithmetic, body(): output + down_bias  5.29 us

profile of v3, /device:TPU:0, one launch (start us, length us, event | category | flops | bytes accessed | tf_op | source)
XLA Modules:
  0.0 180.8 jit_solution(5637627477068567381)
XLA Ops:
  0.6 39.2 %attention_forward.1 = (bf16[2304,2048]{1,0:T(8,128)(2,1)}, bf16[2304,2048]{1,0:T(8,128)(2,1)}, bf16[2304,512]{1,0:T(8,128)(2,1)}, bf16[2304,512]{1,0:T(8,128)(2...) custom-call(s32[2,3]{1,0:T(2,128)} %bitcast.35, ...), custom_call_target="tpu_custom_call" | custom-call | tf_op jit(solution)/shard_map/attention_forward/pallas_call | solution.py:1473
  39.8 62.1 %feed_forward.1 = (f32[2,1152,512]{2,1,0:T(8,128)}, f32[2304,512]{1,0:T(8,128)}, bf16[2304,1024]{1,0:T(8,128)(2,1)}, bf16[2,4,4,64,512]{4,3,2,1,0:T(8,128)(2,1)}...) custom-call(s32[2,3]{1,0:T(2,128)} %bitcast.36, ...), custom_call_target="tpu_custom_call" | custom-call | tf_op jit(solution)/shard_map/feed_forward/pallas_call | solution.py:1506
  102.0 0.0 copy-start.7
  102.0 65.9 %attention_backward.1 = (f32[2,1152,512]{2,1,0:T(8,128)}, f32[64,512]{1,0:T(8,128)}, bf16[2,4,4,16,512]{4,3,2,1,0:T(8,128)(2,1)}, bf16[2,4,4,16,512]{4,3,2,1,0:T...) custom-call(s32[2,3]{1,0:T(2,128)} %bitcast.37, ...), custom_call_target="tpu_custom_call" | custom-call | tf_op jit(solution)/shard_map/attention_backward/pallas_call | solution.py:1560
  167.9 0.0 slice-start
  167.9 0.0 copy-done.7
  167.9 0.0 copy-start.6
  167.9 0.0 copy-start.4
  168.0 0.0 copy-start.5
  168.0 0.0 copy-start.2
  168.0 0.0 copy-start.3
  168.0 0.0 copy-start
  168.0 0.0 copy-start.1
  168.0 0.0 slice-start.1
  168.0 5.3 %broadcast_add_fusion = f32[2,1152,512]{2,1,0:T(8,128)} fusion(f32[2,1152,512]{2,1,0:T(8,128)} %get-tuple-element.52, f32[512]{0:T(512)S(1)} %copy-done.7), kind=kLoop, calls=%fused_computation | loop fusion | flops 1179648 | bytes 9439232 | tf_op jit(solution)/shard_map/add | solution.py:1614
  173.3 0.0 copy-done.6
  173.3 0.6 fusion
  173.9 0.6 copy.32
  174.5 0.0 copy-done.4
  174.5 0.0 copy-done.5
  174.6 0.7 slice_bitcast_fusion
  175.3 0.0 copy-done.2
  175.3 0.0 copy-done.3
  175.3 1.7 bitcast_convert_fusion.2
  177.0 0.0 copy-done
  177.0 0.0 copy-done.1
  177.0 1.7 bitcast_convert_fusion
  178.7 0.0 slice-done
  178.7 0.0 slice-done.1
  178.7 2.2 %copy.35 = f32[2,1152,512]{2,1,0:T(8,128)} copy(f32[2,1152,512]{2,1,0:T(8,128)S(1)} %bitcast.32) | data formatting | bytes 9437184
  (4 shorter events, 0.0 us)
Async XLA Ops:
  102.0 66.0 %copy-start.7 = (f32[512]{0:T(512)S(1)}, f32[512]{0:T(512)}, u32[]{:S(2)}) copy-start(f32[512]{0:T(512)} %param.32) | copy-start | bytes 6148
  167.9 10.7 %slice-start = ((s8[4718592]{0:T(1024)(128)(4,1)}), s8[4194304]{0:T(1024)(128)(4,1)S(1)}, s32[]{:S(2)}) async-start(s8[4718592]{0:T(1024)(128)(4,1)} %bitcast.31), calls=%async_computation | async-start | bytes 8388608
  167.9 5.4 %copy-start.6 = (f32[16,512]{1,0:T(8,128)S(1)}, f32[16,512]{1,0:T(8,128)}, u32[]{:S(2)}) copy-start(f32[16,512]{1,0:T(8,128)} %get-tuple-element.70) | copy-start | bytes 98308
  167.9 6.6 %copy-start.4 = (f32[64,512]{1,0:T(8,128)S(1)}, f32[64,512]{1,0:T(8,128)}, u32[]{:S(2)}) copy-start(f32[64,512]{1,0:T(8,128)} %get-tuple-element.75) | copy-start | bytes 393220
  168.0 6.6 %copy-start.5 = (f32[64,512]{1,0:T(8,128)S(1)}, f32[64,512]{1,0:T(8,128)}, u32[]{:S(2)}) copy-start(f32[64,512]{1,0:T(8,128)} %get-tuple-element.76) | copy-start | bytes 393220
  168.0 7.3 %copy-start.2 = (bf16[2,4,4,16,512]{4,3,2,1,0:T(8,128)(2,1)S(1)}, bf16[2,4,4,16,512]{4,3,2,1,0:T(8,128)(2,1)}, u32[]{:S(2)}) copy-start(bf16[2,4,4,16,512]{4,3,2,1,0:T(8,128)(2,1)} %get-tuple-element.71) | copy-start | bytes 1572868
  168.0 7.3 %copy-start.3 = (bf16[2,4,4,16,512]{4,3,2,1,0:T(8,128)(2,1)S(1)}, bf16[2,4,4,16,512]{4,3,2,1,0:T(8,128)(2,1)}, u32[]{:S(2)}) copy-start(bf16[2,4,4,16,512]{4,3,2,1,0:T(8,128)(2,1)} %get-tuple-element.72) | copy-start | bytes 1572868
  168.0 9.0 %copy-start = (bf16[2,4,4,16,512]{4,3,2,1,0:T(8,128)(2,1)S(1)}, bf16[2,4,4,16,512]{4,3,2,1,0:T(8,128)(2,1)}, u32[]{:S(2)}) copy-start(bf16[2,4,4,16,512]{4,3,2,1,0:T(8,128)(2,1)} %get-tuple-element.74) | copy-start | bytes 1572868
  168.0 9.0 %copy-start.1 = (bf16[2,4,4,16,512]{4,3,2,1,0:T(8,128)(2,1)S(1)}, bf16[2,4,4,16,512]{4,3,2,1,0:T(8,128)(2,1)}, u32[]{:S(2)}) copy-start(bf16[2,4,4,16,512]{4,3,2,1,0:T(8,128)(2,1)} %get-tuple-element.73) | copy-start | bytes 1572868
  168.0 10.7 %slice-start.1 = ((s8[4718592]{0:T(1024)(128)(4,1)}), s8[524288]{0:T(1024)(128)(4,1)S(1)}, s32[]{:S(2)}) async-start(s8[4718592]{0:T(1024)(128)(4,1)} %bitcast.31), calls=%async_computation.1 | async-start | bytes 1048576

commit v4 on v3

--- a/solution.py
+++ b/solution.py
@@ -835,7 +835,7 @@
 
 
 def feed_forward(
-    digits, lens, cot_hbm, att_hbm, mix_hbm, inv_hbm, w_hbm, wo, gain, shift, up_bias,
+    digits, lens, cot_hbm, att_hbm, mix_hbm, inv_hbm, w_hbm, wo, gain, shift, down_bias, up_bias,
     up_own, down_own, q_hbm,
     out_hbm, ga_out, g_out, x_out, ffn_out, wo_grad, vec_grad, bias_grad, long_out, norm_out,
     cot, att, mix, inv, second, branch, grad_second, w_first, w_second, up, down, dup, ddown,
@@ -950,7 +950,7 @@
         between()
         att_rows = att[at]
         xhat, scale = normalize(att_rows)
-        output = att_rows + (branch[at] + more)
+        output = att_rows + (branch[at] + more) + down_bias[...]
         grad = grad_second[at] + grad_more
         grad_att = grad_out + norm_back(grad * gain[...], xhat, scale)
         add_row(2, grad_att)
@@ -1042,7 +1042,7 @@
     long_steps[0]()
     scatter_at = place(
         long_steps[1:] + scatter_steps[1:],
-        spots((0, 2, 4, 6, 2 * count, 2 * count), len(long_steps) - 1)
+        spots((0, 3, 5, 7, 2 * count, 2 * count), len(long_steps) - 1)
         + spots((0, 6, 2 * count), len(scatter_steps) - 1),
         2 * count + 1,
     )
@@ -1148,11 +1148,11 @@
     last_spot = 4 * count
     number = len(out_steps)
     chains = (
-        (out_steps[1:], spots((0, 4, 7, 11, 16, 22), number - 1)),
-        (ffn_steps[1:], spots((0, 12, 24), len(ffn_steps) - 1)),
-        (query_steps, spots((8, 10, 16, 25, 31, 32, 32), number)),
-        (key_steps, spots((16, 20, 29, 32, 32, 32, 32), number)),
-        (value_steps, spots((24, 26, 32, 32, 32, 32, 32), number)),
+        (out_steps[1:], spots((1, 5, 8, 16, 21, 26), number - 1)),
+        (ffn_steps[1:], spots((2, 16, 26), len(ffn_steps) - 1)),
+        (query_steps, spots((8, 11, 20, 24, 30, 32, 32), number)),
+        (value_steps, spots((16, 18, 24, 30, 32, 32, 32), number)),
+        (key_steps, spots((24, 26, 32, 32, 32, 32, 32), number)),
     )
     comm = [[] for _ in range(last_spot)]
     ends = []
@@ -1299,7 +1299,7 @@
         for i in range(len(key_side)):
             key_load(i).wait()
 
-    def key_phase(x, ga, wgrad):
+    def key_phase(x, ga, wgrad, gv):
         wait_x = [loads.start(x_hbm, x), loads.start(ga_hbm, ga)]
 
         def tile_at(t):
@@ -1312,7 +1312,7 @@
 
         def keys(t, _):
             batch = lax.div(t, per)
-            talk(comm[count : 2 * count], t)
+            talk(comm[2 * count : 3 * count], t)
             at = tile_at(t)
             for pair in range(pairs):
                 grad = dot(ones_beside(v[at, pair_cols(pair)]), sg[batch, pair])
@@ -1322,16 +1322,14 @@
 
         def values(t, _):
             batch = lax.div(t, per)
-            talk(comm[2 * count : 3 * count], t)
+            talk(comm[count : 2 * count], t)
             at = tile_at(t)
             for pair in range(pairs):
                 grad = dot_nt(kf[at, feat_lanes(pair)], sg[batch, pair, :PAIR])
-                v[at, pair_cols(pair)] = grad.astype(BF)
-            wgrad[...] += dot(n[1 + t], v[at])
+                gv[at, pair_cols(pair)] = grad.astype(BF)
+            wgrad[...] += dot(n[1 + t], gv[at])
             return 0
 
-        wgrad[...] = jnp.zeros_like(wgrad)
-        lax.fori_loop(0, count, keys, 0)
         for batch in range(2):
             own = slice(batch * LONG, (batch + 1) * LONG)
             for pair in range(pairs):
@@ -1341,13 +1339,15 @@
                 grads = block_grads(unpack_pair(packed), long_norm[row : row + 1])
                 mapped = kf[own, lanes]
                 grad = dot(ones_beside(v[own, cols]), grads)
-                v[own, cols] = dot_nt(mapped, grads[:PAIR]).astype(BF)
+                gv[own, cols] = dot_nt(mapped, grads[:PAIR]).astype(BF)
                 ks[own, cols] = feature_back(grad, mapped, ks[own], pair)
-        wgrad[...] += dot(n[0], ks[edge])
-        pack(key_x)
-        wgrad[...] = dot(n[0], v[edge])
+        gv[shorts] = v[shorts]
+        wgrad[...] = dot(n[0], gv[edge])
         lax.fori_loop(0, count, values, 0)
         pack(value_x)
+        wgrad[...] = dot(n[0], ks[edge])
+        lax.fori_loop(0, count, keys, 0)
+        pack(key_x)
         for copy in wait_x:
             copy.wait()
         swap_rows(x, cuts)
@@ -1361,7 +1361,7 @@
             grad = (
                 dot_nt(qs[at], wqkv[:, :width])
                 + dot_nt(ks[at], wqkv[:, width : 2 * width])
-                + dot_nt(v[at], wqkv[:, 2 * width :])
+                + dot_nt(gv[at], wqkv[:, 2 * width :])
             )
             vec_held[0, 0:1] += jnp.sum(grad * xhat, axis=0, keepdims=True)
             vec_held[0, 1:2] += jnp.sum(grad, axis=0, keepdims=True)
@@ -1413,9 +1413,61 @@
         pltpu.VMEM(x_hbm.shape, F32),
         pltpu.VMEM((inner_rows, width), F32),
         pltpu.VMEM((width, width), F32),
+        pltpu.VMEM((inner_rows, width), BF),
     )
     for item in (ffn_sum, *out_sum, *query_sum, *key_sum, *value_sum, vec_sum):
         item.drain()
+
+
+def finish(
+    out_raw, in_raw, vectors, ffn_first, ffn_second, *refs
+):
+    totals, refs = refs[:4], refs[4:]
+    out, in_grad, grads, refs = refs[0], refs[1], refs[2:6], refs[6:]
+    up_grad, down_grad, up_bias, lines, refs = refs[0], refs[1], refs[2], refs[3:9], refs[9:]
+    held, wide, rows, load_sem, store_sem, row_sem = refs
+    pieces = []
+    size = out_raw.shape[1] // 3
+    for i, (source, target) in enumerate(((out_raw, out), (in_raw, in_grad))):
+        for batch in range(2):
+            for part in range(3):
+                at = (batch, pl.ds(part * size, size))
+                slot = len(pieces)
+                inner = rows.at[(i,) + at]
+                pieces.append(
+                    (
+                        pltpu.make_async_copy(source.at[at], inner, row_sem.at[0, slot]),
+                        pltpu.make_async_copy(inner, target.at[at], row_sem.at[1, slot]),
+                    )
+                )
+    for load, _ in pieces:
+        load.start()
+    loads = []
+    for i, total in enumerate(totals):
+        loads.append(pltpu.make_async_copy(total, held.at[i], load_sem.at[i]))
+        loads[i].start()
+    copies = []
+    for load, keep in pieces:
+        load.wait()
+        keep.start()
+        copies.append(keep)
+    deep, part = up_grad.shape[0], ffn_first.shape[1]
+    for i, ffn in enumerate((ffn_first, ffn_second)):
+        lanes = slice(i * part, (i + 1) * part)
+        up_grad[:, lanes] = ffn[:deep]
+        down_grad[:, lanes] = ffn[deep:]
+    for i, row in enumerate(lines):
+        row[...] = vectors[i : i + 1]
+    width = vectors.shape[1]
+    for i in range(up_bias.shape[1] // width):
+        up_bias[:, i * width : (i + 1) * width] = vectors[6 + i : 7 + i]
+    for i, copy in enumerate(loads):
+        copy.wait()
+        wide[i] = load_blocks(held.at[i], 0, width, width).astype(F32)
+        copies.append(pltpu.make_async_copy(wide.at[i], grads[i], store_sem.at[i]))
+        copies[-1].start()
+    for copy in copies:
+        copy.wait()
 
 
 def body(
@@ -1517,7 +1569,7 @@
             shape(2, *digits, *long_block),
             shape(batches * pairs, 2 * FEAT, dtype=F32),
         ],
-        in_specs=[smem] + [hbm] * 5 + [vmem] * 6 + [hbm],
+        in_specs=[smem] + [hbm] * 5 + [vmem] * 7 + [hbm],
         out_specs=[hbm] * 4 + [vmem] * 6,
         scratch_shapes=[
             pltpu.VMEM(inputs.shape, F32),
@@ -1552,7 +1604,7 @@
         name="feed_forward",
     )(
         lens, cotangent, att, mix, inv, w, wo, line(second_gain), line(second_shift),
-        line(up_bias), up_weight, down_turned, qf,
+        line(down_bias), line(up_bias), up_weight, down_turned, qf,
     )
 
     late_block = block_shape(ways, width, width)
@@ -1602,30 +1654,31 @@
         wo_grad, vec_in, bias_in, long_grad, long_norm, line(first_gain), wqkv, projection,
     )
 
-    def whole(blocks):
-        lanes = blocks.shape[-1]
-        if lanes != width:
-            blocks = blocks.reshape(width // 16, width // lanes, 16, lanes)
-            blocks = jnp.swapaxes(blocks, 1, 2)
-        return blocks.reshape(width, width).astype(F32)
-
-    ffn_all = jnp.concatenate([ffn_grad, ffn_more], axis=1)
+    full = shape(width, width, dtype=F32)
+    output, in_grad, query, key, value, out_w, up_grad, down_grad, up_line, *lines = pl.pallas_call(
+        finish,
+        out_shape=[shape(*inputs.shape, dtype=F32)] * 2
+        + [full] * 4
+        + [shape(deep, half, dtype=F32)] * 2
+        + [shape(1, hidden, dtype=F32)]
+        + [shape(1, width, dtype=F32)] * 6,
+        in_specs=[hbm] * 2 + [vmem] * 3 + [hbm] * 4,
+        out_specs=[hbm] * 6 + [vmem] * 9,
+        scratch_shapes=[
+            pltpu.VMEM((4,) + late_shape, BF),
+            pltpu.VMEM((4, width, width), F32),
+            pltpu.VMEM((2,) + inputs.shape, F32),
+            pltpu.SemaphoreType.DMA((4,)),
+            pltpu.SemaphoreType.DMA((4,)),
+            pltpu.SemaphoreType.DMA((2, 12)),
+        ],
+        compiler_params=pltpu.CompilerParams(vmem_limit_bytes=VMEM_LIMIT),
+        name="finish",
+    )(output, in_grad, vectors, ffn_grad, ffn_more, query, key, value, out_w)
+    lines = [row.reshape(width) for row in lines]
     return (
-        output + down_bias,
-        in_grad,
-        vectors[0],
-        vectors[1],
-        whole(query),
-        whole(key),
-        whole(value),
-        whole(out_w),
-        vectors[2],
-        vectors[3],
-        vectors[4],
-        ffn_all[:deep],
-        vectors[6 : 6 + hidden // width].reshape(hidden),
-        ffn_all[deep:].T,
-        vectors[5],
+        output, in_grad, lines[0], lines[1], query, key, value, out_w, lines[2], lines[3],
+        lines[4], up_grad, up_line.reshape(hidden), down_grad.T, lines[5],
     )
 
 

time: 181 us -> 177 us (0.978)
  Pallas kernels: 167 us -> 176 us
  other arithmetic: 8.65 us -> 0 us
  local copies, waits for them, and re-layouts: 4.18 us -> 0 us
    pallas_call x0 -> x1, Pallas kernels: none -> 10.9 us  [body(): pl.pallas_call(finish, out_shape=[shape(*inputs.shape, dtype=F32)] * 2 +...]
    add x1 -> x0, other arithmetic: 5.29 us -> none  [body(): output + down_bias]
    convert_element_type x2 -> x0, other arithmetic: 3.35 us -> none  [whole(): return blocks.reshape(width, width).astype(F32)]
    unnamed x24 -> x0, local copies, waits for them, and re-layouts: 2.85 us -> none
where the time goes in v4:
time: 177 us
  Pallas kernels  176 us (99%)
    pallas_call x1, Pallas kernels, body(): pl.pallas_call(functools.partial(attention_backward, digits), out_shape=[...  65 us
    pallas_call x1, Pallas kernels, body(): pl.pallas_call(functools.partial(feed_forward, digits), out_shape=[shape(...  61.2 us
    pallas_call x1, Pallas kernels, body(): pl.pallas_call(functools.partial(attention_forward, digits), out_shape=[s...  39.1 us
    pallas_call x1, Pallas kernels, body(): pl.pallas_call(finish, out_shape=[shape(*inputs.shape, dtype=F32)] * 2 +...  10.9 us

profile of v4, /device:TPU:0, one launch (start us, length us, event | category | flops | bytes accessed | tf_op | source)
XLA Modules:
  0.0 177.1 jit_solution(5494266309234327320)
XLA Ops:
  0.6 39.1 %attention_forward.1 = (bf16[2304,2048]{1,0:T(8,128)(2,1)}, bf16[2304,2048]{1,0:T(8,128)(2,1)}, bf16[2304,512]{1,0:T(8,128)(2,1)}, bf16[2304,512]{1,0:T(8,128)(2...) custom-call(s32[2,3]{1,0:T(2,128)} %bitcast.19, ...), custom_call_target="tpu_custom_call" | custom-call | tf_op jit(solution)/shard_map/attention_forward/pallas_call | solution.py:1525
  39.8 61.2 %feed_forward.1 = (f32[2,1152,512]{2,1,0:T(8,128)}, f32[2304,512]{1,0:T(8,128)}, bf16[2304,1024]{1,0:T(8,128)(2,1)}, bf16[2,4,4,64,512]{4,3,2,1,0:T(8,128)(2,1)}...) custom-call(s32[2,3]{1,0:T(2,128)} %bitcast.20, ...), custom_call_target="tpu_custom_call" | custom-call | tf_op jit(solution)/shard_map/feed_forward/pallas_call | solution.py:1558
  101.0 65.0 %attention_backward.1 = (f32[2,1152,512]{2,1,0:T(8,128)}, f32[64,512]{1,0:T(8,128)}, bf16[2,4,4,16,512]{4,3,2,1,0:T(8,128)(2,1)}, bf16[2,4,4,16,512]{4,3,2,1,0:T...) custom-call(s32[2,3]{1,0:T(2,128)} %bitcast.21, ...), custom_call_target="tpu_custom_call" | custom-call | tf_op jit(solution)/shard_map/attention_backward/pallas_call | solution.py:1612
  166.0 10.9 %finish.1 = (f32[2,1152,512]{2,1,0:T(8,128)}, f32[2,1152,512]{2,1,0:T(8,128)}, f32[512,512]{1,0:T(8,128)}, f32[512,512]{1,0:T(8,128)}, f32[512,512]{1,0:T(8,128)...) custom-call(f32[2,1152,512]{2,1,0:T(8,128)} %get-tuple-element.67.ou, ...), custom_call_target="tpu_custom_call" | custom-call | tf_op jit(solution)/shard_map/finish/pallas_call | solution.py:1658

commit v5 on v4

--- a/solution.py
+++ b/solution.py
@@ -1006,7 +1006,9 @@
     last_waits = [loads.start(q_hbm.at[pl.ds(0, 2 * LONG)], qf)]
     for some in (inner[:1], inner[1:]):
         last_waits += load_inner(mix_hbm, mix, some) + load_inner(inv_hbm, inv, some)
-    gather_at = place(gather_steps[1:], spots((1, 3, count), len(gather_steps) - 1), count + 1)
+    gather_at = place(
+        gather_steps[1:-1], spots((1, count), len(gather_steps) - 2), count + 1
+    )
 
     def first_pass(t, _):
         talk(gather_at[:count], t)
@@ -1018,6 +1020,7 @@
     _all(gather_at[count])
     pack(w_first)
     scatter_steps[0]()
+    gather_steps[-1]()
     unpack(w_second)
     dup[...] = jnp.zeros_like(dup)
     ddown[...] = jnp.zeros_like(ddown)
@@ -1427,10 +1430,10 @@
     up_grad, down_grad, up_bias, lines, refs = refs[0], refs[1], refs[2], refs[3:9], refs[9:]
     held, wide, rows, load_sem, store_sem, row_sem = refs
     pieces = []
-    size = out_raw.shape[1] // 3
+    size = out_raw.shape[1] // 6
     for i, (source, target) in enumerate(((out_raw, out), (in_raw, in_grad))):
         for batch in range(2):
-            for part in range(3):
+            for part in range(6):
                 at = (batch, pl.ds(part * size, size))
                 slot = len(pieces)
                 inner = rows.at[(i,) + at]
@@ -1440,17 +1443,13 @@
                         pltpu.make_async_copy(inner, target.at[at], row_sem.at[1, slot]),
                     )
                 )
-    for load, _ in pieces:
-        load.start()
     loads = []
     for i, total in enumerate(totals):
         loads.append(pltpu.make_async_copy(total, held.at[i], load_sem.at[i]))
         loads[i].start()
+    for load, _ in pieces:
+        load.start()
     copies = []
-    for load, keep in pieces:
-        load.wait()
-        keep.start()
-        copies.append(keep)
     deep, part = up_grad.shape[0], ffn_first.shape[1]
     for i, ffn in enumerate((ffn_first, ffn_second)):
         lanes = slice(i * part, (i + 1) * part)
@@ -1466,6 +1465,10 @@
         wide[i] = load_blocks(held.at[i], 0, width, width).astype(F32)
         copies.append(pltpu.make_async_copy(wide.at[i], grads[i], store_sem.at[i]))
         copies[-1].start()
+    for load, keep in pieces:
+        load.wait()
+        keep.start()
+        copies.append(keep)
     for copy in copies:
         copy.wait()
 
@@ -1670,7 +1673,7 @@
             pltpu.VMEM((2,) + inputs.shape, F32),
             pltpu.SemaphoreType.DMA((4,)),
             pltpu.SemaphoreType.DMA((4,)),
-            pltpu.SemaphoreType.DMA((2, 12)),
+            pltpu.SemaphoreType.DMA((2, 24)),
         ],
         compiler_params=pltpu.CompilerParams(vmem_limit_bytes=VMEM_LIMIT),
         name="finish",

time: 177 us -> 176 us (level)
  no operation moved by 1% of the time
where the time goes in v5:
time: 176 us
  Pallas kernels  175 us (99%)
    pallas_call x1, Pallas kernels, body(): pl.pallas_call(functools.partial(attention_backward, digits), out_shape=[...  64.9 us
    pallas_call x1, Pallas kernels, body(): pl.pallas_call(functools.partial(feed_forward, digits), out_shape=[shape(...  60.7 us
    pallas_call x1, Pallas kernels, body(): pl.pallas_call(functools.partial(attention_forward, digits), out_shape=[s...  39.1 us
    pallas_call x1, Pallas kernels, body(): pl.pallas_call(finish, out_shape=[shape(*inputs.shape, dtype=F32)] * 2 +...  10.6 us

profile of v5, /device:TPU:0, one launch (start us, length us, event | category | flops | bytes accessed | tf_op | source)
XLA Modules:
  0.0 176.3 jit_solution(15124271895789417037)
XLA Ops:
  0.6 39.1 %attention_forward.1 = (bf16[2304,2048]{1,0:T(8,128)(2,1)}, bf16[2304,2048]{1,0:T(8,128)(2,1)}, bf16[2304,512]{1,0:T(8,128)(2,1)}, bf16[2304,512]{1,0:T(8,128)(2...) custom-call(s32[2,3]{1,0:T(2,128)} %bitcast.19, ...), custom_call_target="tpu_custom_call" | custom-call | tf_op jit(solution)/shard_map/attention_forward/pallas_call | solution.py:1528
  39.8 60.7 %feed_forward.1 = (f32[2,1152,512]{2,1,0:T(8,128)}, f32[2304,512]{1,0:T(8,128)}, bf16[2304,1024]{1,0:T(8,128)(2,1)}, bf16[2,4,4,64,512]{4,3,2,1,0:T(8,128)(2,1)}...) custom-call(s32[2,3]{1,0:T(2,128)} %bitcast.20, ...), custom_call_target="tpu_custom_call" | custom-call | tf_op jit(solution)/shard_map/feed_forward/pallas_call | solution.py:1561
  100.5 64.9 %attention_backward.1 = (f32[2,1152,512]{2,1,0:T(8,128)}, f32[64,512]{1,0:T(8,128)}, bf16[2,4,4,16,512]{4,3,2,1,0:T(8,128)(2,1)}, bf16[2,4,4,16,512]{4,3,2,1,0:T...) custom-call(s32[2,3]{1,0:T(2,128)} %bitcast.21, ...), custom_call_target="tpu_custom_call" | custom-call | tf_op jit(solution)/shard_map/attention_backward/pallas_call | solution.py:1615
  165.4 10.6 %finish.1 = (f32[2,1152,512]{2,1,0:T(8,128)}, f32[2,1152,512]{2,1,0:T(8,128)}, f32[512,512]{1,0:T(8,128)}, f32[512,512]{1,0:T(8,128)}, f32[512,512]{1,0:T(8,128)...) custom-call(f32[2,1152,512]{2,1,0:T(8,128)} %get-tuple-element.67.ou, ...), custom_call_target="tpu_custom_call" | custom-call | tf_op jit(solution)/shard_map/finish/pallas_call | solution.py:1661
